TPU v7x, 512 devices: a whole 4x8x8 slice. The times are simulated.
512 devices in a mesh: dp: 32 (over z_lo, x, core), tensor: 16 (over y, z_hi).
Axes of the slice: x: 4, y: 8, z: 8 (z_hi: 2, z_lo: 4; z = z_hi * 4 + z_lo), core: 2. Of those that a mesh axis runs over, the one named last changes fastest.
Arguments:
- tokens: bfloat16 [8192, 3072], P('dp', 'tensor'), may hold values from -6 to 6
- keys: bfloat16 [8192, 4096], P('dp', 'tensor'), may hold values from -4 to 4
- values: bfloat16 [8192, 4096], P('dp', 'tensor'), may hold values from -6 to 6
- cotangent: bfloat16 [8192, 4096], P('dp', 'tensor'), may hold values from -48 to 48
- query_weight: bfloat16 [3072, 4096], P('dp', 'tensor'), may hold values from -0.109375 to 0.109375
Outputs:
- grad_query: float32 [3072, 4096], P('dp', 'tensor')
All inputs are finite; a program needn't handle non-finite values.
Results may differ from a plain program's by a relative error of at most 0.04.
Values may be sent and summed in bfloat16 or wider, within the bound.
No kernel may reach another device: no remote copies, remote signals or barrier semaphores. Data moves between devices by JAX's collectives and lax.ppermute only.
A program may use at most 64 MiB of HBM per device.

v0:
```python
import math

import jax
import jax.numpy as jnp
from jax import lax
from jax.sharding import PartitionSpec as P

HEAD = 128
IMAGE_TOK = 256


def layer_norm(rows):
    rows = rows.astype(jnp.float32)
    center = rows - jnp.mean(rows, -1, keepdims=True)
    spread = jnp.mean(center * center, -1, keepdims=True)
    return (center * lax.rsqrt(spread + 1e-06)).astype(jnp.bfloat16)


def query_grad(normed, weight, keys, values, cotangent):
    row_count = normed.shape[0]
    col_count = weight.shape[1]
    blocks_shape = (row_count // IMAGE_TOK, IMAGE_TOK, col_count // HEAD, HEAD)
    temper = 1.0 / math.sqrt(HEAD)
    query = jnp.dot(normed, weight, preferred_element_type=jnp.float32).reshape(blocks_shape)
    center = query - jnp.mean(query, -1, keepdims=True)
    inverse = lax.rsqrt(jnp.mean(center * center, -1, keepdims=True) + 1e-06)
    normal_query = center * inverse
    key_rows = keys.astype(jnp.float32).reshape(blocks_shape)
    value_rows = values.astype(jnp.float32).reshape(blocks_shape)
    cot_rows = cotangent.astype(jnp.float32).reshape(blocks_shape)
    scores = jnp.einsum("ilhd,imhd->ihlm", normal_query, key_rows) * temper
    expon = jnp.exp(scores)
    attend = expon / jnp.sum(expon, -1, keepdims=True)
    pull_prob = jnp.einsum("ilhd,imhd->ihlm", cot_rows, value_rows)
    pull_score = attend * (pull_prob - jnp.sum(attend * pull_prob, -1, keepdims=True))
    pull_normal = jnp.einsum("ihlm,imhd->ilhd", pull_score, key_rows) * temper
    pull_query = inverse * (
        pull_normal
        - jnp.mean(pull_normal, -1, keepdims=True)
        - normal_query * jnp.mean(pull_normal * normal_query, -1, keepdims=True)
    )
    return pull_query.reshape(row_count, col_count).astype(jnp.bfloat16)


def shards(tokens, keys, values, cotangent, query_weight):
    full_rows = lax.all_gather(tokens, "tensor", axis=1, tiled=True)
    weight_whole = lax.all_gather(query_weight, "dp", axis=0, tiled=True)
    total_tokens = full_rows.shape[0] * lax.axis_size("dp")
    token_scale = 1.0 / jnp.sqrt(jnp.float32(total_tokens))
    model_width = full_rows.shape[1]
    query_all = weight_whole.shape[1] * lax.axis_size("tensor")
    radius = 0.3 * jnp.sqrt(jnp.float32(model_width + query_all))
    normed = layer_norm(full_rows)

    def local_term(weight):
        pull_query = query_grad(normed, weight, keys, values, cotangent)
        return jnp.dot(normed.T, pull_query, preferred_element_type=jnp.float32) * token_scale

    first_term = local_term(weight_whole)
    first_shard = lax.psum_scatter(
        first_term.astype(jnp.bfloat16), "dp", scatter_dimension=0, tiled=True
    ).astype(jnp.float32)
    local_sq = jnp.sum(first_shard * first_shard)
    grad_norm = jnp.sqrt(lax.psum(local_sq, ("dp", "tensor")))
    factor = radius / grad_norm
    moved_shard = (query_weight.astype(jnp.float32) + factor * first_shard).astype(jnp.bfloat16)
    moved_whole = lax.all_gather(moved_shard, "dp", axis=0, tiled=True)
    second_term = local_term(moved_whole)
    return lax.psum_scatter(
        second_term.astype(jnp.bfloat16), "dp", scatter_dimension=0, tiled=True
    ).astype(jnp.float32)


def solution(mesh):
    placed = (
        P("dp", "tensor"),
        P("dp", "tensor"),
        P("dp", "tensor"),
        P("dp", "tensor"),
        P("dp", "tensor"),
    )
    return jax.shard_map(
        shards, mesh=mesh, in_specs=placed, out_specs=P("dp", "tensor"), check_vma=False
    )
```

profile of v0, /device:TPU:1, one launch (start us, length us, event | category | flops | bytes accessed | tf_op | source)
XLA Modules:
  0.0 641.7 jit_solution(8683791914787929836)
XLA Ops:
  6.5 0.7 all-gather.4.cloned.1.call-update
  7.3 0.7 all-gather.6.cloned.1.call-update
  8.0 0.0 reduce-scatter.3.cloned.1.call-start
  8.1 1.0 copy.45
  9.1 1.1 fusion.30
  10.2 102.0 %all-gather.4.cloned.1.call-done = bf16[256,3072]{0,1:T(8,128)(2,1)} async-done(((bf16[256,192]{0,1:T(8,128)(2,1)}), bf16[256,3072]{0,1:T(8,128)(2,1)}) %all-gather.4.cloned.1.call-update) | async-done | bytes 1572880 | tf_op jit(solution)/shard_map/all_gather | solution.py:46
  112.2 1.9 convert_reduce_fusion
  114.1 0.5 fusion.4
  114.6 60.0 %all-gather.6.cloned.1.call-done = bf16[3072,256]{1,0:T(8,128)(2,1)} async-done(((bf16[96,256]{1,0:T(8,128)(2,1)}), bf16[3072,256]{1,0:T(8,128)(2,1)}) %all-gather.6.cloned.1.call-update) | async-done | bytes 1572880 | tf_op jit(solution)/shard_map/all_gather | solution.py:47
  174.7 2.3 bitcast_reduce_fusion.1
  177.0 0.1 copy.6
  177.2 0.5 multiply_reduce_fusion.1
  177.7 0.2 fusion.67
  177.9 0.1 multiply_convert_fusion.1
  178.0 0.4 copy-done.5
  178.3 1.8 fusion
  180.2 0.0 all-gather.8.cloned.1.call-start
  180.2 142.6 %reduce-scatter.3.cloned.1.call-done = bf16[96,256]{1,0:T(8,128)(2,1)} async-done(((bf16[3072,256]{1,0:T(8,128)(2,1)}), bf16[96,256]{1,0:T(8,128)(2,1)}) %reduce-scatter.3.cloned.1.call-update) | async-done | bytes 49168 | tf_op jit(solution)/shard_map/reduce_scatter | solution.py:60
  322.8 1.4 fusion.43
  324.3 101.5 %psum.7 = f32[]{:T(128)} all-reduce(f32[]{:T(128)} %fusion.43), channel_id=1, replica_groups=mesh['dp'=32,'tensor'=16] {'dp','tensor'}, use_global_device_ids=true, to_apply=%region_10.0 | all-reduce | flops 1 | bytes 8 | tf_op jit(solution)/shard_map/psum | solution.py:64
  426.4 1.4 fusion.45
  427.9 0.0 reduce-scatter.5.cloned.1.call-start
  428.0 57.6 %all-gather.8.cloned.1.call-done = bf16[3072,256]{1,0:T(8,128)(2,1)} async-done(((bf16[96,256]{1,0:T(8,128)(2,1)}), bf16[3072,256]{1,0:T(8,128)(2,1)}) %all-gather.8.cloned.1.call-update) | async-done | bytes 1572880 | tf_op jit(solution)/shard_map/all_gather | solution.py:67
  485.5 2.3 bitcast_reduce_fusion
  487.9 0.1 copy.12
  488.0 0.5 multiply_reduce_fusion
  488.5 0.2 fusion.66
  488.8 0.1 multiply_convert_fusion
  488.8 0.3 copy-done.6
  489.2 1.8 fusion.1
  491.0 142.7 %reduce-scatter.5.cloned.1.call-done = bf16[96,256]{1,0:T(8,128)(2,1)} async-done(((bf16[3072,256]{1,0:T(8,128)(2,1)}), bf16[96,256]{1,0:T(8,128)(2,1)}) %reduce-scatter.5.cloned.1.call-update) | async-done | bytes 49168 | tf_op jit(solution)/shard_map/reduce_scatter | solution.py:69
  633.7 1.4 convert_element_type.53
  (28 shorter events, 0.3 us)
Async XLA Ops:
  6.5 2.5 copy-start
  6.5 105.6 %all-gather.4.cloned.1.call-start = ((), (), s32[]{:S(2)}) async-start(), calls=%async_computation.2 | async-start | bytes 1671168 | tf_op jit(solution)/shard_map/all_gather | solution.py:46
  7.3 167.4 %all-gather.6.cloned.1.call-start = ((), (), s32[]{:S(2)}) async-start(), calls=%async_computation.3 | async-start | bytes 1622016 | tf_op jit(solution)/shard_map/all_gather | solution.py:47
  8.0 314.8 %reduce-scatter.3.cloned.1.call-start = ((), (), s32[]{:S(2)}) async-start(), calls=%async_computation.4 | async-start | bytes 1622016 | tf_op jit(solution)/shard_map/reduce_scatter | solution.py:60
  112.2 2.0 copy-start.1
  114.6 62.3 %copy-start.4 = (f32[256]{0:T(256)}, f32[256]{0:T(256)S(1)}, u32[]{:S(2)}) copy-start(f32[256]{0:T(256)S(1)} %add_rsqrt_fusion.2) | copy-start | bytes 3076
  114.6 62.5 %copy-start.3 = (bf16[256,256]{1,0:T(8,128)(2,1)S(1)}, bf16[256,256]{1,0:T(8,128)(2,1)}, u32[]{:S(2)}) copy-start(bf16[256,256]{1,0:T(8,128)(2,1)} %param.6) | copy-start | bytes 393220
  177.7 0.7 copy-start.5
  180.1 246.3 %copy-start.2 = (bf16[96,256]{1,0:T(8,128)(2,1)S(1)}, bf16[96,256]{1,0:T(8,128)(2,1)}, u32[]{:S(2)}) copy-start(bf16[96,256]{1,0:T(8,128)(2,1)} %param.9) | copy-start | bytes 147460
  180.2 305.3 %all-gather.8.cloned.1.call-start = ((), (), s32[]{:S(2)}) async-start(), calls=%async_computation.5 | async-start | bytes 1622016 | tf_op jit(solution)/shard_map/all_gather | solution.py:67
  427.9 205.8 %reduce-scatter.5.cloned.1.call-start = ((), (), s32[]{:S(2)}) async-start(), calls=%async_computation.6 | async-start | bytes 1622016 | tf_op jit(solution)/shard_map/reduce_scatter | solution.py:69
  488.5 0.7 copy-start.6
Sparse Core Ops, SparseCore 0:
  10.5 101.5 all-gather.3
  114.3 60.2 all-gather.5
  180.3 142.4 reduce-scatter.2
  428.0 57.4 all-gather.7
  491.1 142.4 reduce-scatter.4
where the time goes:
time: 646 us; the launch traced here: 642 us
  waiting for transfers between devices  506 us (78%)
  blocking collectives  101 us (16%)
  between operations  14 us (2%)
  matrix products  10.8 us (2%)
  other arithmetic  7.01 us (1%)
    reduce_scatter x1, waiting for transfers between devices, shards(): lax.psum_scatter(second_term.astype(jnp.bfloat16), 'dp', scatter_dimensio...  143 us
    reduce_scatter x1, waiting for transfers between devices, shards(): lax.psum_scatter(first_term.astype(jnp.bfloat16), 'dp', scatter_dimension...  143 us
    all_gather x1, waiting for transfers between devices, shards(): full_rows = lax.all_gather(tokens, 'tensor', axis=1, tiled=True)  102 us
    psum x1, blocking collectives, shards(): grad_norm = jnp.sqrt(lax.psum(local_sq, ('dp', 'tensor')))  101 us
    all_gather x1, waiting for transfers between devices, shards(): weight_whole = lax.all_gather(query_weight, 'dp', axis=0, tiled=True)  60 us
    all_gather x1, waiting for transfers between devices, shards(): moved_whole = lax.all_gather(moved_shard, 'dp', axis=0, tiled=True)  57.6 us
  transfers between devices with their start and end apart: 5, of which 5 were waited for; matrix products, arithmetic and copies ran while one was open for 1% of the time, Pallas kernels for 0%

commit v1 on v0

v1 whole, which is shorter than its diff:
```python
import math

import jax
import jax.numpy as jnp
from jax import lax
from jax.experimental import pallas as pl
from jax.experimental.pallas import tpu as pltpu
from jax.sharding import Mesh, PartitionSpec as P

HEAD = 128
ROWS = 96
EPS = 1e-06
F32 = jnp.float32
BF16 = jnp.bfloat16
AXES = ("zl", "x", "core", "y", "zh")
SIZES = (4, 4, 2, 8, 2)
VMEM_LIMIT = 48 * 1024 * 1024


def mm(a, b, dims=((1,), (0,))):
    return lax.dot_general(a, b, (dims, ((), ())), preferred_element_type=F32)


def query_grad(query, keys, values, cotangent):
    temper = 1.0 / math.sqrt(HEAD)
    heads = []
    for h in range(query.shape[1] // HEAD):
        cols = slice(h * HEAD, (h + 1) * HEAD)
        q = query[:, cols]
        key, value, cot = keys[:, cols], values[:, cols], cotangent[:, cols]
        center = q - jnp.mean(q, -1, keepdims=True)
        inverse = lax.rsqrt(jnp.mean(center * center, -1, keepdims=True) + EPS)
        qn = center * inverse
        scores = mm(qn.astype(BF16), key, ((1,), (1,))) * temper
        expon = jnp.exp(scores)
        attend = expon / jnp.sum(expon, -1, keepdims=True)
        dprob = mm(cot, value, ((1,), (1,)))
        dscore = attend * (dprob - jnp.sum(attend * dprob, -1, keepdims=True))
        dqn = mm(dscore.astype(BF16), key) * temper
        dq = inverse * (
            dqn
            - jnp.mean(dqn, -1, keepdims=True)
            - qn * jnp.mean(dqn * qn, -1, keepdims=True)
        )
        heads.append(dq.astype(BF16))
    return jnp.concatenate(heads, axis=1)


def place(y, zh):
    return (2 * (y % 2) + zh) * 4 + y // 2


def first_kernel(scale, at_ref, mine_ref, theirs_ref, w_own_ref, w_oth_ref, keys_ref, values_ref, cot_ref,
                 normt_ref, normed_ref, query_ref, keep_ref, send_ref):
    core, zh = at_ref[0], at_ref[1]
    count = mine_ref.shape[0]
    width = 2 * count * mine_ref.shape[1]
    total = jnp.zeros((1, mine_ref.shape[2]), F32)
    for ref in (mine_ref, theirs_ref):
        for y in range(count):
            total += jnp.sum(ref[y].astype(F32), 0, keepdims=True)
    mean = total / width
    total = jnp.zeros_like(total)
    for ref in (mine_ref, theirs_ref):
        for y in range(count):
            center = ref[y].astype(F32) - mean
            total += jnp.sum(center * center, 0, keepdims=True)
    inverse = lax.rsqrt(total / width + EPS)
    for ref, z in ((mine_ref, zh), (theirs_ref, 1 - zh)):
        for y in range(count):
            block = ((ref[y].astype(F32) - mean) * inverse).astype(BF16)
            for c in range(2):
                half = jnp.bitwise_xor(core, c)
                normt_ref[half, place(y, z)] = block[c * ROWS:(c + 1) * ROWS]
    half_rows = w_own_ref.shape[0]
    for half in range(2):
        rows = normt_ref[half].reshape(half_rows, normt_ref.shape[3])
        normed_ref[:, half * half_rows:(half + 1) * half_rows] = rows.T
    query = mm(normed_ref[:, :half_rows], w_own_ref[...]) + mm(normed_ref[:, half_rows:], w_oth_ref[...])
    query_ref[...] = query
    dq = query_grad(query, keys_ref[...], values_ref[...], cot_ref[...])
    for half, ref in ((0, keep_ref), (1, send_ref)):
        rows = normt_ref[half].reshape(half_rows, normt_ref.shape[3])
        ref[...] = (mm(rows, dq) * scale).astype(BF16).reshape(ref.shape)


def project_kernel(normed_ref, own_ref, oth_ref, out_ref, square_ref):
    half_rows = own_ref.shape[0]
    out_ref[...] = mm(normed_ref[:, :half_rows], own_ref[...]) + mm(normed_ref[:, half_rows:], oth_ref[...])
    own, oth = own_ref[...].astype(F32), oth_ref[...].astype(F32)
    square_ref[...] = jnp.sum((own * own + oth * oth).reshape(-1, 8, own.shape[1]), 0)


def second_kernel(scale, radius, square_ref, query_ref, move_ref, normt_ref, keys_ref, values_ref, cot_ref,
                  keep_ref, send_ref):
    norm = jnp.sqrt(jnp.sum(square_ref[...], keepdims=True))
    query = query_ref[...] + (radius / norm) * move_ref[...]
    dq = query_grad(query, keys_ref[...], values_ref[...], cot_ref[...])
    half_rows = keep_ref.shape[0] * keep_ref.shape[1]
    for half, ref in ((0, keep_ref), (1, send_ref)):
        rows = normt_ref[half].reshape(half_rows, normt_ref.shape[3])
        ref[...] = (mm(rows, dq) * scale).astype(BF16).reshape(ref.shape)


def call(kernel, outs, smem=0):
    spec = pl.BlockSpec(memory_space=pltpu.VMEM)

    def run(*args):
        specs = [pl.BlockSpec(memory_space=pltpu.SMEM)] * smem + [spec] * (len(args) - smem)
        return pl.pallas_call(
            kernel,
            out_shape=[jax.ShapeDtypeStruct(s, d) for s, d in outs],
            in_specs=specs,
            out_specs=[spec] * len(outs),
            compiler_params=pltpu.CompilerParams(vmem_limit_bytes=VMEM_LIMIT),
        )(*args)

    return run


def swap(size, step):
    return [(i, i ^ step) for i in range(size)]


def after(value, *others):
    return lax.optimization_barrier((value, *others))[0]


def gather_dp(shard):
    along_z = lax.all_gather(shard, "zl", axis=0, tiled=True)
    own = lax.all_gather(along_z, "x", axis=0, tiled=True)
    return own, lax.ppermute(own, "core", swap(2, 1))


def scatter_dp(keep, send):
    got = lax.ppermute(send, "core", swap(2, 1))
    both = (keep.astype(F32) + got.astype(F32)).astype(BF16)
    parts = lax.all_to_all(both, ("x", "zl"), 0, 0, tiled=True)
    return jnp.sum(parts.astype(F32), 0)


def shards(tokens, keys, values, cotangent, query_weight):
    tok = tokens.T
    feats, count = tok.shape
    cols = keys.shape[1]
    model_width = feats * 16
    total_tokens = count * 32
    scale = 1.0 / math.sqrt(total_tokens)
    radius = 0.3 * math.sqrt(model_width + cols * 16)
    at = jnp.stack([lax.axis_index("core"), lax.axis_index("zh")]).astype(jnp.int32)

    other = lax.ppermute(tok, "zh", swap(2, 1))
    w_own, w_oth = gather_dp(query_weight)
    mine = lax.all_gather(tok, "y", axis=0)
    other = after(other, mine)
    theirs = lax.all_gather(other, "y", axis=0)

    half = (16, ROWS, cols)
    normt, normed, query, keep, send = call(
        lambda *refs: first_kernel(scale, *refs),
        [((2, 16, ROWS, count), BF16), ((count, model_width), BF16), ((count, cols), F32), (half, BF16), (half, BF16)],
        smem=1,
    )(at, mine, theirs, w_own, w_oth, keys, values, cotangent)

    first = scatter_dp(keep, send)
    own, oth = gather_dp(first.astype(BF16))
    move, square = call(project_kernel, [((count, cols), F32), ((8, cols), F32)])(normed, own, oth)
    square = lax.psum(lax.psum(square, "zh"), "y")
    keep, send = call(
        lambda *refs: second_kernel(scale, radius, *refs), [(half, BF16), (half, BF16)]
    )(square, query, move, normt, keys, values, cotangent)
    return scatter_dp(keep, send)


def solution(mesh):
    cut = Mesh(mesh.devices.reshape(SIZES), AXES)
    spec = P(("zl", "x", "core"), ("y", "zh"))
    return jax.shard_map(shards, mesh=cut, in_specs=(spec,) * 5, out_specs=spec, check_vma=False)
```

time: 646 us -> 228 us (0.35)
  waiting for transfers between devices: 506 us -> 5.68 us
  blocking collectives: 101 us -> 160 us
  starting transfers between devices: 0.16 us -> 49.1 us
  between operations: 14 us -> 0.14 us
  matrix products: 10.8 us -> 0 us
  Pallas kernels: 0 us -> 8.16 us
    reduce_scatter x2 -> x0, waiting for transfers between devices: 285 us -> none  [the longest x1 143 us: shards(): lax.psum_scatter(second_term.astype(jnp.bfloat16), 'dp', scatter_dimensio...]
    all_gather x3 -> x0, waiting for transfers between devices: 220 us -> none  [the longest x1 102 us: shards(): full_rows = lax.all_gather(tokens, 'tensor', axis=1, tiled=True)]
    all_gather x0 -> x6, blocking collectives: none -> 89.7 us  [the longest x2 23.3 us: gather_dp(): along_z = lax.all_gather(shard, 'zl', axis=0, tiled=True)]
    psum x1 -> x2, blocking collectives: 101 us -> 19.9 us  [shards(): square = lax.psum(lax.psum(square, 'zh'), 'y')]
    all_to_all x0 -> x2, blocking collectives: none -> 50 us  [scatter_dp(): parts = lax.all_to_all(both, ('x', 'zl'), 0, 0, tiled=True)]
    ppermute x0 -> x5, starting transfers between devices: none -> 49.1 us  [the longest x2 20 us: scatter_dp(): got = lax.ppermute(send, 'core', swap(2, 1))]
    dot_general x7 -> x0, matrix products: 9.75 us -> none  [the longest x2 4.55 us: query_grad(): jnp.dot(normed, weight, preferred_element_type=jnp.float32)]
    pallas_call x0 -> x3, Pallas kernels: none -> 8.16 us  [run(): pl.pallas_call(kernel, out_shape=[jax.ShapeDtypeStruct(s, d) for s, d in...]
  transfers between devices with their start and end apart: 5 -> 5, of which waited for: 5 -> 3; matrix products, arithmetic and copies ran while one was open for 1% -> 0% of each run, Pallas kernels for 0% -> 0%
where the time goes in v1:
time: 228 us; the launch traced here: 227 us
  blocking collectives  160 us (70%)
  starting transfers between devices  49.1 us (22%)
  Pallas kernels  8.16 us (4%)
  waiting for transfers between devices  5.68 us (2%)
  local copies, waits for them, and re-layouts  3.3 us (1%)
    all_to_all x2, blocking collectives, scatter_dp(): parts = lax.all_to_all(both, ('x', 'zl'), 0, 0, tiled=True)  50 us
    all_gather x2, blocking collectives, gather_dp(): along_z = lax.all_gather(shard, 'zl', axis=0, tiled=True)  23.3 us
    all_gather x2, blocking collectives, gather_dp(): own = lax.all_gather(along_z, 'x', axis=0, tiled=True)  22.9 us
    all_gather x1, blocking collectives, shards(): mine = lax.all_gather(tok, 'y', axis=0)  22.2 us
    all_gather x1, blocking collectives, shards(): theirs = lax.all_gather(other, 'y', axis=0)  21.3 us
    ppermute x2, starting transfers between devices, scatter_dp(): got = lax.ppermute(send, 'core', swap(2, 1))  20 us
    psum x2, blocking collectives, shards(): square = lax.psum(lax.psum(square, 'zh'), 'y')  19.9 us
    ppermute x2, starting transfers between devices, gather_dp(): return (own, lax.ppermute(own, 'core', swap(2, 1)))  17.5 us
  transfers between devices with their start and end apart: 5, of which 3 were waited for; matrix products, arithmetic and copies ran while one was open for 0% of the time, Pallas kernels for 0%

profile of v1, /device:TPU:1, one launch (start us, length us, event | category | flops | bytes accessed | tf_op | source)
XLA Modules:
  0.0 227.4 jit_solution(5769759026168935743)
XLA Ops:
  0.0 11.6 %collective-permute-start = (bf16[192,256]{1,0:T(8,128)(2,1)}, bf16[192,256]{1,0:T(8,128)(2,1)S(1)}, u32[]{:S(2)}, u32[]{:S(2)}) collective-permute-start(bf16[192,256]{1,0:T(8,128)(2,1)} %bitcast.7), channel_id=1, source_target_pairs={{0,1},{1,0},{2,3},{3,2},{4,5},{5,4},{6,7},{7,6},{8,9},{9,8},{10,11... | collective-permute-start | bytes 294920 | tf_op jit(solution)/shard_map/ppermute | solution.py:152
  11.6 12.5 %all_gather.28 = bf16[384,256]{1,0:T(8,128)(2,1)S(1)} all-gather(bf16[96,256]{1,0:T(8,128)(2,1)} %param.9), channel_id=1, replica_groups=mesh['zl'=4,'x'=4,'core'=2,'y'=8,'zh'=2] {'zl'}, dimensions={0}, use_global_device_ids=true | all-gather | bytes 245760 | tf_op jit(solution)/shard_map/all_gather | solution.py:130
  24.1 11.5 %all_gather.29.refs_3_ = bf16[1536,256]{1,0:T(8,128)(2,1)S(1)} all-gather(bf16[384,256]{1,0:T(8,128)(2,1)S(1)} %all_gather.28), channel_id=1, replica_groups=mesh['zl'=4,'x'=4,'core'=2,'y'=8,'zh'=2] {'x'}, dimensions={0}, use_global_device_ids=true | all-gather | bytes 983040 | tf_op jit(solution)/shard_map/all_gather | solution.py:131
  35.6 8.3 %collective-permute-start.1 = (bf16[1536,256]{1,0:T(8,128)(2,1)S(1)}, bf16[1536,256]{1,0:T(8,128)(2,1)S(1)}, u32[]{:S(2)}, u32[]{:S(2)}) collective-permute-start(bf16[1536,256]{1,0:T(8,128)(2,1)S(1)} %all_gather.29.refs_3_), channel_id=1, source_target_pairs={{0,16},{16,0},{1,17},{17,1},{2,18},{18,2},{3,19},{19,3},{4,20},{20... | collective-permute-start | bytes 2359304 | tf_op jit(solution)/shard_map/ppermute | solution.py:132
  44.0 22.2 %all-gather = bf16[1536,256]{1,0:T(8,128)(2,1)S(1)} all-gather(bf16[192,256]{1,0:T(8,128)(2,1)} %bitcast.8), channel_id=2, replica_groups=mesh['zl'=4,'x'=4,'core'=2,'y'=8,'zh'=2] {'y'}, dimensions={0}, use_global_device_ids=true | all-gather | bytes 884736 | tf_op jit(solution)/shard_map/all_gather | solution.py:154
  66.1 0.1 pad_add_fusion.refs_0_
  66.2 0.0 collective-permute-done
  66.2 21.3 %all-gather.1 = bf16[1536,256]{1,0:T(8,128)(2,1)S(1)} all-gather(bf16[192,256]{1,0:T(8,128)(2,1)S(1)} %collective-permute-done), channel_id=3, replica_groups=mesh['zl'=4,'x'=4,'core'=2,'y'=8,'zh'=2] {'y'}, dimensions={0}, use_global_device_ids=true | all-gather | bytes 884736 | tf_op jit(solution)/shard_map/all_gather | solution.py:156
  87.5 0.0 collective-permute-done.1.refs_4_
  87.5 5.6 %shard_map.55 = (bf16[2,16,96,256]{3,2,1,0:T(8,128)(2,1)}, bf16[256,3072]{1,0:T(8,128)(2,1)}, f32[256,256]{1,0:T(8,128)S(1)}, bf16[16,96,256]{2,1,0:T(8,128)(2,1)S(1)}, bf16[16,96,256]{2,1,0:T(8,128)(2,1)S(1)}) custom-call(s32[2]{0:T(128)S(1)} %pad_add_fusion.refs_0_, bf16[8,192,256]{2,1,0:T(8,128)(2,1)S(1)} %bitcast.5, bf16[8,192,256]{2,1,0:T(8,128)(2,1)S(1)} %bitcast.6, ...), custom_call_target="tpu_custom_call" | custom-call | tf_op jit(solution)/shard_map/pallas_call | solution.py:110
  93.1 0.7 copy-done.5
  93.8 12.8 %collective-permute-start.2 = (bf16[16,96,256]{2,1,0:T(8,128)(2,1)S(1)}, bf16[16,96,256]{2,1,0:T(8,128)(2,1)S(1)}, u32[]{:S(2)}, u32[]{:S(2)}) collective-permute-start(bf16[16,96,256]{2,1,0:T(8,128)(2,1)S(1)} %get-tuple-element.18), channel_id=1, source_target_pairs={{0,16},{16,0},{1,17},{17,1},{2,18},{18,2},{3,19},{19,3},{4,20},{20... | collective-permute-start | bytes 2359304 | tf_op jit(solution)/shard_map/ppermute | solution.py:136
  106.7 1.9 collective-permute-done.2
  108.5 0.2 add_convert_fusion.1
  108.8 25.9 %all_to_all.10 = bf16[16,96,256]{2,1,0:T(8,128)(2,1)S(1)} all-to-all(bf16[16,96,256]{2,1,0:T(8,128)(2,1)S(1)} %add_convert_fusion.1), channel_id=1, replica_groups=mesh['zl'=4,'x'=4,'core'=2,'y'=8,'zh'=2] {'x','zl'}, dimensions={0} | all-to-all | bytes 1572864 | tf_op jit(solution)/shard_map/all_to_all | solution.py:138
  134.7 0.1 reduce_sum.21
  134.9 10.8 %all_gather.30 = bf16[384,256]{1,0:T(8,128)(2,1)S(1)} all-gather(bf16[96,256]{1,0:T(8,128)(2,1)S(1)} %reduce_sum.21), channel_id=1, replica_groups=mesh['zl'=4,'x'=4,'core'=2,'y'=8,'zh'=2] {'zl'}, dimensions={0}, use_global_device_ids=true | all-gather | bytes 245760 | tf_op jit(solution)/shard_map/all_gather | solution.py:130
  145.7 11.4 %all_gather.31.own_ref = bf16[1536,256]{1,0:T(8,128)(2,1)S(1)} all-gather(bf16[384,256]{1,0:T(8,128)(2,1)S(1)} %all_gather.30), channel_id=1, replica_groups=mesh['zl'=4,'x'=4,'core'=2,'y'=8,'zh'=2] {'x'}, dimensions={0}, use_global_device_ids=true | all-gather | bytes 983040 | tf_op jit(solution)/shard_map/all_gather | solution.py:131
  157.0 9.1 %collective-permute-start.3 = (bf16[1536,256]{1,0:T(8,128)(2,1)S(1)}, bf16[1536,256]{1,0:T(8,128)(2,1)S(1)}, u32[]{:S(2)}, u32[]{:S(2)}) collective-permute-start(bf16[1536,256]{1,0:T(8,128)(2,1)S(1)} %all_gather.31.own_ref), channel_id=1, source_target_pairs={{0,16},{16,0},{1,17},{17,1},{2,18},{18,2},{3,19},{19,3},{4,20},{20... | collective-permute-start | bytes 2359304 | tf_op jit(solution)/shard_map/ppermute | solution.py:132
  166.2 1.9 collective-permute-done.3.oth_ref
  168.1 0.8 shard_map.56
  168.9 0.7 copy-done.7
  169.6 7.7 %psum.14 = f32[8,256]{1,0:T(8,128)S(1)} all-reduce(f32[8,256]{1,0:T(8,128)S(1)} %get-tuple-element.19), channel_id=1, replica_groups=mesh['zl'=4,'x'=4,'core'=2,'y'=8,'zh'=2] {'zh'}, use_global_device_ids=true, to_apply=%region_1.0 | all-reduce | flops 2048 | bytes 16384 | tf_op jit(solution)/shard_map/psum | solution.py:168
  177.3 12.2 %psum.15.refs_0_ = f32[8,256]{1,0:T(8,128)S(1)} all-reduce(f32[8,256]{1,0:T(8,128)S(1)} %psum.14), channel_id=1, replica_groups=mesh['zl'=4,'x'=4,'core'=2,'y'=8,'zh'=2] {'y'}, use_global_device_ids=true, to_apply=%region_2.0 | all-reduce | flops 2048 | bytes 16384 | tf_op jit(solution)/shard_map/psum | solution.py:168
  189.6 0.9 copy-done.6
  190.5 0.9 copy-done.8
  191.5 1.8 shard_map.57
  193.2 7.2 %collective-permute-start.4 = (bf16[16,96,256]{2,1,0:T(8,128)(2,1)S(1)}, bf16[16,96,256]{2,1,0:T(8,128)(2,1)S(1)}, u32[]{:S(2)}, u32[]{:S(2)}) collective-permute-start(bf16[16,96,256]{2,1,0:T(8,128)(2,1)S(1)} %get-tuple-element.24), channel_id=1, source_target_pairs={{0,16},{16,0},{1,17},{17,1},{2,18},{18,2},{3,19},{19,3},{4,20},{20... | collective-permute-start | bytes 2359304 | tf_op jit(solution)/shard_map/ppermute | solution.py:136
  200.4 1.9 collective-permute-done.4
  202.3 0.3 add_convert_fusion
  202.6 24.1 %all_to_all.11 = bf16[16,96,256]{2,1,0:T(8,128)(2,1)S(1)} all-to-all(bf16[16,96,256]{2,1,0:T(8,128)(2,1)S(1)} %add_convert_fusion), channel_id=1, replica_groups=mesh['zl'=4,'x'=4,'core'=2,'y'=8,'zh'=2] {'x','zl'}, dimensions={0} | all-to-all | bytes 1572864 | tf_op jit(solution)/shard_map/all_to_all | solution.py:138
  226.6 0.7 convert_reduce_fusion
  (14 shorter events, 0.0 us)
Async XLA Ops:
  0.0 87.5 %copy-start.4 = (bf16[256,256]{1,0:T(8,128)(2,1)S(1)}, bf16[256,256]{1,0:T(8,128)(2,1)}, u32[]{:S(2)}) copy-start(bf16[256,256]{1,0:T(8,128)(2,1)} %refs_6_.3) | copy-start | bytes 393220
  0.0 87.5 %copy-start.3 = (bf16[256,256]{1,0:T(8,128)(2,1)S(1)}, bf16[256,256]{1,0:T(8,128)(2,1)}, u32[]{:S(2)}) copy-start(bf16[256,256]{1,0:T(8,128)(2,1)} %refs_5_.3) | copy-start | bytes 393220
  0.0 87.5 %copy-start.2 = (bf16[256,256]{1,0:T(8,128)(2,1)S(1)}, bf16[256,256]{1,0:T(8,128)(2,1)}, u32[]{:S(2)}) copy-start(bf16[256,256]{1,0:T(8,128)(2,1)} %refs_4_.1) | copy-start | bytes 393220
  0.0 66.2 %collective-permute-start = (bf16[192,256]{1,0:T(8,128)(2,1)}, bf16[192,256]{1,0:T(8,128)(2,1)S(1)}, u32[]{:S(2)}, u32[]{:S(2)}) collective-permute-start(bf16[192,256]{1,0:T(8,128)(2,1)} %bitcast.7), channel_id=1, source_target_pairs={{0,1},{1,0},{2,3},{3,2},{4,5},{5,4},{6,7},{7,6},{8,9},{9,8},{10,11... | collective-permute-start | bytes 294920 | tf_op jit(solution)/shard_map/ppermute | solution.py:152
  35.6 51.9 %collective-permute-start.1 = (bf16[1536,256]{1,0:T(8,128)(2,1)S(1)}, bf16[1536,256]{1,0:T(8,128)(2,1)S(1)}, u32[]{:S(2)}, u32[]{:S(2)}) collective-permute-start(bf16[1536,256]{1,0:T(8,128)(2,1)S(1)} %all_gather.29.refs_3_), channel_id=1, source_target_pairs={{0,16},{16,0},{1,17},{17,1},{2,18},{18,2},{3,19},{19,3},{4,20},{20... | collective-permute-start | bytes 2359304 | tf_op jit(solution)/shard_map/ppermute | solution.py:132
  93.1 0.7 copy-start.5
  93.8 14.7 %collective-permute-start.2 = (bf16[16,96,256]{2,1,0:T(8,128)(2,1)S(1)}, bf16[16,96,256]{2,1,0:T(8,128)(2,1)S(1)}, u32[]{:S(2)}, u32[]{:S(2)}) collective-permute-start(bf16[16,96,256]{2,1,0:T(8,128)(2,1)S(1)} %get-tuple-element.18), channel_id=1, source_target_pairs={{0,16},{16,0},{1,17},{17,1},{2,18},{18,2},{3,19},{19,3},{4,20},{20... | collective-permute-start | bytes 2359304 | tf_op jit(solution)/shard_map/ppermute | solution.py:136
  108.8 59.3 %copy-start.1 = (bf16[256,3072]{1,0:T(8,128)(2,1)S(1)}, bf16[256,3072]{1,0:T(8,128)(2,1)}, u32[]{:S(2)}) copy-start(bf16[256,3072]{1,0:T(8,128)(2,1)} %get-tuple-element.16.normed_ref) | copy-start | bytes 4718596
  157.0 11.0 %collective-permute-start.3 = (bf16[1536,256]{1,0:T(8,128)(2,1)S(1)}, bf16[1536,256]{1,0:T(8,128)(2,1)S(1)}, u32[]{:S(2)}, u32[]{:S(2)}) collective-permute-start(bf16[1536,256]{1,0:T(8,128)(2,1)S(1)} %all_gather.31.own_ref), channel_id=1, source_target_pairs={{0,16},{16,0},{1,17},{17,1},{2,18},{18,2},{3,19},{19,3},{4,20},{20... | collective-permute-start | bytes 2359304 | tf_op jit(solution)/shard_map/ppermute | solution.py:132
  168.1 21.5 %copy-start = (bf16[2,16,96,256]{3,2,1,0:T(8,128)(2,1)S(1)}, bf16[2,16,96,256]{3,2,1,0:T(8,128)(2,1)}, u32[]{:S(2)}) copy-start(bf16[2,16,96,256]{3,2,1,0:T(8,128)(2,1)} %get-tuple-element.22.refs_3_) | copy-start | bytes 4718596
  168.9 0.7 copy-start.7
  189.6 1.0 copy-start.6
  190.5 0.9 copy-start.8
  193.2 9.1 %collective-permute-start.4 = (bf16[16,96,256]{2,1,0:T(8,128)(2,1)S(1)}, bf16[16,96,256]{2,1,0:T(8,128)(2,1)S(1)}, u32[]{:S(2)}, u32[]{:S(2)}) collective-permute-start(bf16[16,96,256]{2,1,0:T(8,128)(2,1)S(1)} %get-tuple-element.24), channel_id=1, source_target_pairs={{0,16},{16,0},{1,17},{17,1},{2,18},{18,2},{3,19},{19,3},{4,20},{20... | collective-permute-start | bytes 2359304 | tf_op jit(solution)/shard_map/ppermute | solution.py:136

commit v2 on v1

--- a/solution.py
+++ b/solution.py
@@ -50,28 +50,24 @@
     return (2 * (y % 2) + zh) * 4 + y // 2
 
 
-def first_kernel(scale, at_ref, mine_ref, theirs_ref, w_own_ref, w_oth_ref, keys_ref, values_ref, cot_ref,
+def first_kernel(scale, at_ref, tok_ref, w_own_ref, w_oth_ref, keys_ref, values_ref, cot_ref,
                  normt_ref, normed_ref, query_ref, keep_ref, send_ref):
     core, zh = at_ref[0], at_ref[1]
-    count = mine_ref.shape[0]
-    width = 2 * count * mine_ref.shape[1]
-    total = jnp.zeros((1, mine_ref.shape[2]), F32)
-    for ref in (mine_ref, theirs_ref):
-        for y in range(count):
-            total += jnp.sum(ref[y].astype(F32), 0, keepdims=True)
+    count, width = tok_ref.shape[0], tok_ref.shape[0] * tok_ref.shape[1]
+    total = jnp.zeros((1, tok_ref.shape[2]), F32)
+    for y in range(count):
+        total += jnp.sum(tok_ref[y].astype(F32), 0, keepdims=True)
     mean = total / width
     total = jnp.zeros_like(total)
-    for ref in (mine_ref, theirs_ref):
-        for y in range(count):
-            center = ref[y].astype(F32) - mean
-            total += jnp.sum(center * center, 0, keepdims=True)
+    for y in range(count):
+        center = tok_ref[y].astype(F32) - mean
+        total += jnp.sum(center * center, 0, keepdims=True)
     inverse = lax.rsqrt(total / width + EPS)
-    for ref, z in ((mine_ref, zh), (theirs_ref, 1 - zh)):
-        for y in range(count):
-            block = ((ref[y].astype(F32) - mean) * inverse).astype(BF16)
-            for c in range(2):
-                half = jnp.bitwise_xor(core, c)
-                normt_ref[half, place(y, z)] = block[c * ROWS:(c + 1) * ROWS]
+    for y in range(count):
+        block = ((tok_ref[y].astype(F32) - mean) * inverse).astype(BF16)
+        for part in range(4):
+            half = jnp.bitwise_xor(core, part % 2)
+            normt_ref[half, place(y, jnp.bitwise_xor(zh, part // 2))] = block[part * ROWS:(part + 1) * ROWS]
     half_rows = w_own_ref.shape[0]
     for half in range(2):
         rows = normt_ref[half].reshape(half_rows, normt_ref.shape[3])
@@ -88,12 +84,13 @@
     half_rows = own_ref.shape[0]
     out_ref[...] = mm(normed_ref[:, :half_rows], own_ref[...]) + mm(normed_ref[:, half_rows:], oth_ref[...])
     own, oth = own_ref[...].astype(F32), oth_ref[...].astype(F32)
-    square_ref[...] = jnp.sum((own * own + oth * oth).reshape(-1, 8, own.shape[1]), 0)
+    square = jnp.sum((own * own + oth * oth).reshape(-1, 8, own.shape[1]), 0)
+    square_ref[...] = square[:, :HEAD] + square[:, HEAD:]
 
 
 def second_kernel(scale, radius, square_ref, query_ref, move_ref, normt_ref, keys_ref, values_ref, cot_ref,
                   keep_ref, send_ref):
-    norm = jnp.sqrt(jnp.sum(square_ref[...], keepdims=True))
+    norm = jnp.sqrt(jnp.sum(jnp.sum(square_ref[...], 0), keepdims=True))
     query = query_ref[...] + (radius / norm) * move_ref[...]
     dq = query_grad(query, keys_ref[...], values_ref[...], cot_ref[...])
     half_rows = keep_ref.shape[0] * keep_ref.shape[1]
@@ -151,21 +148,19 @@
 
     other = lax.ppermute(tok, "zh", swap(2, 1))
     w_own, w_oth = gather_dp(query_weight)
-    mine = lax.all_gather(tok, "y", axis=0)
-    other = after(other, mine)
-    theirs = lax.all_gather(other, "y", axis=0)
+    both = lax.all_gather(jnp.concatenate([tok, other], 0), "y", axis=0)
 
     half = (16, ROWS, cols)
     normt, normed, query, keep, send = call(
         lambda *refs: first_kernel(scale, *refs),
         [((2, 16, ROWS, count), BF16), ((count, model_width), BF16), ((count, cols), F32), (half, BF16), (half, BF16)],
         smem=1,
-    )(at, mine, theirs, w_own, w_oth, keys, values, cotangent)
+    )(at, both, w_own, w_oth, keys, values, cotangent)
 
     first = scatter_dp(keep, send)
     own, oth = gather_dp(first.astype(BF16))
-    move, square = call(project_kernel, [((count, cols), F32), ((8, cols), F32)])(normed, own, oth)
-    square = lax.psum(lax.psum(square, "zh"), "y")
+    move, square = call(project_kernel, [((count, cols), F32), ((8, HEAD), F32)])(normed, own, oth)
+    square = lax.all_to_all(jnp.broadcast_to(square, (16, *square.shape)), ("y", "zh"), 0, 0, tiled=True)
     keep, send = call(
         lambda *refs: second_kernel(scale, radius, *refs), [(half, BF16), (half, BF16)]
     )(square, query, move, normt, keys, values, cotangent)

time: 228 us -> 202 us (0.89)
  blocking collectives: 160 us -> 119 us
  between operations: 0.14 us -> 13.5 us
  waiting for transfers between devices: 5.68 us -> 16.9 us
  starting transfers between devices: 49.1 us -> 39.8 us
    all_gather x2 -> x0, blocking collectives: 43.5 us -> none  [the longest x1 22.2 us: shards(): mine = lax.all_gather(tok, 'y', axis=0)]
    psum x2 -> x0, blocking collectives: 19.9 us -> none  [shards(): square = lax.psum(lax.psum(square, 'zh'), 'y')]
    all_to_all x0 -> x1, blocking collectives: none -> 18.6 us  [shards(): lax.all_to_all(jnp.broadcast_to(square, (16, *square.shape)), ('y', 'zh')...]
    ppermute x2, starting transfers between devices: 20 us -> 10.4 us  [scatter_dp(): got = lax.ppermute(send, 'core', swap(2, 1))]
    all_gather x0 -> x1, waiting for transfers between devices: none -> 7.07 us  [shards(): both = lax.all_gather(jnp.concatenate([tok, other], 0), 'y', axis=0)]
    all_to_all x2, blocking collectives: 50 us -> 52.7 us  [scatter_dp(): parts = lax.all_to_all(both, ('x', 'zl'), 0, 0, tiled=True)]
    ppermute x1, waiting for transfers between devices: 0.01 us -> 2.3 us  [shards(): other = lax.ppermute(tok, 'zh', swap(2, 1))]
  transfers between devices with their start and end apart: 5 -> 6, of which waited for: 3 -> 6; matrix products, arithmetic and copies ran while one was open for 0% -> 0% of each run, Pallas kernels for 0% -> 0%
where the time goes in v2:
time: 202 us
  blocking collectives  119 us (59%)
  starting transfers between devices  39.8 us (20%)
  waiting for transfers between devices  16.9 us (8%)
  between operations  13.5 us (7%)
  Pallas kernels  8.23 us (4%)
  other arithmetic  2.97 us (1%)
    all_to_all x2, blocking collectives, scatter_dp(): parts = lax.all_to_all(both, ('x', 'zl'), 0, 0, tiled=True)  52.7 us
    all_gather x2, blocking collectives, gather_dp(): along_z = lax.all_gather(shard, 'zl', axis=0, tiled=True)  24.4 us
    all_gather x2, blocking collectives, gather_dp(): own = lax.all_gather(along_z, 'x', axis=0, tiled=True)  23.1 us
    all_to_all x1, blocking collectives, shards(): lax.all_to_all(jnp.broadcast_to(square, (16, *square.shape)), ('y', 'zh')...  18.6 us
    ppermute x2, starting transfers between devices, gather_dp(): return (own, lax.ppermute(own, 'core', swap(2, 1)))  17.9 us
    ppermute x1, starting transfers between devices, shards(): other = lax.ppermute(tok, 'zh', swap(2, 1))  11.6 us
    ppermute x2, starting transfers between devices, scatter_dp(): got = lax.ppermute(send, 'core', swap(2, 1))  10.4 us
    pallas_call x3, Pallas kernels, run(): pl.pallas_call(kernel, out_shape=[jax.ShapeDtypeStruct(s, d) for s, d in...  8.23 us
  transfers between devices with their start and end apart: 6, of which 6 were waited for; matrix products, arithmetic and copies ran while one was open for 0% of the time, Pallas kernels for 0%

profile of v2, /device:TPU:1, one launch (start us, length us, event | category | flops | bytes accessed | tf_op | source)
XLA Modules:
  0.0 201.6 jit_solution(3875043143470571403)
XLA Ops:
  6.5 0.0 all-gather.3.cloned.1.call-start
  6.5 11.6 %collective-permute-start = (bf16[192,256]{1,0:T(8,128)(2,1)}, bf16[192,256]{1,0:T(8,128)(2,1)S(1)}, u32[]{:S(2)}, u32[]{:S(2)}) collective-permute-start(bf16[192,256]{1,0:T(8,128)(2,1)} %bitcast.5), channel_id=1, source_target_pairs={{0,1},{1,0},{2,3},{3,2},{4,5},{5,4},{6,7},{7,6},{8,9},{9,8},{10,11... | collective-permute-start | bytes 294920 | tf_op jit(solution)/shard_map/ppermute | solution.py:149
  18.1 2.3 %collective-permute-done = bf16[192,256]{1,0:T(8,128)(2,1)S(1)} collective-permute-done((bf16[192,256]{1,0:T(8,128)(2,1)}, bf16[192,256]{1,0:T(8,128)(2,1)S(1)}, u32[]{:S(2)}, u32[]{:S(2)}) %collective-permute-start) | collective-permute-done | bytes 98336 | tf_op jit(solution)/shard_map/ppermute | solution.py:149
  20.4 1.6 pad_maximum_fusion
  22.0 0.0 all-gather.3.cloned.1.call-update
  22.0 13.6 %all_gather.20 = bf16[384,256]{1,0:T(8,128)(2,1)S(1)} all-gather(bf16[96,256]{1,0:T(8,128)(2,1)} %param.9), channel_id=1, replica_groups=mesh['zl'=4,'x'=4,'core'=2,'y'=8,'zh'=2] {'zl'}, dimensions={0}, use_global_device_ids=true | all-gather | bytes 245760 | tf_op jit(solution)/shard_map/all_gather | solution.py:127
  35.7 11.7 %all_gather.21.refs_2_ = bf16[1536,256]{1,0:T(8,128)(2,1)S(1)} all-gather(bf16[384,256]{1,0:T(8,128)(2,1)S(1)} %all_gather.20), channel_id=1, replica_groups=mesh['zl'=4,'x'=4,'core'=2,'y'=8,'zh'=2] {'x'}, dimensions={0}, use_global_device_ids=true | all-gather | bytes 983040 | tf_op jit(solution)/shard_map/all_gather | solution.py:128
  47.3 8.7 %collective-permute-start.1 = (bf16[1536,256]{1,0:T(8,128)(2,1)S(1)}, bf16[1536,256]{1,0:T(8,128)(2,1)S(1)}, u32[]{:S(2)}, u32[]{:S(2)}) collective-permute-start(bf16[1536,256]{1,0:T(8,128)(2,1)S(1)} %all_gather.21.refs_2_), channel_id=1, source_target_pairs={{0,16},{16,0},{1,17},{17,1},{2,18},{18,2},{3,19},{19,3},{4,20},{20... | collective-permute-start | bytes 2359304 | tf_op jit(solution)/shard_map/ppermute | solution.py:129
  56.1 0.1 pad_add_fusion.refs_0_
  56.2 1.8 collective-permute-done.1.refs_3_
  58.0 7.1 %all-gather.3.cloned.1.call-done = bf16[3072,256]{1,0:T(8,128)(2,1)} async-done(((bf16[384,256]{1,0:T(8,128)(2,1)}), bf16[3072,256]{1,0:T(8,128)(2,1)}) %all-gather.3.cloned.1.call-update) | async-done | bytes 1572880 | tf_op jit(solution)/shard_map/all_gather | solution.py:151
  65.1 0.0 copy-done.3
  65.1 5.6 %shard_map.55 = (bf16[2,16,96,256]{3,2,1,0:T(8,128)(2,1)S(1)}, bf16[256,3072]{1,0:T(8,128)(2,1)}, f32[256,256]{1,0:T(8,128)S(1)}, bf16[16,96,256]{2,1,0:T(8,128)(2,1)S(1)}, bf16[16,96,256]{2,1,0:T(8,128)(2,1)S(1)}) custom-call(s32[2]{0:T(128)S(1)} %pad_add_fusion.refs_0_, bf16[8,384,256]{2,1,0:T(8,128)(2,1)} %bitcast.4, ...), custom_call_target="tpu_custom_call" | custom-call | tf_op jit(solution)/shard_map/pallas_call | solution.py:107
  70.7 6.6 %collective-permute-start.2 = (bf16[16,96,256]{2,1,0:T(8,128)(2,1)S(1)}, bf16[16,96,256]{2,1,0:T(8,128)(2,1)S(1)}, u32[]{:S(2)}, u32[]{:S(2)}) collective-permute-start(bf16[16,96,256]{2,1,0:T(8,128)(2,1)S(1)} %get-tuple-element.16), channel_id=1, source_target_pairs={{0,16},{16,0},{1,17},{17,1},{2,18},{18,2},{3,19},{19,3},{4,20},{20... | collective-permute-start | bytes 2359304 | tf_op jit(solution)/shard_map/ppermute | solution.py:133
  77.4 1.9 collective-permute-done.2
  79.3 0.2 add_convert_fusion.1
  79.5 28.6 %all_to_all.15 = bf16[16,96,256]{2,1,0:T(8,128)(2,1)S(1)} all-to-all(bf16[16,96,256]{2,1,0:T(8,128)(2,1)S(1)} %add_convert_fusion.1), channel_id=1, replica_groups=mesh['zl'=4,'x'=4,'core'=2,'y'=8,'zh'=2] {'x','zl'}, dimensions={0} | all-to-all | bytes 1572864 | tf_op jit(solution)/shard_map/all_to_all | solution.py:135
  108.2 0.1 reduce_sum.21
  108.3 10.8 %all_gather.22 = bf16[384,256]{1,0:T(8,128)(2,1)S(1)} all-gather(bf16[96,256]{1,0:T(8,128)(2,1)S(1)} %reduce_sum.21), channel_id=1, replica_groups=mesh['zl'=4,'x'=4,'core'=2,'y'=8,'zh'=2] {'zl'}, dimensions={0}, use_global_device_ids=true | all-gather | bytes 245760 | tf_op jit(solution)/shard_map/all_gather | solution.py:127
  119.1 11.4 %all_gather.23.own_ref = bf16[1536,256]{1,0:T(8,128)(2,1)S(1)} all-gather(bf16[384,256]{1,0:T(8,128)(2,1)S(1)} %all_gather.22), channel_id=1, replica_groups=mesh['zl'=4,'x'=4,'core'=2,'y'=8,'zh'=2] {'x'}, dimensions={0}, use_global_device_ids=true | all-gather | bytes 983040 | tf_op jit(solution)/shard_map/all_gather | solution.py:128
  130.5 9.1 %collective-permute-start.3 = (bf16[1536,256]{1,0:T(8,128)(2,1)S(1)}, bf16[1536,256]{1,0:T(8,128)(2,1)S(1)}, u32[]{:S(2)}, u32[]{:S(2)}) collective-permute-start(bf16[1536,256]{1,0:T(8,128)(2,1)S(1)} %all_gather.23.own_ref), channel_id=1, source_target_pairs={{0,16},{16,0},{1,17},{17,1},{2,18},{18,2},{3,19},{19,3},{4,20},{20... | collective-permute-start | bytes 2359304 | tf_op jit(solution)/shard_map/ppermute | solution.py:129
  139.6 1.9 collective-permute-done.3.oth_ref
  141.5 1.4 copy-done
  142.9 0.8 shard_map.56
  143.7 18.6 %all_to_all.16.refs_0_ = f32[16,8,128]{2,1,0:T(8,128)S(1)} all-to-all(f32[16,8,128]{2,1,0:T(8,128)S(1)} %broadcast_in_dim.3), channel_id=1, replica_groups=mesh['zl'=4,'x'=4,'core'=2,'y'=8,'zh'=2] {'y','zh'}, dimensions={0} | all-to-all | bytes 131072 | tf_op jit(solution)/shard_map/all_to_all | solution.py:163
  162.4 0.0 copy-done.5
  162.4 1.8 shard_map.57
  164.1 3.7 %collective-permute-start.4 = (bf16[16,96,256]{2,1,0:T(8,128)(2,1)S(1)}, bf16[16,96,256]{2,1,0:T(8,128)(2,1)S(1)}, u32[]{:S(2)}, u32[]{:S(2)}) collective-permute-start(bf16[16,96,256]{2,1,0:T(8,128)(2,1)S(1)} %get-tuple-element.22), channel_id=1, source_target_pairs={{0,16},{16,0},{1,17},{17,1},{2,18},{18,2},{3,19},{19,3},{4,20},{20... | collective-permute-start | bytes 2359304 | tf_op jit(solution)/shard_map/ppermute | solution.py:133
  167.8 1.9 collective-permute-done.4
  169.7 0.2 add_convert_fusion
  170.0 24.1 %all_to_all.17 = bf16[16,96,256]{2,1,0:T(8,128)(2,1)S(1)} all-to-all(bf16[16,96,256]{2,1,0:T(8,128)(2,1)S(1)} %add_convert_fusion), channel_id=1, replica_groups=mesh['zl'=4,'x'=4,'core'=2,'y'=8,'zh'=2] {'x','zl'}, dimensions={0} | all-to-all | bytes 1572864 | tf_op jit(solution)/shard_map/all_to_all | solution.py:135
  194.0 0.7 convert_reduce_fusion
  (10 shorter events, 0.0 us)
Async XLA Ops:
  6.5 58.5 %copy-start.3 = (bf16[256,256]{1,0:T(8,128)(2,1)S(1)}, bf16[256,256]{1,0:T(8,128)(2,1)}, u32[]{:S(2)}) copy-start(bf16[256,256]{1,0:T(8,128)(2,1)} %refs_6_.3) | copy-start | bytes 393220
  6.5 58.5 %copy-start.2 = (bf16[256,256]{1,0:T(8,128)(2,1)S(1)}, bf16[256,256]{1,0:T(8,128)(2,1)}, u32[]{:S(2)}) copy-start(bf16[256,256]{1,0:T(8,128)(2,1)} %refs_5_.3) | copy-start | bytes 393220
  6.5 58.5 %copy-start.1 = (bf16[256,256]{1,0:T(8,128)(2,1)S(1)}, bf16[256,256]{1,0:T(8,128)(2,1)}, u32[]{:S(2)}) copy-start(bf16[256,256]{1,0:T(8,128)(2,1)} %refs_4_.3) | copy-start | bytes 393220
  6.5 58.5 %all-gather.3.cloned.1.call-start = ((), (), s32[]{:S(2)}) async-start(), calls=%async_computation.3 | async-start | bytes 1769472 | tf_op jit(solution)/shard_map/all_gather | solution.py:151
  6.5 13.9 %collective-permute-start = (bf16[192,256]{1,0:T(8,128)(2,1)}, bf16[192,256]{1,0:T(8,128)(2,1)S(1)}, u32[]{:S(2)}, u32[]{:S(2)}) collective-permute-start(bf16[192,256]{1,0:T(8,128)(2,1)} %bitcast.5), channel_id=1, source_target_pairs={{0,1},{1,0},{2,3},{3,2},{4,5},{5,4},{6,7},{7,6},{8,9},{9,8},{10,11... | collective-permute-start | bytes 294920 | tf_op jit(solution)/shard_map/ppermute | solution.py:149
  47.3 10.6 %collective-permute-start.1 = (bf16[1536,256]{1,0:T(8,128)(2,1)S(1)}, bf16[1536,256]{1,0:T(8,128)(2,1)S(1)}, u32[]{:S(2)}, u32[]{:S(2)}) collective-permute-start(bf16[1536,256]{1,0:T(8,128)(2,1)S(1)} %all_gather.21.refs_2_), channel_id=1, source_target_pairs={{0,16},{16,0},{1,17},{17,1},{2,18},{18,2},{3,19},{19,3},{4,20},{20... | collective-permute-start | bytes 2359304 | tf_op jit(solution)/shard_map/ppermute | solution.py:129
  70.7 8.8 %copy-start.4 = (f32[256,256]{1,0:T(8,128)}, f32[256,256]{1,0:T(8,128)S(1)}, u32[]{:S(2)}) copy-start(f32[256,256]{1,0:T(8,128)S(1)} %get-tuple-element.18.refs_1_) | copy-start | bytes 786436
  70.7 8.5 %collective-permute-start.2 = (bf16[16,96,256]{2,1,0:T(8,128)(2,1)S(1)}, bf16[16,96,256]{2,1,0:T(8,128)(2,1)S(1)}, u32[]{:S(2)}, u32[]{:S(2)}) collective-permute-start(bf16[16,96,256]{2,1,0:T(8,128)(2,1)S(1)} %get-tuple-element.16), channel_id=1, source_target_pairs={{0,16},{16,0},{1,17},{17,1},{2,18},{18,2},{3,19},{19,3},{4,20},{20... | collective-permute-start | bytes 2359304 | tf_op jit(solution)/shard_map/ppermute | solution.py:133
  130.5 11.0 %collective-permute-start.3 = (bf16[1536,256]{1,0:T(8,128)(2,1)S(1)}, bf16[1536,256]{1,0:T(8,128)(2,1)S(1)}, u32[]{:S(2)}, u32[]{:S(2)}) collective-permute-start(bf16[1536,256]{1,0:T(8,128)(2,1)S(1)} %all_gather.23.own_ref), channel_id=1, source_target_pairs={{0,16},{16,0},{1,17},{17,1},{2,18},{18,2},{3,19},{19,3},{4,20},{20... | collective-permute-start | bytes 2359304 | tf_op jit(solution)/shard_map/ppermute | solution.py:129
  141.5 1.4 copy-start
  142.9 19.5 %copy-start.5 = (f32[256,256]{1,0:T(8,128)S(1)}, f32[256,256]{1,0:T(8,128)}, u32[]{:S(2)}) copy-start(f32[256,256]{1,0:T(8,128)} %copy-done.4) | copy-start | bytes 786436
  164.1 5.6 %collective-permute-start.4 = (bf16[16,96,256]{2,1,0:T(8,128)(2,1)S(1)}, bf16[16,96,256]{2,1,0:T(8,128)(2,1)S(1)}, u32[]{:S(2)}, u32[]{:S(2)}) collective-permute-start(bf16[16,96,256]{2,1,0:T(8,128)(2,1)S(1)} %get-tuple-element.22), channel_id=1, source_target_pairs={{0,16},{16,0},{1,17},{17,1},{2,18},{18,2},{3,19},{19,3},{4,20},{20... | collective-permute-start | bytes 2359304 | tf_op jit(solution)/shard_map/ppermute | solution.py:133
Sparse Core Ops, SparseCore 0:
  22.2 42.8 all-gather.2

commit v3 on v2

v3 whole, which is shorter than its diff:
```python
import math

import jax
import jax.numpy as jnp
from jax import lax
from jax.experimental import pallas as pl
from jax.experimental.pallas import tpu as pltpu
from jax.sharding import Mesh, PartitionSpec as P

HEAD = 128
ROWS = 96
EPS = 1e-06
F32 = jnp.float32
BF16 = jnp.bfloat16
AXES = ("zl", "x", "core", "y", "zh")
SIZES = (4, 4, 2, 8, 2)
STEPS = (0, -1, 1, -2, 2, -3, 3, -4)
VMEM_LIMIT = 48 * 1024 * 1024


def mm(a, b, dims=((1,), (0,))):
    return lax.dot_general(a, b, (dims, ((), ())), preferred_element_type=F32)


def query_grad(query, keys, values, cotangent):
    temper = 1.0 / math.sqrt(HEAD)
    heads = []
    for h in range(query.shape[1] // HEAD):
        cols = slice(h * HEAD, (h + 1) * HEAD)
        q = query[:, cols]
        key, value, cot = keys[:, cols], values[:, cols], cotangent[:, cols]
        center = q - jnp.mean(q, -1, keepdims=True)
        inverse = lax.rsqrt(jnp.mean(center * center, -1, keepdims=True) + EPS)
        qn = center * inverse
        scores = mm(qn.astype(BF16), key, ((1,), (1,))) * temper
        expon = jnp.exp(scores)
        attend = expon / jnp.sum(expon, -1, keepdims=True)
        dprob = mm(cot, value, ((1,), (1,)))
        dscore = attend * (dprob - jnp.sum(attend * dprob, -1, keepdims=True))
        dqn = mm(dscore.astype(BF16), key) * temper
        dq = inverse * (
            dqn
            - jnp.mean(dqn, -1, keepdims=True)
            - qn * jnp.mean(dqn * qn, -1, keepdims=True)
        )
        heads.append(dq.astype(BF16))
    return jnp.concatenate(heads, axis=1)


def first_kernel(scale, at_ref, *refs):
    toks, (w_ref, keys_ref, values_ref, cot_ref, normt_ref, normed_ref, query_ref, keep_ref, send_ref) = refs[:8], refs[8:]
    core, y, zh = at_ref[0], at_ref[1], at_ref[2]
    width = normed_ref.shape[1]
    total = jnp.zeros((1, normt_ref.shape[-1]), F32)
    for ref in toks:
        total += jnp.sum(ref[...].astype(F32), 0, keepdims=True)
    mean = total / width
    total = jnp.zeros_like(total)
    for ref in toks:
        center = ref[...].astype(F32) - mean
        total += jnp.sum(center * center, 0, keepdims=True)
    inverse = lax.rsqrt(total / width + EPS)
    for ref, step in zip(toks, STEPS):
        block = ((ref[...].astype(F32) - mean) * inverse).astype(BF16)
        from_y = lax.rem(y + (step + 8), 8)
        for part in range(4):
            x = 2 * lax.rem(from_y, 2) + jnp.bitwise_xor(zh, part // 2)
            normt_ref[part % 2, x, from_y // 2] = block[part * ROWS:(part + 1) * ROWS]
    run = 4 * ROWS
    for x in range(4):
        for c in range(2):
            at = (2 * x + c) * run
            normed_ref[:, at:at + run] = normt_ref[c, x].reshape(run, normt_ref.shape[-1]).T
    query = mm(normed_ref[...], w_ref[...])
    query_ref[...] = query
    dq = query_grad(query, keys_ref[...], values_ref[...], cot_ref[...])
    term(scale, core, normt_ref, dq, keep_ref, send_ref)


def term(scale, core, normt_ref, dq, keep_ref, send_ref):
    for c, ref in ((core, keep_ref), (1 - core, send_ref)):
        rows = normt_ref[c].reshape(16 * ROWS, normt_ref.shape[-1])
        ref[...] = (mm(rows, dq) * scale).astype(BF16).reshape(ref.shape)


def sum_kernel(parts_ref, first_ref, square_ref):
    total = jnp.sum(parts_ref[...].astype(F32), 0)
    first_ref[...] = total.astype(BF16)
    square = jnp.sum((total * total).reshape(-1, 8, total.shape[1]), 0)
    square_ref[...] = square[:, :HEAD] + square[:, HEAD:]


def second_kernel(scale, radius, at_ref, square_ref, query_ref, first_ref, normed_ref, normt_ref, keys_ref, values_ref,
                  cot_ref, keep_ref, send_ref):
    norm = jnp.sqrt(jnp.sum(jnp.sum(square_ref[...], 0), keepdims=True))
    query = query_ref[...] + (radius / norm) * mm(normed_ref[...], first_ref[...])
    dq = query_grad(query, keys_ref[...], values_ref[...], cot_ref[...])
    term(scale, at_ref[0], normt_ref, dq, keep_ref, send_ref)


def call(kernel, outs, smem=0):
    spec = pl.BlockSpec(memory_space=pltpu.VMEM)

    def run(*args):
        specs = [pl.BlockSpec(memory_space=pltpu.SMEM)] * smem + [spec] * (len(args) - smem)
        return pl.pallas_call(
            kernel,
            out_shape=[jax.ShapeDtypeStruct(s, d) for s, d in outs],
            in_specs=specs,
            out_specs=[spec] * len(outs),
            compiler_params=pltpu.CompilerParams(vmem_limit_bytes=VMEM_LIMIT),
        )(*args)

    return run


def swap(size, step):
    return [(i, i ^ step) for i in range(size)]


def turn(value, step):
    return lax.ppermute(value, "y", [(i, (i + step) % 8) for i in range(8)])


def after(value, *others):
    return lax.optimization_barrier((value, *others))[0]


def gather_tokens(block):
    back1, ahead1, back2, ahead2 = turn(block, 1), turn(block, 7), turn(block, 2), turn(block, 6)
    back3, ahead3, back4 = turn(back2, 1), turn(ahead2, 7), turn(back2, 2)
    return block, back1, ahead1, back2, ahead2, back3, ahead3, back4


def scatter_parts(keep, send):
    got = lax.ppermute(send, "core", swap(2, 1))
    both = (keep.astype(F32) + got.astype(F32)).astype(BF16)
    return lax.all_to_all(both, ("x", "zl"), 0, 0, tiled=True)


def everywhere(value, axes, size):
    return lax.all_to_all(jnp.broadcast_to(value, (size, *value.shape)), axes, 0, 0, tiled=True)


def shards(tokens, keys, values, cotangent, query_weight):
    tok = tokens.T
    feats, count = tok.shape
    cols = keys.shape[1]
    model_width = feats * 16
    scale = 1.0 / math.sqrt(count * 32)
    radius = 0.3 * math.sqrt(model_width + cols * 16)
    at = jnp.stack([lax.axis_index(name) for name in ("core", "y", "zh")]).astype(jnp.int32)

    other = lax.ppermute(tok, "zh", swap(2, 1))
    weight_z = lax.all_gather(query_weight, "zl", axis=0, tiled=True)
    weight_z, other = lax.optimization_barrier((weight_z, other))
    weight = lax.all_gather(weight_z, ("x", "core"), axis=0, tiled=True)
    blocks = gather_tokens(jnp.concatenate([tok, other], 0))

    half = (16, ROWS, cols)
    normt, normed, query, keep, send = call(
        lambda *refs: first_kernel(scale, *refs),
        [((2, 4, 4, ROWS, count), BF16), ((count, model_width), BF16), ((count, cols), F32), (half, BF16), (half, BF16)],
        smem=1,
    )(at, *blocks, weight, keys, values, cotangent)

    first, square = call(sum_kernel, [((ROWS, cols), BF16), ((8, HEAD), F32)])(scatter_parts(keep, send))
    first_z = lax.all_gather(first, "zl", axis=0, tiled=True)
    first_all = lax.all_gather(first_z, ("x", "core"), axis=0, tiled=True)
    square = jnp.sum(everywhere(after(square, first_z), ("zh", "y"), 16), 0)
    square = everywhere(square, ("zl", "x", "core"), 32)
    keep, send = call(
        lambda *refs: second_kernel(scale, radius, *refs), [(half, BF16), (half, BF16)], smem=1
    )(at, square, query, first_all, normed, normt, keys, values, cotangent)
    return jnp.sum(scatter_parts(keep, send).astype(F32), 0)


def solution(mesh):
    cut = Mesh(mesh.devices.reshape(SIZES), AXES)
    spec = P(("zl", "x", "core"), ("y", "zh"))
    return jax.shard_map(shards, mesh=cut, in_specs=(spec,) * 5, out_specs=spec, check_vma=False)
```

time: 202 us -> 199 us (0.985)
  blocking collectives: 119 us -> 111 us
  starting transfers between devices: 39.8 us -> 42.7 us
  local copies, waits for them, and re-layouts: 1.43 us -> 4.16 us
  waiting for transfers between devices: 16.9 us -> 14.3 us
    all_gather x4 -> x2, blocking collectives: 47.5 us -> 25.1 us  [the longest x1 13.5 us: shards(): weight_z = lax.all_gather(query_weight, 'zl', axis=0, tiled=True)]
    all_to_all x3 -> x4, blocking collectives: 71.3 us -> 86.1 us  [the longest x2 51.9 us: scatter_parts(): return lax.all_to_all(both, ('x', 'zl'), 0, 0, tiled=True)]
    all_gather x1 -> x2, waiting for transfers between devices: 7.07 us -> 0.01 us  [the longest x1 0.01 us: shards(): weight = lax.all_gather(weight_z, ('x', 'core'), axis=0, tiled=True)]
    ppermute x4 -> x9, waiting for transfers between devices: 7.48 us -> 14.3 us  [the longest x7 10.5 us: turn(): return lax.ppermute(value, 'y', [(i, (i + step) % 8) for i in range(8)])]
    ppermute x4 -> x9, starting transfers between devices: 28.2 us -> 31.2 us  [the longest x7 23.2 us: turn(): return lax.ppermute(value, 'y', [(i, (i + step) % 8) for i in range(8)])]
    unnamed x12 -> x18, local copies, waits for them, and re-layouts: 1.43 us -> 4.14 us
    ppermute x1, waiting for transfers between devices: 2.3 us -> 0.01 us  [shards(): other = lax.ppermute(tok, 'zh', swap(2, 1))]
  transfers between devices with their start and end apart: 6 -> 12, of which waited for: 6 -> 4; matrix products, arithmetic and copies ran while one was open for 0% -> 1% of each run, Pallas kernels for 0% -> 0%
where the time goes in v3:
time: 199 us; the launch traced here: 198 us
  blocking collectives  111 us (56%)
  starting transfers between devices  42.7 us (21%)
  waiting for transfers between devices  14.3 us (7%)
  between operations  13.6 us (7%)
  Pallas kernels  9.98 us (5%)
  local copies, waits for them, and re-layouts  4.16 us (2%)
  other arithmetic  2.23 us (1%)
    all_to_all x2, blocking collectives, scatter_parts(): return lax.all_to_all(both, ('x', 'zl'), 0, 0, tiled=True)  51.9 us
    all_to_all x2, blocking collectives, everywhere(): lax.all_to_all(jnp.broadcast_to(value, (size, *value.shape)), axes, 0, 0,...  34.2 us
    ppermute x7, starting transfers between devices, turn(): return lax.ppermute(value, 'y', [(i, (i + step) % 8) for i in range(8)])  23.2 us
    all_gather x1, blocking collectives, shards(): weight_z = lax.all_gather(query_weight, 'zl', axis=0, tiled=True)  13.5 us
    all_gather x1, blocking collectives, shards(): first_z = lax.all_gather(first, 'zl', axis=0, tiled=True)  11.6 us
    ppermute x1, starting transfers between devices, shards(): other = lax.ppermute(tok, 'zh', swap(2, 1))  11.5 us
    ppermute x7, waiting for transfers between devices, turn(): return lax.ppermute(value, 'y', [(i, (i + step) % 8) for i in range(8)])  10.5 us
    pallas_call x3, Pallas kernels, run(): pl.pallas_call(kernel, out_shape=[jax.ShapeDtypeStruct(s, d) for s, d in...  9.98 us
  transfers between devices with their start and end apart: 12, of which 4 were waited for; matrix products, arithmetic and copies ran while one was open for 1% of the time, Pallas kernels for 0%

profile of v3, /device:TPU:1, one launch (start us, length us, event | category | flops | bytes accessed | tf_op | source)
XLA Modules:
  0.0 198.3 jit_solution(11620161690443180251)
XLA Ops:
  6.5 11.5 %collective-permute-start = (bf16[192,256]{1,0:T(8,128)(2,1)}, bf16[192,256]{1,0:T(8,128)(2,1)S(1)}, u32[]{:S(2)}, u32[]{:S(2)}) collective-permute-start(bf16[192,256]{1,0:T(8,128)(2,1)} %bitcast.4), channel_id=1, source_target_pairs={{0,1},{1,0},{2,3},{3,2},{4,5},{5,4},{6,7},{7,6},{8,9},{9,8},{10,11... | collective-permute-start | bytes 294920 | tf_op jit(solution)/shard_map/ppermute | solution.py:154
  18.0 13.5 %all_gather.12 = bf16[384,256]{1,0:T(8,128)(2,1)} all-gather(bf16[96,256]{1,0:T(8,128)(2,1)} %param.9), channel_id=1, replica_groups=mesh['zl'=4,'x'=4,'core'=2,'y'=8,'zh'=2] {'zl'}, dimensions={0}, use_global_device_ids=true | all-gather | bytes 245760 | tf_op jit(solution)/shard_map/all_gather | solution.py:155
  31.6 0.9 pad_maximum_fusion.refs_1_
  32.5 5.9 %collective-permute-start.4 = (bf16[384,256]{1,0:T(8,128)(2,1)S(1)}, bf16[384,256]{1,0:T(8,128)(2,1)S(1)}, u32[]{:S(2)}, u32[]{:S(2)}) collective-permute-start(bf16[384,256]{1,0:T(8,128)(2,1)S(1)} %pad_maximum_fusion.refs_1_), channel_id=1, source_target_pairs={{0,12},{2,14},{4,0},{6,2},{8,4},{10,6},{12,8},{14,10},{1,13},{3,15... | collective-permute-start | bytes 589832 | tf_op jit(solution)/shard_map/ppermute | solution.py:122
  38.4 1.9 collective-permute-start.3
  40.4 4.7 %collective-permute-start.2 = (bf16[384,256]{1,0:T(8,128)(2,1)S(1)}, bf16[384,256]{1,0:T(8,128)(2,1)S(1)}, u32[]{:S(2)}, u32[]{:S(2)}) collective-permute-start(bf16[384,256]{1,0:T(8,128)(2,1)S(1)} %pad_maximum_fusion.refs_1_), channel_id=1, source_target_pairs={{0,14},{2,0},{4,2},{6,4},{8,6},{10,8},{12,10},{14,12},{1,15},{3,1}... | collective-permute-start | bytes 589832 | tf_op jit(solution)/shard_map/ppermute | solution.py:122
  45.1 1.9 collective-permute-start.1
  47.0 4.6 %collective-permute-start.6 = (bf16[384,256]{1,0:T(8,128)(2,1)S(1)}, bf16[384,256]{1,0:T(8,128)(2,1)S(1)}, u32[]{:S(2)}, u32[]{:S(2)}) collective-permute-start(bf16[384,256]{1,0:T(8,128)(2,1)S(1)} %collective-permute-done.4.refs_5_), channel_id=1, source_target_pairs={{0,14},{2,0},{4,2},{6,4},{8,6},{10,8},{12,10},{14,12},{1,15},{3,1}... | collective-permute-start | bytes 589832 | tf_op jit(solution)/shard_map/ppermute | solution.py:122
  51.6 1.9 collective-permute-start.7
  53.5 2.3 %collective-permute-start.5 = (bf16[384,256]{1,0:T(8,128)(2,1)S(1)}, bf16[384,256]{1,0:T(8,128)(2,1)S(1)}, u32[]{:S(2)}, u32[]{:S(2)}) collective-permute-start(bf16[384,256]{1,0:T(8,128)(2,1)S(1)} %collective-permute-done.3.refs_4_), channel_id=1, source_target_pairs={{0,2},{2,4},{4,6},{6,8},{8,10},{10,12},{12,14},{14,0},{1,3},{3,5},... | collective-permute-start | bytes 589832 | tf_op jit(solution)/shard_map/ppermute | solution.py:122
  55.9 0.1 pad_add_fusion.refs_0_
  55.9 6.3 %collective-permute-done.7.refs_8_ = bf16[384,256]{1,0:T(8,128)(2,1)S(1)} collective-permute-done((bf16[384,256]{1,0:T(8,128)(2,1)S(1)}, bf16[384,256]{1,0:T(8,128)(2,1)S(1)}, u32[]{:S(2)}, u32[]{:S(2)}) %collective-permute-start.7) | collective-permute-done | bytes 196640 | tf_op jit(solution)/shard_map/ppermute | solution.py:122
  62.2 4.2 %collective-permute-done.5.refs_6_ = bf16[384,256]{1,0:T(8,128)(2,1)S(1)} collective-permute-done((bf16[384,256]{1,0:T(8,128)(2,1)S(1)}, bf16[384,256]{1,0:T(8,128)(2,1)S(1)}, u32[]{:S(2)}, u32[]{:S(2)}) %collective-permute-start.5) | collective-permute-done | bytes 196640 | tf_op jit(solution)/shard_map/ppermute | solution.py:122
  66.5 0.9 copy-done.3
  67.4 0.9 copy-done.5
  68.3 0.9 copy-done.7
  69.2 5.6 %shard_map.55 = (bf16[2,4,4,96,256]{4,3,2,1,0:T(8,128)(2,1)S(1)}, bf16[256,3072]{1,0:T(8,128)(2,1)}, f32[256,256]{1,0:T(8,128)S(1)}, bf16[16,96,256]{2,1,0:T(8,128)(2,1)S(1)}, bf16[16,96,256]{2,1,0:T(8,128)(2,1)S(1)}) custom-call(s32[3]{0:T(128)S(1)} %pad_add_fusion.refs_0_, bf16[384,256]{1,0:T(8,128)(2,1)S(1)} %pad_maximum_fusion.refs_1_, ...), custom_call_target="tpu_custom_call" | custom-call | tf_op jit(solution)/shard_map/pallas_call | solution.py:106
  74.8 5.7 %collective-permute-start.8 = (bf16[16,96,256]{2,1,0:T(8,128)(2,1)S(1)}, bf16[16,96,256]{2,1,0:T(8,128)(2,1)S(1)}, u32[]{:S(2)}, u32[]{:S(2)}) collective-permute-start(bf16[16,96,256]{2,1,0:T(8,128)(2,1)S(1)} %get-tuple-element.20), channel_id=1, source_target_pairs={{0,16},{16,0},{1,17},{17,1},{2,18},{18,2},{3,19},{19,3},{4,20},{20... | collective-permute-start | bytes 2359304 | tf_op jit(solution)/shard_map/ppermute | solution.py:136
  80.5 1.9 collective-permute-done.8
  82.4 0.2 add_convert_fusion.1
  82.7 27.5 %all_to_all.20.parts_ref = bf16[16,96,256]{2,1,0:T(8,128)(2,1)S(1)} all-to-all(bf16[16,96,256]{2,1,0:T(8,128)(2,1)S(1)} %add_convert_fusion.1), channel_id=1, replica_groups=mesh['zl'=4,'x'=4,'core'=2,'y'=8,'zh'=2] {'x','zl'}, dimensions={0} | all-to-all | bytes 1572864 | tf_op jit(solution)/shard_map/all_to_all | solution.py:138
  110.2 0.1 shard_map.56
  110.3 11.6 %all_gather.14 = bf16[384,256]{1,0:T(8,128)(2,1)} all-gather(bf16[96,256]{1,0:T(8,128)(2,1)S(1)} %get-tuple-element.22), channel_id=1, replica_groups=mesh['zl'=4,'x'=4,'core'=2,'y'=8,'zh'=2] {'zl'}, dimensions={0}, use_global_device_ids=true | all-gather | bytes 245760 | tf_op jit(solution)/shard_map/all_gather | solution.py:168
  121.9 16.7 %all_to_all.21 = f32[16,8,128]{2,1,0:T(8,128)S(1)} all-to-all(f32[16,8,128]{2,1,0:T(8,128)S(1)} %broadcast_in_dim.6), channel_id=1, replica_groups=mesh['zl'=4,'x'=4,'core'=2,'y'=8,'zh'=2] {'zh','y'}, dimensions={0} | all-to-all | bytes 131072 | tf_op jit(solution)/shard_map/all_to_all | solution.py:142
  138.6 17.5 %all_to_all.22.refs_1_ = f32[32,8,128]{2,1,0:T(8,128)S(1)} all-to-all(f32[32,8,128]{2,1,0:T(8,128)S(1)} %broadcast_in_dim.7), channel_id=1, replica_groups=mesh['zl'=4,'x'=4,'core'=2,'y'=8,'zh'=2] {'zl','x','core'}, dimensions={0} | all-to-all | bytes 262144 | tf_op jit(solution)/shard_map/all_to_all | solution.py:142
  156.2 1.4 copy-done.2
  157.6 4.2 %shard_map.57 = (bf16[16,96,256]{2,1,0:T(8,128)(2,1)S(1)}, bf16[16,96,256]{2,1,0:T(8,128)(2,1)S(1)}) custom-call(s32[3]{0:T(128)S(1)} %pad_add_fusion.refs_0_, f32[32,8,128]{2,1,0:T(8,128)S(1)} %all_to_all.22.refs_1_, f32[256,256]{1,0:T(8,128)S(1)} %get-tuple-element.24.refs_2_, bf16[3072,256]{1,0:T(8,128)(2,1)S(1)} %copy-done.2, ...), custom_call_target="tpu_custom_call" | custom-call | tf_op jit(solution)/shard_map/pallas_call | solution.py:106
  161.8 2.3 %collective-permute-start.9 = (bf16[16,96,256]{2,1,0:T(8,128)(2,1)S(1)}, bf16[16,96,256]{2,1,0:T(8,128)(2,1)S(1)}, u32[]{:S(2)}, u32[]{:S(2)}) collective-permute-start(bf16[16,96,256]{2,1,0:T(8,128)(2,1)S(1)} %get-tuple-element.28), channel_id=1, source_target_pairs={{0,16},{16,0},{1,17},{17,1},{2,18},{18,2},{3,19},{19,3},{4,20},{20... | collective-permute-start | bytes 2359304 | tf_op jit(solution)/shard_map/ppermute | solution.py:136
  164.1 1.9 collective-permute-done.9
  166.0 0.2 add_convert_fusion
  166.2 24.4 %all_to_all.23 = bf16[16,96,256]{2,1,0:T(8,128)(2,1)S(1)} all-to-all(bf16[16,96,256]{2,1,0:T(8,128)(2,1)S(1)} %add_convert_fusion), channel_id=1, replica_groups=mesh['zl'=4,'x'=4,'core'=2,'y'=8,'zh'=2] {'x','zl'}, dimensions={0} | all-to-all | bytes 1572864 | tf_op jit(solution)/shard_map/all_to_all | solution.py:138
  190.7 0.7 convert_reduce_fusion
  (29 shorter events, 0.2 us)
Async XLA Ops:
  6.5 59.9 %all-gather.3.cloned.1.call-start = ((), (), s32[]{:S(2)}) async-start(), calls=%async_computation.4 | async-start | bytes 1769472 | tf_op jit(solution)/shard_map/all_gather | solution.py:157
  6.5 25.0 %collective-permute-start = (bf16[192,256]{1,0:T(8,128)(2,1)}, bf16[192,256]{1,0:T(8,128)(2,1)S(1)}, u32[]{:S(2)}, u32[]{:S(2)}) collective-permute-start(bf16[192,256]{1,0:T(8,128)(2,1)} %bitcast.4), channel_id=1, source_target_pairs={{0,1},{1,0},{2,3},{3,2},{4,5},{5,4},{6,7},{7,6},{8,9},{9,8},{10,11... | collective-permute-start | bytes 294920 | tf_op jit(solution)/shard_map/ppermute | solution.py:154
  31.6 124.6 %all-gather.5.cloned.1.call-start = ((), (), s32[]{:S(2)}) async-start(), calls=%async_computation.5 | async-start | bytes 1769472 | tf_op jit(solution)/shard_map/all_gather | solution.py:169
  32.5 14.4 %collective-permute-start.4 = (bf16[384,256]{1,0:T(8,128)(2,1)S(1)}, bf16[384,256]{1,0:T(8,128)(2,1)S(1)}, u32[]{:S(2)}, u32[]{:S(2)}) collective-permute-start(bf16[384,256]{1,0:T(8,128)(2,1)S(1)} %pad_maximum_fusion.refs_1_), channel_id=1, source_target_pairs={{0,12},{2,14},{4,0},{6,2},{8,4},{10,6},{12,8},{14,10},{1,13},{3,15... | collective-permute-start | bytes 589832 | tf_op jit(solution)/shard_map/ppermute | solution.py:122
  38.4 13.1 %collective-permute-start.3 = (bf16[384,256]{1,0:T(8,128)(2,1)S(1)}, bf16[384,256]{1,0:T(8,128)(2,1)S(1)}, u32[]{:S(2)}, u32[]{:S(2)}) collective-permute-start(bf16[384,256]{1,0:T(8,128)(2,1)S(1)} %pad_maximum_fusion.refs_1_), channel_id=1, source_target_pairs={{0,4},{2,6},{4,8},{6,10},{8,12},{10,14},{12,0},{14,2},{1,5},{3,7},... | collective-permute-start | bytes 589832 | tf_op jit(solution)/shard_map/ppermute | solution.py:122
  40.4 15.6 %collective-permute-start.2 = (bf16[384,256]{1,0:T(8,128)(2,1)S(1)}, bf16[384,256]{1,0:T(8,128)(2,1)S(1)}, u32[]{:S(2)}, u32[]{:S(2)}) collective-permute-start(bf16[384,256]{1,0:T(8,128)(2,1)S(1)} %pad_maximum_fusion.refs_1_), channel_id=1, source_target_pairs={{0,14},{2,0},{4,2},{6,4},{8,6},{10,8},{12,10},{14,12},{1,15},{3,1}... | collective-permute-start | bytes 589832 | tf_op jit(solution)/shard_map/ppermute | solution.py:122
  45.1 10.9 %collective-permute-start.1 = (bf16[384,256]{1,0:T(8,128)(2,1)S(1)}, bf16[384,256]{1,0:T(8,128)(2,1)S(1)}, u32[]{:S(2)}, u32[]{:S(2)}) collective-permute-start(bf16[384,256]{1,0:T(8,128)(2,1)S(1)} %pad_maximum_fusion.refs_1_), channel_id=1, source_target_pairs={{0,2},{2,4},{4,6},{6,8},{8,10},{10,12},{12,14},{14,0},{1,3},{3,5},... | collective-permute-start | bytes 589832 | tf_op jit(solution)/shard_map/ppermute | solution.py:122
  47.0 8.9 %collective-permute-start.6 = (bf16[384,256]{1,0:T(8,128)(2,1)S(1)}, bf16[384,256]{1,0:T(8,128)(2,1)S(1)}, u32[]{:S(2)}, u32[]{:S(2)}) collective-permute-start(bf16[384,256]{1,0:T(8,128)(2,1)S(1)} %collective-permute-done.4.refs_5_), channel_id=1, source_target_pairs={{0,14},{2,0},{4,2},{6,4},{8,6},{10,8},{12,10},{14,12},{1,15},{3,1}... | collective-permute-start | bytes 589832 | tf_op jit(solution)/shard_map/ppermute | solution.py:122
  51.6 10.7 %collective-permute-start.7 = (bf16[384,256]{1,0:T(8,128)(2,1)S(1)}, bf16[384,256]{1,0:T(8,128)(2,1)S(1)}, u32[]{:S(2)}, u32[]{:S(2)}) collective-permute-start(bf16[384,256]{1,0:T(8,128)(2,1)S(1)} %collective-permute-done.3.refs_4_), channel_id=1, source_target_pairs={{0,4},{2,6},{4,8},{6,10},{8,12},{10,14},{12,0},{14,2},{1,5},{3,7},... | collective-permute-start | bytes 589832 | tf_op jit(solution)/shard_map/ppermute | solution.py:122
  53.5 12.9 %collective-permute-start.5 = (bf16[384,256]{1,0:T(8,128)(2,1)S(1)}, bf16[384,256]{1,0:T(8,128)(2,1)S(1)}, u32[]{:S(2)}, u32[]{:S(2)}) collective-permute-start(bf16[384,256]{1,0:T(8,128)(2,1)S(1)} %collective-permute-done.3.refs_4_), channel_id=1, source_target_pairs={{0,2},{2,4},{4,6},{6,8},{8,10},{10,12},{12,14},{14,0},{1,3},{3,5},... | collective-permute-start | bytes 589832 | tf_op jit(solution)/shard_map/ppermute | solution.py:122
  66.5 0.9 copy-start.3
  67.4 0.9 copy-start.5
  68.3 0.9 copy-start.7
  74.8 35.4 %copy-start = (bf16[2,4,4,96,256]{4,3,2,1,0:T(8,128)(2,1)}, bf16[2,4,4,96,256]{4,3,2,1,0:T(8,128)(2,1)S(1)}, u32[]{:S(2)}) copy-start(bf16[2,4,4,96,256]{4,3,2,1,0:T(8,128)(2,1)S(1)} %get-tuple-element.26.refs_5_) | copy-start | bytes 4718596
  74.8 7.6 %collective-permute-start.8 = (bf16[16,96,256]{2,1,0:T(8,128)(2,1)S(1)}, bf16[16,96,256]{2,1,0:T(8,128)(2,1)S(1)}, u32[]{:S(2)}, u32[]{:S(2)}) collective-permute-start(bf16[16,96,256]{2,1,0:T(8,128)(2,1)S(1)} %get-tuple-element.20), channel_id=1, source_target_pairs={{0,16},{16,0},{1,17},{17,1},{2,18},{18,2},{3,19},{19,3},{4,20},{20... | collective-permute-start | bytes 2359304 | tf_op jit(solution)/shard_map/ppermute | solution.py:136
  82.6 73.5 %copy-start.1 = (bf16[256,3072]{1,0:T(8,128)(2,1)S(1)}, bf16[256,3072]{1,0:T(8,128)(2,1)}, u32[]{:S(2)}) copy-start(bf16[256,3072]{1,0:T(8,128)(2,1)} %get-tuple-element.25.refs_4_) | copy-start | bytes 4718596
  82.6 73.5 %copy-start.4 = (bf16[256,256]{1,0:T(8,128)(2,1)S(1)}, bf16[256,256]{1,0:T(8,128)(2,1)}, u32[]{:S(2)}) copy-start(bf16[256,256]{1,0:T(8,128)(2,1)} %refs_6_.1) | copy-start | bytes 393220
  82.7 73.5 %copy-start.6 = (bf16[256,256]{1,0:T(8,128)(2,1)S(1)}, bf16[256,256]{1,0:T(8,128)(2,1)}, u32[]{:S(2)}) copy-start(bf16[256,256]{1,0:T(8,128)(2,1)} %refs_7_.1) | copy-start | bytes 393220
  82.7 73.5 %copy-start.8 = (bf16[256,256]{1,0:T(8,128)(2,1)S(1)}, bf16[256,256]{1,0:T(8,128)(2,1)}, u32[]{:S(2)}) copy-start(bf16[256,256]{1,0:T(8,128)(2,1)} %refs_8_.1) | copy-start | bytes 393220
  156.2 1.4 copy-start.2
  161.8 4.2 %collective-permute-start.9 = (bf16[16,96,256]{2,1,0:T(8,128)(2,1)S(1)}, bf16[16,96,256]{2,1,0:T(8,128)(2,1)S(1)}, u32[]{:S(2)}, u32[]{:S(2)}) collective-permute-start(bf16[16,96,256]{2,1,0:T(8,128)(2,1)S(1)} %get-tuple-element.28), channel_id=1, source_target_pairs={{0,16},{16,0},{1,17},{17,1},{2,18},{18,2},{3,19},{19,3},{4,20},{20... | collective-permute-start | bytes 2359304 | tf_op jit(solution)/shard_map/ppermute | solution.py:136
Sparse Core Ops, SparseCore 0:
  31.7 30.4 all-gather.2
  122.0 26.6 all-gather.4

commit v4 on v3

--- a/solution.py
+++ b/solution.py
@@ -15,7 +15,6 @@
 AXES = ("zl", "x", "core", "y", "zh")
 SIZES = (4, 4, 2, 8, 2)
 STEPS = (0, -1, 1, -2, 2, -3, 3, -4)
-VMEM_LIMIT = 48 * 1024 * 1024
 
 
 def mm(a, b, dims=((1,), (0,))):
@@ -47,9 +46,28 @@
     return jnp.concatenate(heads, axis=1)
 
 
-def first_kernel(scale, at_ref, *refs):
-    toks, (w_ref, keys_ref, values_ref, cot_ref, normt_ref, normed_ref, query_ref, keep_ref, send_ref) = refs[:8], refs[8:]
-    core, y, zh = at_ref[0], at_ref[1], at_ref[2]
+def fetch(pairs, sems):
+    copies = [pltpu.make_async_copy(src, dst, sems.at[i]) for i, (src, dst) in enumerate(pairs)]
+    for copy in copies:
+        copy.start()
+    return copies
+
+
+def wait(copies):
+    for copy in copies:
+        copy.wait()
+
+
+def by_zl(src_ref, dst_ref):
+    zl = lax.axis_index("zl")
+    return [(src_ref.at[:, k, :ROWS], dst_ref.at[:, jnp.bitwise_xor(zl, k)]) for k in range(4)]
+
+
+def first_kernel(scale, *refs):
+    toks, refs = refs[:8], refs[8:]
+    w_any, sides_any, normt_ref, normed_ref, query_ref, keep_ref, send_ref, w_ref, sides_ref, sems = refs
+    copies = fetch(by_zl(w_any, w_ref) + [(sides_any, sides_ref)], sems)
+    y, zh = lax.axis_index("y"), lax.axis_index("zh")
     width = normed_ref.shape[1]
     total = jnp.zeros((1, normt_ref.shape[-1]), F32)
     for ref in toks:
@@ -71,44 +89,54 @@
         for c in range(2):
             at = (2 * x + c) * run
             normed_ref[:, at:at + run] = normt_ref[c, x].reshape(run, normt_ref.shape[-1]).T
-    query = mm(normed_ref[...], w_ref[...])
+    wait(copies)
+    query = mm(normed_ref[...], w_ref[...].reshape(width, w_ref.shape[-1]))
     query_ref[...] = query
-    dq = query_grad(query, keys_ref[...], values_ref[...], cot_ref[...])
-    term(scale, core, normt_ref, dq, keep_ref, send_ref)
-
-
-def term(scale, core, normt_ref, dq, keep_ref, send_ref):
+    dq = query_grad(query, sides_ref[0], sides_ref[1], sides_ref[2])
+    term(scale, normt_ref, dq, keep_ref, send_ref)
+
+
+def term(scale, normt_ref, dq, keep_ref, send_ref):
+    core = lax.axis_index("core")
     for c, ref in ((core, keep_ref), (1 - core, send_ref)):
         rows = normt_ref[c].reshape(16 * ROWS, normt_ref.shape[-1])
         ref[...] = (mm(rows, dq) * scale).astype(BF16).reshape(ref.shape)
 
 
-def sum_kernel(parts_ref, first_ref, square_ref):
+def sum_kernel(parts_ref, out_ref):
     total = jnp.sum(parts_ref[...].astype(F32), 0)
-    first_ref[...] = total.astype(BF16)
     square = jnp.sum((total * total).reshape(-1, 8, total.shape[1]), 0)
-    square_ref[...] = square[:, :HEAD] + square[:, HEAD:]
-
-
-def second_kernel(scale, radius, at_ref, square_ref, query_ref, first_ref, normed_ref, normt_ref, keys_ref, values_ref,
-                  cot_ref, keep_ref, send_ref):
+    high = square.astype(BF16)
+    out_ref[:ROWS] = total.astype(BF16)
+    out_ref[ROWS:] = jnp.concatenate([high.astype(F32), square - high.astype(F32)], 0).astype(BF16)
+
+
+def second_kernel(scale, radius, square_any, query_any, first_any, normed_any, normt_any, sides_any,
+                  keep_ref, send_ref, square_ref, query_ref, first_ref, normed_ref, normt_ref, sides_ref, sems):
+    pairs = by_zl(first_any, first_ref) + [(normed_any, normed_ref), (square_any, square_ref)]
+    pairs += [(query_any, query_ref), (sides_any, sides_ref), (normt_any, normt_ref)]
+    copies = fetch(pairs, sems)
+    wait(copies[:5])
+    move = mm(normed_ref[...], first_ref[...].reshape(normed_ref.shape[1], first_ref.shape[-1]))
+    wait(copies[5:8])
     norm = jnp.sqrt(jnp.sum(jnp.sum(square_ref[...], 0), keepdims=True))
-    query = query_ref[...] + (radius / norm) * mm(normed_ref[...], first_ref[...])
-    dq = query_grad(query, keys_ref[...], values_ref[...], cot_ref[...])
-    term(scale, at_ref[0], normt_ref, dq, keep_ref, send_ref)
-
-
-def call(kernel, outs, smem=0):
+    query = query_ref[...] + (radius / norm) * move
+    dq = query_grad(query, sides_ref[0], sides_ref[1], sides_ref[2])
+    wait(copies[8:])
+    term(scale, normt_ref, dq, keep_ref, send_ref)
+
+
+def call(kernel, outs, limit, anywhere=(), scratch=()):
     spec = pl.BlockSpec(memory_space=pltpu.VMEM)
 
     def run(*args):
-        specs = [pl.BlockSpec(memory_space=pltpu.SMEM)] * smem + [spec] * (len(args) - smem)
         return pl.pallas_call(
             kernel,
             out_shape=[jax.ShapeDtypeStruct(s, d) for s, d in outs],
-            in_specs=specs,
+            in_specs=[pl.BlockSpec(memory_space=pl.ANY) if i in anywhere else spec for i in range(len(args))],
             out_specs=[spec] * len(outs),
-            compiler_params=pltpu.CompilerParams(vmem_limit_bytes=VMEM_LIMIT),
+            scratch_shapes=list(scratch),
+            compiler_params=pltpu.CompilerParams(vmem_limit_bytes=limit * 1024 * 1024),
         )(*args)
 
     return run
@@ -140,6 +168,14 @@
 
 def everywhere(value, axes, size):
     return lax.all_to_all(jnp.broadcast_to(value, (size, *value.shape)), axes, 0, 0, tiled=True)
+
+
+def gather_z(block):
+    return jnp.stack([block] + [lax.ppermute(block, "zl", swap(4, k)) for k in (1, 2, 3)])
+
+
+def gather_chips(blocks):
+    return lax.all_gather(blocks, ("x", "core"), axis=0)
 
 
 def shards(tokens, keys, values, cotangent, query_weight):
@@ -149,29 +185,38 @@
     model_width = feats * 16
     scale = 1.0 / math.sqrt(count * 32)
     radius = 0.3 * math.sqrt(model_width + cols * 16)
-    at = jnp.stack([lax.axis_index(name) for name in ("core", "y", "zh")]).astype(jnp.int32)
+    whole, half = (8, 4, ROWS, cols), (16, ROWS, cols)
+    normt_like = (2, 4, 4, ROWS, count)
+    sides = jnp.stack([keys, values, cotangent])
 
     other = lax.ppermute(tok, "zh", swap(2, 1))
-    weight_z = lax.all_gather(query_weight, "zl", axis=0, tiled=True)
-    weight_z, other = lax.optimization_barrier((weight_z, other))
-    weight = lax.all_gather(weight_z, ("x", "core"), axis=0, tiled=True)
+    weight_z, other = lax.optimization_barrier((gather_z(query_weight), other))
+    weight = gather_chips(weight_z)
     blocks = gather_tokens(jnp.concatenate([tok, other], 0))
 
-    half = (16, ROWS, cols)
     normt, normed, query, keep, send = call(
         lambda *refs: first_kernel(scale, *refs),
-        [((2, 4, 4, ROWS, count), BF16), ((count, model_width), BF16), ((count, cols), F32), (half, BF16), (half, BF16)],
-        smem=1,
-    )(at, *blocks, weight, keys, values, cotangent)
-
-    first, square = call(sum_kernel, [((ROWS, cols), BF16), ((8, HEAD), F32)])(scatter_parts(keep, send))
-    first_z = lax.all_gather(first, "zl", axis=0, tiled=True)
-    first_all = lax.all_gather(first_z, ("x", "core"), axis=0, tiled=True)
-    square = jnp.sum(everywhere(after(square, first_z), ("zh", "y"), 16), 0)
-    square = everywhere(square, ("zl", "x", "core"), 32)
+        [(normt_like, BF16), ((count, model_width), BF16), ((count, cols), F32), (half, BF16), (half, BF16)],
+        48,
+        anywhere=(8, 9),
+        scratch=(pltpu.VMEM(whole, BF16), pltpu.VMEM(sides.shape, BF16), pltpu.SemaphoreType.DMA((5,))),
+    )(*blocks, weight, sides)
+
+    first = call(sum_kernel, [((ROWS + 16, cols), BF16)], 48)(scatter_parts(keep, send))[0]
+    first_z = gather_z(first)
+    first_all = gather_chips(first_z)
+    square = jnp.sum(first_z[:, ROWS:].astype(F32).reshape(8, 8, 2, HEAD), (0, 2))
+    square = jnp.sum(everywhere(square, ("zh", "y"), 16), 0)
+    square = everywhere(square, ("x", "core"), 8)
+    args = (square, query, first_all, normed, normt, sides)
     keep, send = call(
-        lambda *refs: second_kernel(scale, radius, *refs), [(half, BF16), (half, BF16)], smem=1
-    )(at, square, query, first_all, normed, normt, keys, values, cotangent)
+        lambda *refs: second_kernel(scale, radius, *refs),
+        [(half, BF16), (half, BF16)],
+        58,
+        anywhere=range(len(args)),
+        scratch=[pltpu.VMEM(whole if arg is first_all else arg.shape, arg.dtype) for arg in args]
+        + [pltpu.SemaphoreType.DMA((9,))],
+    )(*args)
     return jnp.sum(scatter_parts(keep, send).astype(F32), 0)
 
 

time: 199 us -> 198 us (level)
  blocking collectives: 111 us -> 88.2 us
  starting transfers between devices: 42.7 us -> 60.9 us
  other arithmetic: 2.23 us -> 6.64 us
  local copies, waits for them, and re-layouts: 4.16 us -> 0.79 us
    all_gather x2 -> x0, blocking collectives: 25.1 us -> none  [the longest x1 13.5 us: shards(): weight_z = lax.all_gather(query_weight, 'zl', axis=0, tiled=True)]
    ppermute x0 -> x6, starting transfers between devices: none -> 21.8 us  [gather_z(): lax.ppermute(block, 'zl', swap(4, k))]
    all_to_all x2, blocking collectives: 51.9 us -> 56.6 us  [scatter_parts(): return lax.all_to_all(both, ('x', 'zl'), 0, 0, tiled=True)]
    unnamed x18 -> x6, local copies, waits for them, and re-layouts: 4.14 us -> 0.01 us
    ppermute x1, starting transfers between devices: 11.5 us -> 7.94 us  [shards(): other = lax.ppermute(tok, 'zh', swap(2, 1))]
    another operation x1 -> x3, other arithmetic: 0.08 us -> 3.35 us  [the longest x2 2.25 us: gather_z(): jnp.stack([block] + [lax.ppermute(block, 'zl', swap(4, k)) for k in (1, 2...]
    all_to_all x2, blocking collectives: 34.2 us -> 31.6 us  [everywhere(): lax.all_to_all(jnp.broadcast_to(value, (size, *value.shape)), axes, 0, 0,...]
  transfers between devices with their start and end apart: 12 -> 18, of which waited for: 4 -> 7; matrix products, arithmetic and copies ran while one was open for 1% -> 2% of each run, Pallas kernels for 0% -> 0%
where the time goes in v4:
time: 198 us; the launch traced here: 197 us
  blocking collectives  88.2 us (45%)
  starting transfers between devices  60.9 us (31%)
  waiting for transfers between devices  16.2 us (8%)
  between operations  13.7 us (7%)
  Pallas kernels  11.1 us (6%)
  other arithmetic  6.64 us (3%)
    all_to_all x2, blocking collectives, scatter_parts(): return lax.all_to_all(both, ('x', 'zl'), 0, 0, tiled=True)  56.6 us
    all_to_all x2, blocking collectives, everywhere(): lax.all_to_all(jnp.broadcast_to(value, (size, *value.shape)), axes, 0, 0,...  31.6 us
    ppermute x7, starting transfers between devices, turn(): return lax.ppermute(value, 'y', [(i, (i + step) % 8) for i in range(8)])  23.2 us
    ppermute x6, starting transfers between devices, gather_z(): lax.ppermute(block, 'zl', swap(4, k))  21.8 us
    pallas_call x3, Pallas kernels, run(): pl.pallas_call(kernel, out_shape=[jax.ShapeDtypeStruct(s, d) for s, d in...  11.1 us
    ppermute x7, waiting for transfers between devices, turn(): return lax.ppermute(value, 'y', [(i, (i + step) % 8) for i in range(8)])  9.72 us
    ppermute x1, starting transfers between devices, shards(): other = lax.ppermute(tok, 'zh', swap(2, 1))  7.94 us
    ppermute x2, starting transfers between devices, scatter_parts(): got = lax.ppermute(send, 'core', swap(2, 1))  7.86 us
  transfers between devices with their start and end apart: 18, of which 7 were waited for; matrix products, arithmetic and copies ran while one was open for 2% of the time, Pallas kernels for 0%

profile of v4, /device:TPU:1, one launch (start us, length us, event | category | flops | bytes accessed | tf_op | source)
XLA Modules:
  0.0 197.4 jit_solution(447754051184515453)
XLA Ops:
  6.5 4.8 %collective-permute-start = (bf16[96,256]{1,0:T(8,128)(2,1)}, bf16[96,256]{1,0:T(8,128)(2,1)S(1)}, u32[]{:S(2)}, u32[]{:S(2)}) collective-permute-start(bf16[96,256]{1,0:T(8,128)(2,1)} %param.9), channel_id=1, source_target_pairs={{0,128},{128,0},{256,384},{384,256},{1,129},{129,1},{257,385},{385... | collective-permute-start | bytes 147464 | tf_op jit(solution)/shard_map/ppermute | solution.py:174
  11.4 5.5 %collective-permute-start.2 = (bf16[96,256]{1,0:T(8,128)(2,1)}, bf16[96,256]{1,0:T(8,128)(2,1)S(1)}, u32[]{:S(2)}, u32[]{:S(2)}) collective-permute-start(bf16[96,256]{1,0:T(8,128)(2,1)} %param.9), channel_id=1, source_target_pairs={{0,384},{128,256},{256,128},{384,0},{1,385},{129,257},{257,129},{3... | collective-permute-start | bytes 147464 | tf_op jit(solution)/shard_map/ppermute | solution.py:174
  16.9 2.2 %collective-permute-start.1 = (bf16[96,256]{1,0:T(8,128)(2,1)}, bf16[96,256]{1,0:T(8,128)(2,1)S(1)}, u32[]{:S(2)}, u32[]{:S(2)}) collective-permute-start(bf16[96,256]{1,0:T(8,128)(2,1)} %param.9), channel_id=1, source_target_pairs={{0,256},{128,384},{256,0},{384,128},{1,257},{129,385},{257,1},{385... | collective-permute-start | bytes 147464 | tf_op jit(solution)/shard_map/ppermute | solution.py:174
  19.1 7.9 %collective-permute-start.3 = (bf16[192,256]{1,0:T(8,128)(2,1)}, bf16[192,256]{1,0:T(8,128)(2,1)S(1)}, u32[]{:S(2)}, u32[]{:S(2)}) collective-permute-start(bf16[192,256]{1,0:T(8,128)(2,1)} %bitcast.23), channel_id=1, source_target_pairs={{0,1},{1,0},{2,3},{3,2},{4,5},{5,4},{6,7},{7,6},{8,9},{9,8},{10,11... | collective-permute-start | bytes 294920 | tf_op jit(solution)/shard_map/ppermute | solution.py:192
  27.1 1.5 pad_maximum_fusion.2
  28.6 0.9 collective-permute-done.3
  29.5 0.9 pad_maximum_fusion.3.refs_0_
  30.5 5.9 %collective-permute-start.7 = (bf16[384,256]{1,0:T(8,128)(2,1)S(1)}, bf16[384,256]{1,0:T(8,128)(2,1)S(1)}, u32[]{:S(2)}, u32[]{:S(2)}) collective-permute-start(bf16[384,256]{1,0:T(8,128)(2,1)S(1)} %pad_maximum_fusion.3.refs_0_), channel_id=1, source_target_pairs={{0,12},{2,14},{4,0},{6,2},{8,4},{10,6},{12,8},{14,10},{1,13},{3,15... | collective-permute-start | bytes 589832 | tf_op jit(solution)/shard_map/ppermute | solution.py:150
  36.3 1.9 collective-permute-start.6
  38.3 4.7 %collective-permute-start.5 = (bf16[384,256]{1,0:T(8,128)(2,1)S(1)}, bf16[384,256]{1,0:T(8,128)(2,1)S(1)}, u32[]{:S(2)}, u32[]{:S(2)}) collective-permute-start(bf16[384,256]{1,0:T(8,128)(2,1)S(1)} %pad_maximum_fusion.3.refs_0_), channel_id=1, source_target_pairs={{0,14},{2,0},{4,2},{6,4},{8,6},{10,8},{12,10},{14,12},{1,15},{3,1}... | collective-permute-start | bytes 589832 | tf_op jit(solution)/shard_map/ppermute | solution.py:150
  43.0 1.9 collective-permute-start.4
  44.9 4.6 %collective-permute-start.9 = (bf16[384,256]{1,0:T(8,128)(2,1)S(1)}, bf16[384,256]{1,0:T(8,128)(2,1)S(1)}, u32[]{:S(2)}, u32[]{:S(2)}) collective-permute-start(bf16[384,256]{1,0:T(8,128)(2,1)S(1)} %collective-permute-done.7.refs_4_), channel_id=1, source_target_pairs={{0,14},{2,0},{4,2},{6,4},{8,6},{10,8},{12,10},{14,12},{1,15},{3,1}... | collective-permute-start | bytes 589832 | tf_op jit(solution)/shard_map/ppermute | solution.py:150
  49.5 1.9 collective-permute-start.10
  51.4 2.3 %collective-permute-start.8 = (bf16[384,256]{1,0:T(8,128)(2,1)S(1)}, bf16[384,256]{1,0:T(8,128)(2,1)S(1)}, u32[]{:S(2)}, u32[]{:S(2)}) collective-permute-start(bf16[384,256]{1,0:T(8,128)(2,1)S(1)} %collective-permute-done.6.refs_3_), channel_id=1, source_target_pairs={{0,2},{2,4},{4,6},{6,8},{8,10},{10,12},{12,14},{14,0},{1,3},{3,5},... | collective-permute-start | bytes 589832 | tf_op jit(solution)/shard_map/ppermute | solution.py:150
  53.8 1.1 pad_maximum_fusion.refs_9_.refs_5_
  54.9 5.6 %collective-permute-done.10.refs_7_ = bf16[384,256]{1,0:T(8,128)(2,1)S(1)} collective-permute-done((bf16[384,256]{1,0:T(8,128)(2,1)S(1)}, bf16[384,256]{1,0:T(8,128)(2,1)S(1)}, u32[]{:S(2)}, u32[]{:S(2)}) %collective-permute-start.10) | collective-permute-done | bytes 196640 | tf_op jit(solution)/shard_map/ppermute | solution.py:150
  60.6 4.1 %collective-permute-done.8.refs_5_ = bf16[384,256]{1,0:T(8,128)(2,1)S(1)} collective-permute-done((bf16[384,256]{1,0:T(8,128)(2,1)S(1)}, bf16[384,256]{1,0:T(8,128)(2,1)S(1)}, u32[]{:S(2)}, u32[]{:S(2)}) %collective-permute-start.8) | collective-permute-done | bytes 196640 | tf_op jit(solution)/shard_map/ppermute | solution.py:150
  64.6 4.9 %shard_map.55 = (bf16[2,4,4,96,256]{4,3,2,1,0:T(8,128)(2,1)S(1)}, bf16[256,3072]{1,0:T(8,128)(2,1)}, f32[256,256]{1,0:T(8,128)S(1)}, bf16[16,96,256]{2,1,0:T(8,128)(2,1)S(1)}, bf16[16,96,256]{2,1,0:T(8,128)(2,1)S(1)}) custom-call(bf16[384,256]{1,0:T(8,128)(2,1)S(1)} %pad_maximum_fusion.3.refs_0_, bf16[384,256]{1,0:T(8,128)(2,1)S(1)} %collective-permute-done.4.refs_1_, ...), custom_call_target="tpu_custom_call" | custom-call | tf_op jit(solution)/shard_map/pallas_call | solution.py:133
  69.6 5.2 %collective-permute-start.11 = (bf16[16,96,256]{2,1,0:T(8,128)(2,1)S(1)}, bf16[16,96,256]{2,1,0:T(8,128)(2,1)S(1)}, u32[]{:S(2)}, u32[]{:S(2)}) collective-permute-start(bf16[16,96,256]{2,1,0:T(8,128)(2,1)S(1)} %get-tuple-element.17), channel_id=1, source_target_pairs={{0,16},{16,0},{1,17},{17,1},{2,18},{18,2},{3,19},{19,3},{4,20},{20... | collective-permute-start | bytes 2359304 | tf_op jit(solution)/shard_map/ppermute | solution.py:164
  74.8 1.9 collective-permute-done.11
  76.9 31.6 %all_to_all.20.parts_ref = bf16[16,96,256]{2,1,0:T(8,128)(2,1)S(1)} all-to-all(bf16[16,96,256]{2,1,0:T(8,128)(2,1)S(1)} %add_convert_fusion.1), channel_id=1, replica_groups=mesh['zl'=4,'x'=4,'core'=2,'y'=8,'zh'=2] {'x','zl'}, dimensions={0} | all-to-all | bytes 1572864 | tf_op jit(solution)/shard_map/all_to_all | solution.py:166
  108.6 2.4 %collective-permute-start.14 = (bf16[112,256]{1,0:T(8,128)(2,1)S(1)}, bf16[112,256]{1,0:T(8,128)(2,1)S(1)}, u32[]{:S(2)}, u32[]{:S(2)}) collective-permute-start(bf16[112,256]{1,0:T(8,128)(2,1)S(1)} %shard_map.56), channel_id=1, source_target_pairs={{0,384},{128,256},{256,128},{384,0},{1,385},{129,257},{257,129},{3... | collective-permute-start | bytes 172040 | tf_op jit(solution)/shard_map/ppermute | solution.py:174
  111.0 2.4 %collective-permute-start.13 = (bf16[112,256]{1,0:T(8,128)(2,1)S(1)}, bf16[112,256]{1,0:T(8,128)(2,1)S(1)}, u32[]{:S(2)}, u32[]{:S(2)}) collective-permute-start(bf16[112,256]{1,0:T(8,128)(2,1)S(1)} %shard_map.56), channel_id=1, source_target_pairs={{0,256},{128,384},{256,0},{384,128},{1,257},{129,385},{257,1},{385... | collective-permute-start | bytes 172040 | tf_op jit(solution)/shard_map/ppermute | solution.py:174
  113.5 4.5 %collective-permute-start.12 = (bf16[112,256]{1,0:T(8,128)(2,1)S(1)}, bf16[112,256]{1,0:T(8,128)(2,1)S(1)}, u32[]{:S(2)}, u32[]{:S(2)}) collective-permute-start(bf16[112,256]{1,0:T(8,128)(2,1)S(1)} %shard_map.56), channel_id=1, source_target_pairs={{0,128},{128,0},{256,384},{384,256},{1,129},{129,1},{257,385},{385... | collective-permute-start | bytes 172040 | tf_op jit(solution)/shard_map/ppermute | solution.py:174
  118.3 1.2 collective-permute-done.12
  121.0 19.4 %all_to_all.21 = f32[16,8,128]{2,1,0:T(8,128)S(1)} all-to-all(f32[16,8,128]{2,1,0:T(8,128)S(1)} %broadcast_in_dim.6), channel_id=1, replica_groups=mesh['zl'=4,'x'=4,'core'=2,'y'=8,'zh'=2] {'zh','y'}, dimensions={0} | all-to-all | bytes 131072 | tf_op jit(solution)/shard_map/all_to_all | solution.py:170
  140.5 12.1 %all_to_all.22.refs_0_ = f32[8,8,128]{2,1,0:T(8,128)} all-to-all(f32[8,8,128]{2,1,0:T(8,128)S(1)} %broadcast_in_dim.7), channel_id=1, replica_groups=mesh['zl'=4,'x'=4,'core'=2,'y'=8,'zh'=2] {'x','core'}, dimensions={0} | all-to-all | bytes 65536 | tf_op jit(solution)/shard_map/all_to_all | solution.py:170
  152.7 6.0 %shard_map.57 = (bf16[16,96,256]{2,1,0:T(8,128)(2,1)}, bf16[16,96,256]{2,1,0:T(8,128)(2,1)}) custom-call(f32[8,8,128]{2,1,0:T(8,128)} %all_to_all.22.refs_0_, f32[256,256]{1,0:T(8,128)} %copy-done.2, bf16[8,4,112,256]{3,2,1,0:T(8,128)(2,1)} %bitcast.17, bf16[256,3072]{1,0:T(8,128)(2,1)} %get-tuple-element.19.refs_3_, bf16[2,4,4,96,256]{4,3,2,1,0:T(8,128)(2,1)} %copy-done.1, ...), custom_call_target="tpu_custom_call" | custom-call | tf_op jit(solution)/shard_map/pallas_call | solution.py:133
  158.7 2.6 %collective-permute-start.15 = (bf16[16,96,256]{2,1,0:T(8,128)(2,1)}, bf16[16,96,256]{2,1,0:T(8,128)(2,1)S(1)}, u32[]{:S(2)}, u32[]{:S(2)}) collective-permute-start(bf16[16,96,256]{2,1,0:T(8,128)(2,1)} %get-tuple-element.22), channel_id=1, source_target_pairs={{0,16},{16,0},{1,17},{17,1},{2,18},{18,2},{3,19},{19,3},{4,20},{20... | collective-permute-start | bytes 2359304 | tf_op jit(solution)/shard_map/ppermute | solution.py:164
  161.3 2.1 %collective-permute-done.15 = bf16[16,96,256]{2,1,0:T(8,128)(2,1)S(1)} collective-permute-done((bf16[16,96,256]{2,1,0:T(8,128)(2,1)}, bf16[16,96,256]{2,1,0:T(8,128)(2,1)S(1)}, u32[]{:S(2)}, u32[]{:S(2)}) %collective-permute-start.15) | collective-permute-done | bytes 786464 | tf_op jit(solution)/shard_map/ppermute | solution.py:164
  163.4 1.4 add_convert_fusion
  164.8 25.0 %all_to_all.23 = bf16[16,96,256]{2,1,0:T(8,128)(2,1)S(1)} all-to-all(bf16[16,96,256]{2,1,0:T(8,128)(2,1)S(1)} %add_convert_fusion), channel_id=1, replica_groups=mesh['zl'=4,'x'=4,'core'=2,'y'=8,'zh'=2] {'x','zl'}, dimensions={0} | all-to-all | bytes 1572864 | tf_op jit(solution)/shard_map/all_to_all | solution.py:166
  (31 shorter events, 3.1 us)
Async XLA Ops:
  6.5 58.1 %all-gather.5.cloned.1.call-start = ((), (), s32[]{:S(2)}) async-start(), calls=%async_computation.4 | async-start | bytes 1769472 | tf_op jit(solution)/shard_map/all_gather | solution.py:178
  6.5 20.5 %collective-permute-start = (bf16[96,256]{1,0:T(8,128)(2,1)}, bf16[96,256]{1,0:T(8,128)(2,1)S(1)}, u32[]{:S(2)}, u32[]{:S(2)}) collective-permute-start(bf16[96,256]{1,0:T(8,128)(2,1)} %param.9), channel_id=1, source_target_pairs={{0,128},{128,0},{256,384},{384,256},{1,129},{129,1},{257,385},{385... | collective-permute-start | bytes 147464 | tf_op jit(solution)/shard_map/ppermute | solution.py:174
  11.4 15.7 %collective-permute-start.2 = (bf16[96,256]{1,0:T(8,128)(2,1)}, bf16[96,256]{1,0:T(8,128)(2,1)S(1)}, u32[]{:S(2)}, u32[]{:S(2)}) collective-permute-start(bf16[96,256]{1,0:T(8,128)(2,1)} %param.9), channel_id=1, source_target_pairs={{0,384},{128,256},{256,128},{384,0},{1,385},{129,257},{257,129},{3... | collective-permute-start | bytes 147464 | tf_op jit(solution)/shard_map/ppermute | solution.py:174
  16.9 10.2 %collective-permute-start.1 = (bf16[96,256]{1,0:T(8,128)(2,1)}, bf16[96,256]{1,0:T(8,128)(2,1)S(1)}, u32[]{:S(2)}, u32[]{:S(2)}) collective-permute-start(bf16[96,256]{1,0:T(8,128)(2,1)} %param.9), channel_id=1, source_target_pairs={{0,256},{128,384},{256,0},{384,128},{1,257},{129,385},{257,1},{385... | collective-permute-start | bytes 147464 | tf_op jit(solution)/shard_map/ppermute | solution.py:174
  19.1 10.4 %collective-permute-start.3 = (bf16[192,256]{1,0:T(8,128)(2,1)}, bf16[192,256]{1,0:T(8,128)(2,1)S(1)}, u32[]{:S(2)}, u32[]{:S(2)}) collective-permute-start(bf16[192,256]{1,0:T(8,128)(2,1)} %bitcast.23), channel_id=1, source_target_pairs={{0,1},{1,0},{2,3},{3,2},{4,5},{5,4},{6,7},{7,6},{8,9},{9,8},{10,11... | collective-permute-start | bytes 294920 | tf_op jit(solution)/shard_map/ppermute | solution.py:192
  29.5 123.2 %all-gather.7.cloned.1.call-start = ((), (), s32[]{:S(2)}) async-start(), calls=%async_computation.5 | async-start | bytes 2064384 | tf_op jit(solution)/shard_map/all_gather | solution.py:178
  30.5 14.4 %collective-permute-start.7 = (bf16[384,256]{1,0:T(8,128)(2,1)S(1)}, bf16[384,256]{1,0:T(8,128)(2,1)S(1)}, u32[]{:S(2)}, u32[]{:S(2)}) collective-permute-start(bf16[384,256]{1,0:T(8,128)(2,1)S(1)} %pad_maximum_fusion.3.refs_0_), channel_id=1, source_target_pairs={{0,12},{2,14},{4,0},{6,2},{8,4},{10,6},{12,8},{14,10},{1,13},{3,15... | collective-permute-start | bytes 589832 | tf_op jit(solution)/shard_map/ppermute | solution.py:150
  36.3 13.1 %collective-permute-start.6 = (bf16[384,256]{1,0:T(8,128)(2,1)S(1)}, bf16[384,256]{1,0:T(8,128)(2,1)S(1)}, u32[]{:S(2)}, u32[]{:S(2)}) collective-permute-start(bf16[384,256]{1,0:T(8,128)(2,1)S(1)} %pad_maximum_fusion.3.refs_0_), channel_id=1, source_target_pairs={{0,4},{2,6},{4,8},{6,10},{8,12},{10,14},{12,0},{14,2},{1,5},{3,7},... | collective-permute-start | bytes 589832 | tf_op jit(solution)/shard_map/ppermute | solution.py:150
  38.3 16.6 %collective-permute-start.5 = (bf16[384,256]{1,0:T(8,128)(2,1)S(1)}, bf16[384,256]{1,0:T(8,128)(2,1)S(1)}, u32[]{:S(2)}, u32[]{:S(2)}) collective-permute-start(bf16[384,256]{1,0:T(8,128)(2,1)S(1)} %pad_maximum_fusion.3.refs_0_), channel_id=1, source_target_pairs={{0,14},{2,0},{4,2},{6,4},{8,6},{10,8},{12,10},{14,12},{1,15},{3,1}... | collective-permute-start | bytes 589832 | tf_op jit(solution)/shard_map/ppermute | solution.py:150
  43.0 11.9 %collective-permute-start.4 = (bf16[384,256]{1,0:T(8,128)(2,1)S(1)}, bf16[384,256]{1,0:T(8,128)(2,1)S(1)}, u32[]{:S(2)}, u32[]{:S(2)}) collective-permute-start(bf16[384,256]{1,0:T(8,128)(2,1)S(1)} %pad_maximum_fusion.3.refs_0_), channel_id=1, source_target_pairs={{0,2},{2,4},{4,6},{6,8},{8,10},{10,12},{12,14},{14,0},{1,3},{3,5},... | collective-permute-start | bytes 589832 | tf_op jit(solution)/shard_map/ppermute | solution.py:150
  44.9 10.0 %collective-permute-start.9 = (bf16[384,256]{1,0:T(8,128)(2,1)S(1)}, bf16[384,256]{1,0:T(8,128)(2,1)S(1)}, u32[]{:S(2)}, u32[]{:S(2)}) collective-permute-start(bf16[384,256]{1,0:T(8,128)(2,1)S(1)} %collective-permute-done.7.refs_4_), channel_id=1, source_target_pairs={{0,14},{2,0},{4,2},{6,4},{8,6},{10,8},{12,10},{14,12},{1,15},{3,1}... | collective-permute-start | bytes 589832 | tf_op jit(solution)/shard_map/ppermute | solution.py:150
  49.5 11.1 %collective-permute-start.10 = (bf16[384,256]{1,0:T(8,128)(2,1)S(1)}, bf16[384,256]{1,0:T(8,128)(2,1)S(1)}, u32[]{:S(2)}, u32[]{:S(2)}) collective-permute-start(bf16[384,256]{1,0:T(8,128)(2,1)S(1)} %collective-permute-done.6.refs_3_), channel_id=1, source_target_pairs={{0,4},{2,6},{4,8},{6,10},{8,12},{10,14},{12,0},{14,2},{1,5},{3,7},... | collective-permute-start | bytes 589832 | tf_op jit(solution)/shard_map/ppermute | solution.py:150
  51.4 13.2 %collective-permute-start.8 = (bf16[384,256]{1,0:T(8,128)(2,1)S(1)}, bf16[384,256]{1,0:T(8,128)(2,1)S(1)}, u32[]{:S(2)}, u32[]{:S(2)}) collective-permute-start(bf16[384,256]{1,0:T(8,128)(2,1)S(1)} %collective-permute-done.6.refs_3_), channel_id=1, source_target_pairs={{0,2},{2,4},{4,6},{6,8},{8,10},{10,12},{12,14},{14,0},{1,3},{3,5},... | collective-permute-start | bytes 589832 | tf_op jit(solution)/shard_map/ppermute | solution.py:150
  54.9 14.7 %copy-start = (bf16[3,256,256]{2,1,0:T(8,128)(2,1)}, bf16[3,256,256]{2,1,0:T(8,128)(2,1)S(1)}, u32[]{:S(2)}) copy-start(bf16[3,256,256]{2,1,0:T(8,128)(2,1)S(1)} %pad_maximum_fusion.refs_9_.refs_5_) | copy-start | bytes 1179652
  69.6 39.0 %copy-start.1 = (bf16[2,4,4,96,256]{4,3,2,1,0:T(8,128)(2,1)}, bf16[2,4,4,96,256]{4,3,2,1,0:T(8,128)(2,1)S(1)}, u32[]{:S(2)}) copy-start(bf16[2,4,4,96,256]{4,3,2,1,0:T(8,128)(2,1)S(1)} %get-tuple-element.20.refs_4_) | copy-start | bytes 4718596
  69.6 38.9 %copy-start.2 = (f32[256,256]{1,0:T(8,128)}, f32[256,256]{1,0:T(8,128)S(1)}, u32[]{:S(2)}) copy-start(f32[256,256]{1,0:T(8,128)S(1)} %get-tuple-element.18.refs_1_) | copy-start | bytes 786436
  69.6 7.1 %collective-permute-start.11 = (bf16[16,96,256]{2,1,0:T(8,128)(2,1)S(1)}, bf16[16,96,256]{2,1,0:T(8,128)(2,1)S(1)}, u32[]{:S(2)}, u32[]{:S(2)}) collective-permute-start(bf16[16,96,256]{2,1,0:T(8,128)(2,1)S(1)} %get-tuple-element.17), channel_id=1, source_target_pairs={{0,16},{16,0},{1,17},{17,1},{2,18},{18,2},{3,19},{19,3},{4,20},{20... | collective-permute-start | bytes 2359304 | tf_op jit(solution)/shard_map/ppermute | solution.py:164
  108.6 9.3 %collective-permute-start.14 = (bf16[112,256]{1,0:T(8,128)(2,1)S(1)}, bf16[112,256]{1,0:T(8,128)(2,1)S(1)}, u32[]{:S(2)}, u32[]{:S(2)}) collective-permute-start(bf16[112,256]{1,0:T(8,128)(2,1)S(1)} %shard_map.56), channel_id=1, source_target_pairs={{0,384},{128,256},{256,128},{384,0},{1,385},{129,257},{257,129},{3... | collective-permute-start | bytes 172040 | tf_op jit(solution)/shard_map/ppermute | solution.py:174
  111.0 7.3 %collective-permute-start.13 = (bf16[112,256]{1,0:T(8,128)(2,1)S(1)}, bf16[112,256]{1,0:T(8,128)(2,1)S(1)}, u32[]{:S(2)}, u32[]{:S(2)}) collective-permute-start(bf16[112,256]{1,0:T(8,128)(2,1)S(1)} %shard_map.56), channel_id=1, source_target_pairs={{0,256},{128,384},{256,0},{384,128},{1,257},{129,385},{257,1},{385... | collective-permute-start | bytes 172040 | tf_op jit(solution)/shard_map/ppermute | solution.py:174
  113.5 6.0 %collective-permute-start.12 = (bf16[112,256]{1,0:T(8,128)(2,1)S(1)}, bf16[112,256]{1,0:T(8,128)(2,1)S(1)}, u32[]{:S(2)}, u32[]{:S(2)}) collective-permute-start(bf16[112,256]{1,0:T(8,128)(2,1)S(1)} %shard_map.56), channel_id=1, source_target_pairs={{0,128},{128,0},{256,384},{384,256},{1,129},{129,1},{257,385},{385... | collective-permute-start | bytes 172040 | tf_op jit(solution)/shard_map/ppermute | solution.py:174
  158.7 4.8 %collective-permute-start.15 = (bf16[16,96,256]{2,1,0:T(8,128)(2,1)}, bf16[16,96,256]{2,1,0:T(8,128)(2,1)S(1)}, u32[]{:S(2)}, u32[]{:S(2)}) collective-permute-start(bf16[16,96,256]{2,1,0:T(8,128)(2,1)} %get-tuple-element.22), channel_id=1, source_target_pairs={{0,16},{16,0},{1,17},{17,1},{2,18},{18,2},{3,19},{19,3},{4,20},{20... | collective-permute-start | bytes 2359304 | tf_op jit(solution)/shard_map/ppermute | solution.py:164
Sparse Core Ops, SparseCore 0:
  29.6 34.8 all-gather.4
  120.4 28.9 all-gather.6

commit v5 on v4

--- a/solution.py
+++ b/solution.py
@@ -104,25 +104,25 @@
 
 
 def sum_kernel(parts_ref, out_ref):
-    total = jnp.sum(parts_ref[...].astype(F32), 0)
+    out_ref[...] = jnp.sum(parts_ref[...].astype(F32), 0).astype(BF16)
+
+
+def last_sum_kernel(*refs):
+    parts, (first_ref, square_ref) = refs[:4], refs[4:]
+    total = sum(ref[...].astype(F32) for ref in parts)
+    first_ref[...] = total.astype(BF16)
     square = jnp.sum((total * total).reshape(-1, 8, total.shape[1]), 0)
-    high = square.astype(BF16)
-    out_ref[:ROWS] = total.astype(BF16)
-    out_ref[ROWS:] = jnp.concatenate([high.astype(F32), square - high.astype(F32)], 0).astype(BF16)
-
-
-def second_kernel(scale, radius, square_any, query_any, first_any, normed_any, normt_any, sides_any,
-                  keep_ref, send_ref, square_ref, query_ref, first_ref, normed_ref, normt_ref, sides_ref, sems):
-    pairs = by_zl(first_any, first_ref) + [(normed_any, normed_ref), (square_any, square_ref)]
-    pairs += [(query_any, query_ref), (sides_any, sides_ref), (normt_any, normt_ref)]
-    copies = fetch(pairs, sems)
-    wait(copies[:5])
+    square_ref[...] = square[:, :HEAD] + square[:, HEAD:]
+
+
+def second_kernel(scale, radius, square_ref, query_ref, first_ref, normed_ref, normt_any, sides_ref,
+                  keep_ref, send_ref, normt_ref, sems):
+    copies = fetch([(normt_any, normt_ref)], sems)
+    norm = jnp.sqrt(jnp.sum(jnp.sum(square_ref[...], 0), keepdims=True))
     move = mm(normed_ref[...], first_ref[...].reshape(normed_ref.shape[1], first_ref.shape[-1]))
-    wait(copies[5:8])
-    norm = jnp.sqrt(jnp.sum(jnp.sum(square_ref[...], 0), keepdims=True))
     query = query_ref[...] + (radius / norm) * move
     dq = query_grad(query, sides_ref[0], sides_ref[1], sides_ref[2])
-    wait(copies[8:])
+    wait(copies)
     term(scale, normt_ref, dq, keep_ref, send_ref)
 
 
@@ -160,18 +160,17 @@
     return block, back1, ahead1, back2, ahead2, back3, ahead3, back4
 
 
-def scatter_parts(keep, send):
+def sum_core(keep, send):
     got = lax.ppermute(send, "core", swap(2, 1))
-    both = (keep.astype(F32) + got.astype(F32)).astype(BF16)
-    return lax.all_to_all(both, ("x", "zl"), 0, 0, tiled=True)
+    return (keep.astype(F32) + got.astype(F32)).astype(BF16)
 
 
 def everywhere(value, axes, size):
     return lax.all_to_all(jnp.broadcast_to(value, (size, *value.shape)), axes, 0, 0, tiled=True)
 
 
-def gather_z(block):
-    return jnp.stack([block] + [lax.ppermute(block, "zl", swap(4, k)) for k in (1, 2, 3)])
+def along_z(block):
+    return [block] + [lax.ppermute(block, "zl", swap(4, k)) for k in (1, 2, 3)]
 
 
 def gather_chips(blocks):
@@ -190,7 +189,9 @@
     sides = jnp.stack([keys, values, cotangent])
 
     other = lax.ppermute(tok, "zh", swap(2, 1))
-    weight_z, other = lax.optimization_barrier((gather_z(query_weight), other))
+    weight_z = along_z(query_weight)
+    *weight_z, other = lax.optimization_barrier((*weight_z, other))
+    weight_z = jnp.stack(weight_z)
     weight = gather_chips(weight_z)
     blocks = gather_tokens(jnp.concatenate([tok, other], 0))
 
@@ -202,22 +203,22 @@
         scratch=(pltpu.VMEM(whole, BF16), pltpu.VMEM(sides.shape, BF16), pltpu.SemaphoreType.DMA((5,))),
     )(*blocks, weight, sides)
 
-    first = call(sum_kernel, [((ROWS + 16, cols), BF16)], 48)(scatter_parts(keep, send))[0]
-    first_z = gather_z(first)
-    first_all = gather_chips(first_z)
-    square = jnp.sum(first_z[:, ROWS:].astype(F32).reshape(8, 8, 2, HEAD), (0, 2))
+    quarter = (4 * ROWS, cols)
+    parts = lax.all_to_all(sum_core(keep, send).reshape(4, *quarter), "x", 0, 0, tiled=True)
+    partial = call(sum_kernel, [(quarter, BF16)], 48)(parts)[0]
+    first, square = call(last_sum_kernel, [(quarter, BF16), ((8, HEAD), F32)], 48)(*along_z(partial))
+    first_all = gather_chips(first)
     square = jnp.sum(everywhere(square, ("zh", "y"), 16), 0)
     square = everywhere(square, ("x", "core"), 8)
-    args = (square, query, first_all, normed, normt, sides)
     keep, send = call(
         lambda *refs: second_kernel(scale, radius, *refs),
         [(half, BF16), (half, BF16)],
-        58,
-        anywhere=range(len(args)),
-        scratch=[pltpu.VMEM(whole if arg is first_all else arg.shape, arg.dtype) for arg in args]
-        + [pltpu.SemaphoreType.DMA((9,))],
-    )(*args)
-    return jnp.sum(scatter_parts(keep, send).astype(F32), 0)
+        48,
+        anywhere=(4,),
+        scratch=(pltpu.VMEM(normt_like, BF16), pltpu.SemaphoreType.DMA((1,))),
+    )(square, query, first_all, normed, normt, sides)
+    parts = lax.all_to_all(sum_core(keep, send), ("x", "zl"), 0, 0, tiled=True)
+    return jnp.sum(parts.astype(F32), 0)
 
 
 def solution(mesh):

time: 198 us -> 186 us (0.939)
  blocking collectives: 88.2 us -> 65.9 us
  waiting for transfers between devices: 16.2 us -> 27.9 us
    all_to_all x2, blocking collectives: 56.6 us -> 40.1 us  [the longest x1 24.7 us: shards(): parts = lax.all_to_all(sum_core(keep, send), ('x', 'zl'), 0, 0, tiled=True)]
    ppermute x8, waiting for transfers between devices: 5.54 us -> 18.4 us  [the longest x6 14.6 us: along_z(): return [block] + [lax.ppermute(block, 'zl', swap(4, k)) for k in (1, 2, 3)]]
    all_to_all x2, blocking collectives: 31.6 us -> 25.8 us  [everywhere(): lax.all_to_all(jnp.broadcast_to(value, (size, *value.shape)), axes, 0, 0,...]
    ppermute x1, starting transfers between devices: 7.94 us -> 11.5 us  [shards(): other = lax.ppermute(tok, 'zh', swap(2, 1))]
    ppermute x8, starting transfers between devices: 29.7 us -> 26.7 us  [the longest x6 18.5 us: along_z(): return [block] + [lax.ppermute(block, 'zl', swap(4, k)) for k in (1, 2, 3)]]
    pallas_call x3 -> x4, Pallas kernels: 11.1 us -> 9.62 us  [run(): pl.pallas_call(kernel, out_shape=[jax.ShapeDtypeStruct(s, d) for s, d in...]
  transfers between devices with their start and end apart: 18 -> 18, of which waited for: 7 -> 6; matrix products, arithmetic and copies ran while one was open for 2% -> 1% of each run, Pallas kernels for 0% -> 0%
where the time goes in v5:
time: 186 us; the launch traced here: 185 us
  blocking collectives  65.9 us (35%)
  starting transfers between devices  61.4 us (33%)
  waiting for transfers between devices  27.9 us (15%)
  between operations  13.7 us (7%)
  Pallas kernels  9.62 us (5%)
  other arithmetic  4.72 us (3%)
    all_to_all x2, blocking collectives, everywhere(): lax.all_to_all(jnp.broadcast_to(value, (size, *value.shape)), axes, 0, 0,...  25.8 us
    all_to_all x1, blocking collectives, shards(): parts = lax.all_to_all(sum_core(keep, send), ('x', 'zl'), 0, 0, tiled=True)  24.7 us
    ppermute x7, starting transfers between devices, turn(): return lax.ppermute(value, 'y', [(i, (i + step) % 8) for i in range(8)])  23.2 us
    ppermute x6, starting transfers between devices, along_z(): return [block] + [lax.ppermute(block, 'zl', swap(4, k)) for k in (1, 2, 3)]  18.5 us
    all_to_all x1, blocking collectives, shards(): lax.all_to_all(sum_core(keep, send).reshape(4, *quarter), 'x', 0, 0, tile...  15.4 us
    ppermute x6, waiting for transfers between devices, along_z(): return [block] + [lax.ppermute(block, 'zl', swap(4, k)) for k in (1, 2, 3)]  14.6 us
    ppermute x1, starting transfers between devices, shards(): other = lax.ppermute(tok, 'zh', swap(2, 1))  11.5 us
    pallas_call x4, Pallas kernels, run(): pl.pallas_call(kernel, out_shape=[jax.ShapeDtypeStruct(s, d) for s, d in...  9.62 us
  transfers between devices with their start and end apart: 18, of which 6 were waited for; matrix products, arithmetic and copies ran while one was open for 1% of the time, Pallas kernels for 0%

profile of v5, /device:TPU:1, one launch (start us, length us, event | category | flops | bytes accessed | tf_op | source)
XLA Modules:
  0.0 184.7 jit_solution(15860319487067536402)
XLA Ops:
  6.5 11.5 %collective-permute-start.3 = (bf16[192,256]{1,0:T(8,128)(2,1)}, bf16[192,256]{1,0:T(8,128)(2,1)S(1)}, u32[]{:S(2)}, u32[]{:S(2)}) collective-permute-start(bf16[192,256]{1,0:T(8,128)(2,1)} %bitcast.17), channel_id=1, source_target_pairs={{0,1},{1,0},{2,3},{3,2},{4,5},{5,4},{6,7},{7,6},{8,9},{9,8},{10,11... | collective-permute-start | bytes 294920 | tf_op jit(solution)/shard_map/ppermute | solution.py:191
  18.0 4.0 %collective-permute-start.1 = (bf16[96,256]{1,0:T(8,128)(2,1)}, bf16[96,256]{1,0:T(8,128)(2,1)S(1)}, u32[]{:S(2)}, u32[]{:S(2)}) collective-permute-start(bf16[96,256]{1,0:T(8,128)(2,1)} %param.9), channel_id=1, source_target_pairs={{0,256},{128,384},{256,0},{384,128},{1,257},{129,385},{257,1},{385... | collective-permute-start | bytes 147464 | tf_op jit(solution)/shard_map/ppermute | solution.py:173
  22.0 3.1 %collective-permute-start = (bf16[96,256]{1,0:T(8,128)(2,1)}, bf16[96,256]{1,0:T(8,128)(2,1)S(1)}, u32[]{:S(2)}, u32[]{:S(2)}) collective-permute-start(bf16[96,256]{1,0:T(8,128)(2,1)} %param.9), channel_id=1, source_target_pairs={{0,128},{128,0},{256,384},{384,256},{1,129},{129,1},{257,385},{385... | collective-permute-start | bytes 147464 | tf_op jit(solution)/shard_map/ppermute | solution.py:173
  25.1 2.2 %collective-permute-start.2 = (bf16[96,256]{1,0:T(8,128)(2,1)}, bf16[96,256]{1,0:T(8,128)(2,1)S(1)}, u32[]{:S(2)}, u32[]{:S(2)}) collective-permute-start(bf16[96,256]{1,0:T(8,128)(2,1)} %param.9), channel_id=1, source_target_pairs={{0,384},{128,256},{256,128},{384,0},{1,385},{129,257},{257,129},{3... | collective-permute-start | bytes 147464 | tf_op jit(solution)/shard_map/ppermute | solution.py:173
  27.3 4.7 %collective-permute-done.2 = bf16[96,256]{1,0:T(8,128)(2,1)S(1)} collective-permute-done((bf16[96,256]{1,0:T(8,128)(2,1)}, bf16[96,256]{1,0:T(8,128)(2,1)S(1)}, u32[]{:S(2)}, u32[]{:S(2)}) %collective-permute-start.2) | collective-permute-done | bytes 49184 | tf_op jit(solution)/shard_map/ppermute | solution.py:173
  32.0 1.5 pad_maximum_fusion.2
  33.6 0.9 pad_maximum_fusion.1.refs_0_
  34.5 5.9 %collective-permute-start.7 = (bf16[384,256]{1,0:T(8,128)(2,1)S(1)}, bf16[384,256]{1,0:T(8,128)(2,1)S(1)}, u32[]{:S(2)}, u32[]{:S(2)}) collective-permute-start(bf16[384,256]{1,0:T(8,128)(2,1)S(1)} %pad_maximum_fusion.1.refs_0_), channel_id=1, source_target_pairs={{0,12},{2,14},{4,0},{6,2},{8,4},{10,6},{12,8},{14,10},{1,13},{3,15... | collective-permute-start | bytes 589832 | tf_op jit(solution)/shard_map/ppermute | solution.py:150
  40.4 1.9 %collective-permute-start.6 = (bf16[384,256]{1,0:T(8,128)(2,1)S(1)}, bf16[384,256]{1,0:T(8,128)(2,1)S(1)}, u32[]{:S(2)}, u32[]{:S(2)}) collective-permute-start(bf16[384,256]{1,0:T(8,128)(2,1)S(1)} %pad_maximum_fusion.1.refs_0_), channel_id=1, source_target_pairs={{0,4},{2,6},{4,8},{6,10},{8,12},{10,14},{12,0},{14,2},{1,5},{3,7},... | collective-permute-start | bytes 589832 | tf_op jit(solution)/shard_map/ppermute | solution.py:150
  42.3 4.7 %collective-permute-start.5 = (bf16[384,256]{1,0:T(8,128)(2,1)S(1)}, bf16[384,256]{1,0:T(8,128)(2,1)S(1)}, u32[]{:S(2)}, u32[]{:S(2)}) collective-permute-start(bf16[384,256]{1,0:T(8,128)(2,1)S(1)} %pad_maximum_fusion.1.refs_0_), channel_id=1, source_target_pairs={{0,14},{2,0},{4,2},{6,4},{8,6},{10,8},{12,10},{14,12},{1,15},{3,1}... | collective-permute-start | bytes 589832 | tf_op jit(solution)/shard_map/ppermute | solution.py:150
  47.0 1.9 %collective-permute-start.4 = (bf16[384,256]{1,0:T(8,128)(2,1)S(1)}, bf16[384,256]{1,0:T(8,128)(2,1)S(1)}, u32[]{:S(2)}, u32[]{:S(2)}) collective-permute-start(bf16[384,256]{1,0:T(8,128)(2,1)S(1)} %pad_maximum_fusion.1.refs_0_), channel_id=1, source_target_pairs={{0,2},{2,4},{4,6},{6,8},{8,10},{10,12},{12,14},{14,0},{1,3},{3,5},... | collective-permute-start | bytes 589832 | tf_op jit(solution)/shard_map/ppermute | solution.py:150
  48.9 4.6 %collective-permute-start.9 = (bf16[384,256]{1,0:T(8,128)(2,1)S(1)}, bf16[384,256]{1,0:T(8,128)(2,1)S(1)}, u32[]{:S(2)}, u32[]{:S(2)}) collective-permute-start(bf16[384,256]{1,0:T(8,128)(2,1)S(1)} %collective-permute-done.7.refs_4_), channel_id=1, source_target_pairs={{0,14},{2,0},{4,2},{6,4},{8,6},{10,8},{12,10},{14,12},{1,15},{3,1}... | collective-permute-start | bytes 589832 | tf_op jit(solution)/shard_map/ppermute | solution.py:150
  53.5 1.9 %collective-permute-start.10 = (bf16[384,256]{1,0:T(8,128)(2,1)S(1)}, bf16[384,256]{1,0:T(8,128)(2,1)S(1)}, u32[]{:S(2)}, u32[]{:S(2)}) collective-permute-start(bf16[384,256]{1,0:T(8,128)(2,1)S(1)} %collective-permute-done.6.refs_3_), channel_id=1, source_target_pairs={{0,4},{2,6},{4,8},{6,10},{8,12},{10,14},{12,0},{14,2},{1,5},{3,7},... | collective-permute-start | bytes 589832 | tf_op jit(solution)/shard_map/ppermute | solution.py:150
  55.5 2.3 %collective-permute-start.8 = (bf16[384,256]{1,0:T(8,128)(2,1)S(1)}, bf16[384,256]{1,0:T(8,128)(2,1)S(1)}, u32[]{:S(2)}, u32[]{:S(2)}) collective-permute-start(bf16[384,256]{1,0:T(8,128)(2,1)S(1)} %collective-permute-done.6.refs_3_), channel_id=1, source_target_pairs={{0,2},{2,4},{4,6},{6,8},{8,10},{10,12},{12,14},{14,0},{1,3},{3,5},... | collective-permute-start | bytes 589832 | tf_op jit(solution)/shard_map/ppermute | solution.py:150
  57.8 1.1 pad_maximum_fusion.refs_9_.refs_5_
  58.9 5.2 %collective-permute-done.10.refs_7_ = bf16[384,256]{1,0:T(8,128)(2,1)S(1)} collective-permute-done((bf16[384,256]{1,0:T(8,128)(2,1)S(1)}, bf16[384,256]{1,0:T(8,128)(2,1)S(1)}, u32[]{:S(2)}, u32[]{:S(2)}) %collective-permute-start.10) | collective-permute-done | bytes 196640 | tf_op jit(solution)/shard_map/ppermute | solution.py:150
  64.1 4.3 %collective-permute-done.8.refs_5_ = bf16[384,256]{1,0:T(8,128)(2,1)S(1)} collective-permute-done((bf16[384,256]{1,0:T(8,128)(2,1)S(1)}, bf16[384,256]{1,0:T(8,128)(2,1)S(1)}, u32[]{:S(2)}, u32[]{:S(2)}) %collective-permute-start.8) | collective-permute-done | bytes 196640 | tf_op jit(solution)/shard_map/ppermute | solution.py:150
  68.4 4.9 %shard_map.55 = (bf16[2,4,4,96,256]{4,3,2,1,0:T(8,128)(2,1)S(1)}, bf16[256,3072]{1,0:T(8,128)(2,1)}, f32[256,256]{1,0:T(8,128)S(1)}, bf16[16,96,256]{2,1,0:T(8,128)(2,1)S(1)}, bf16[16,96,256]{2,1,0:T(8,128)(2,1)S(1)}) custom-call(bf16[384,256]{1,0:T(8,128)(2,1)S(1)} %pad_maximum_fusion.1.refs_0_, bf16[384,256]{1,0:T(8,128)(2,1)S(1)} %collective-permute-done.4.refs_1_, ...), custom_call_target="tpu_custom_call" | custom-call | tf_op jit(solution)/shard_map/pallas_call | solution.py:133
  73.3 5.5 %collective-permute-start.11 = (bf16[16,96,256]{2,1,0:T(8,128)(2,1)S(1)}, bf16[16,96,256]{2,1,0:T(8,128)(2,1)S(1)}, u32[]{:S(2)}, u32[]{:S(2)}) collective-permute-start(bf16[16,96,256]{2,1,0:T(8,128)(2,1)S(1)} %get-tuple-element.25), channel_id=1, source_target_pairs={{0,16},{16,0},{1,17},{17,1},{2,18},{18,2},{3,19},{19,3},{4,20},{20... | collective-permute-start | bytes 2359304 | tf_op jit(solution)/shard_map/ppermute | solution.py:164
  78.9 1.9 %collective-permute-done.11 = bf16[16,96,256]{2,1,0:T(8,128)(2,1)S(1)} collective-permute-done((bf16[16,96,256]{2,1,0:T(8,128)(2,1)S(1)}, bf16[16,96,256]{2,1,0:T(8,128)(2,1)S(1)}, u32[]{:S(2)}, u32[]{:S(2)}) %collective-permute-start.11) | collective-permute-done | bytes 786464 | tf_op jit(solution)/shard_map/ppermute | solution.py:164
  81.0 15.4 %all_to_all.20.parts_ref = bf16[4,384,256]{2,1,0:T(8,128)(2,1)S(1)} all-to-all(bf16[4,384,256]{2,1,0:T(8,128)(2,1)S(1)} %bitcast.12), channel_id=1, replica_groups=mesh['zl'=4,'x'=4,'core'=2,'y'=8,'zh'=2] {'x'}, dimensions={0} | all-to-all | bytes 1572864 | tf_op jit(solution)/shard_map/all_to_all | solution.py:207
  96.5 2.2 %collective-permute-start.14 = (bf16[384,256]{1,0:T(8,128)(2,1)S(1)}, bf16[384,256]{1,0:T(8,128)(2,1)S(1)}, u32[]{:S(2)}, u32[]{:S(2)}) collective-permute-start(bf16[384,256]{1,0:T(8,128)(2,1)S(1)} %shard_map.56.refs_0_), channel_id=1, source_target_pairs={{0,384},{128,256},{256,128},{384,0},{1,385},{129,257},{257,129},{3... | collective-permute-start | bytes 589832 | tf_op jit(solution)/shard_map/ppermute | solution.py:173
  98.6 1.9 %collective-permute-start.13 = (bf16[384,256]{1,0:T(8,128)(2,1)S(1)}, bf16[384,256]{1,0:T(8,128)(2,1)S(1)}, u32[]{:S(2)}, u32[]{:S(2)}) collective-permute-start(bf16[384,256]{1,0:T(8,128)(2,1)S(1)} %shard_map.56.refs_0_), channel_id=1, source_target_pairs={{0,256},{128,384},{256,0},{384,128},{1,257},{129,385},{257,1},{385... | collective-permute-start | bytes 589832 | tf_op jit(solution)/shard_map/ppermute | solution.py:173
  100.6 5.2 %collective-permute-start.12 = (bf16[384,256]{1,0:T(8,128)(2,1)S(1)}, bf16[384,256]{1,0:T(8,128)(2,1)S(1)}, u32[]{:S(2)}, u32[]{:S(2)}) collective-permute-start(bf16[384,256]{1,0:T(8,128)(2,1)S(1)} %shard_map.56.refs_0_), channel_id=1, source_target_pairs={{0,128},{128,0},{256,384},{384,256},{1,129},{129,1},{257,385},{385... | collective-permute-start | bytes 589832 | tf_op jit(solution)/shard_map/ppermute | solution.py:173
  105.8 9.9 %collective-permute-done.13.refs_2_ = bf16[384,256]{1,0:T(8,128)(2,1)S(1)} collective-permute-done((bf16[384,256]{1,0:T(8,128)(2,1)S(1)}, bf16[384,256]{1,0:T(8,128)(2,1)S(1)}, u32[]{:S(2)}, u32[]{:S(2)}) %collective-permute-start.13) | collective-permute-done | bytes 196640 | tf_op jit(solution)/shard_map/ppermute | solution.py:173
  116.5 15.9 %all_to_all.21 = f32[16,8,128]{2,1,0:T(8,128)S(1)} all-to-all(f32[16,8,128]{2,1,0:T(8,128)S(1)} %broadcast_in_dim.6), channel_id=1, replica_groups=mesh['zl'=4,'x'=4,'core'=2,'y'=8,'zh'=2] {'zh','y'}, dimensions={0} | all-to-all | bytes 131072 | tf_op jit(solution)/shard_map/all_to_all | solution.py:169
  132.4 10.0 %all_to_all.22.refs_0_ = f32[8,8,128]{2,1,0:T(8,128)S(1)} all-to-all(f32[8,8,128]{2,1,0:T(8,128)S(1)} %broadcast_in_dim.7), channel_id=1, replica_groups=mesh['zl'=4,'x'=4,'core'=2,'y'=8,'zh'=2] {'x','core'}, dimensions={0} | all-to-all | bytes 65536 | tf_op jit(solution)/shard_map/all_to_all | solution.py:169
  142.4 1.4 copy-done.2
  143.8 3.8 %shard_map.58 = (bf16[16,96,256]{2,1,0:T(8,128)(2,1)S(1)}, bf16[16,96,256]{2,1,0:T(8,128)(2,1)S(1)}) custom-call(f32[8,8,128]{2,1,0:T(8,128)S(1)} %all_to_all.22.refs_0_, f32[256,256]{1,0:T(8,128)S(1)} %get-tuple-element.27.refs_1_, bf16[8,384,256]{2,1,0:T(8,128)(2,1)S(1)} %bitcast.11, bf16[256,3072]{1,0:T(8,128)(2,1)S(1)} %copy-done.1, ...), custom_call_target="tpu_custom_call" | custom-call | tf_op jit(solution)/shard_map/pallas_call | solution.py:133
  147.6 2.6 %collective-permute-start.15 = (bf16[16,96,256]{2,1,0:T(8,128)(2,1)S(1)}, bf16[16,96,256]{2,1,0:T(8,128)(2,1)S(1)}, u32[]{:S(2)}, u32[]{:S(2)}) collective-permute-start(bf16[16,96,256]{2,1,0:T(8,128)(2,1)S(1)} %get-tuple-element.32), channel_id=1, source_target_pairs={{0,16},{16,0},{1,17},{17,1},{2,18},{18,2},{3,19},{19,3},{4,20},{20... | collective-permute-start | bytes 2359304 | tf_op jit(solution)/shard_map/ppermute | solution.py:164
  150.2 1.9 %collective-permute-done.15 = bf16[16,96,256]{2,1,0:T(8,128)(2,1)S(1)} collective-permute-done((bf16[16,96,256]{2,1,0:T(8,128)(2,1)S(1)}, bf16[16,96,256]{2,1,0:T(8,128)(2,1)S(1)}, u32[]{:S(2)}, u32[]{:S(2)}) %collective-permute-start.15) | collective-permute-done | bytes 786464 | tf_op jit(solution)/shard_map/ppermute | solution.py:164
  152.4 24.7 %all_to_all.23 = bf16[16,96,256]{2,1,0:T(8,128)(2,1)S(1)} all-to-all(bf16[16,96,256]{2,1,0:T(8,128)(2,1)S(1)} %add_convert_fusion), channel_id=1, replica_groups=mesh['zl'=4,'x'=4,'core'=2,'y'=8,'zh'=2] {'x','zl'}, dimensions={0} | all-to-all | bytes 1572864 | tf_op jit(solution)/shard_map/all_to_all | solution.py:220
  (29 shorter events, 2.3 us)
Async XLA Ops:
  6.5 61.9 %all-gather.5.cloned.1.call-start = ((), (), s32[]{:S(2)}) async-start(), calls=%async_computation.4 | async-start | bytes 1769472 | tf_op jit(solution)/shard_map/all_gather | solution.py:177
  6.5 25.5 %collective-permute-start.3 = (bf16[192,256]{1,0:T(8,128)(2,1)}, bf16[192,256]{1,0:T(8,128)(2,1)S(1)}, u32[]{:S(2)}, u32[]{:S(2)}) collective-permute-start(bf16[192,256]{1,0:T(8,128)(2,1)} %bitcast.17), channel_id=1, source_target_pairs={{0,1},{1,0},{2,3},{3,2},{4,5},{5,4},{6,7},{7,6},{8,9},{9,8},{10,11... | collective-permute-start | bytes 294920 | tf_op jit(solution)/shard_map/ppermute | solution.py:191
  18.0 9.3 %collective-permute-start.1 = (bf16[96,256]{1,0:T(8,128)(2,1)}, bf16[96,256]{1,0:T(8,128)(2,1)S(1)}, u32[]{:S(2)}, u32[]{:S(2)}) collective-permute-start(bf16[96,256]{1,0:T(8,128)(2,1)} %param.9), channel_id=1, source_target_pairs={{0,256},{128,384},{256,0},{384,128},{1,257},{129,385},{257,1},{385... | collective-permute-start | bytes 147464 | tf_op jit(solution)/shard_map/ppermute | solution.py:173
  22.0 5.3 %collective-permute-start = (bf16[96,256]{1,0:T(8,128)(2,1)}, bf16[96,256]{1,0:T(8,128)(2,1)S(1)}, u32[]{:S(2)}, u32[]{:S(2)}) collective-permute-start(bf16[96,256]{1,0:T(8,128)(2,1)} %param.9), channel_id=1, source_target_pairs={{0,128},{128,0},{256,384},{384,256},{1,129},{129,1},{257,385},{385... | collective-permute-start | bytes 147464 | tf_op jit(solution)/shard_map/ppermute | solution.py:173
  25.1 6.9 %collective-permute-start.2 = (bf16[96,256]{1,0:T(8,128)(2,1)}, bf16[96,256]{1,0:T(8,128)(2,1)S(1)}, u32[]{:S(2)}, u32[]{:S(2)}) collective-permute-start(bf16[96,256]{1,0:T(8,128)(2,1)} %param.9), channel_id=1, source_target_pairs={{0,384},{128,256},{256,128},{384,0},{1,385},{129,257},{257,129},{3... | collective-permute-start | bytes 147464 | tf_op jit(solution)/shard_map/ppermute | solution.py:173
  33.5 108.8 %all-gather.7.cloned.1.call-start = ((), (), s32[]{:S(2)}) async-start(), calls=%async_computation.5 | async-start | bytes 1769472 | tf_op jit(solution)/shard_map/all_gather | solution.py:177
  34.5 14.4 %collective-permute-start.7 = (bf16[384,256]{1,0:T(8,128)(2,1)S(1)}, bf16[384,256]{1,0:T(8,128)(2,1)S(1)}, u32[]{:S(2)}, u32[]{:S(2)}) collective-permute-start(bf16[384,256]{1,0:T(8,128)(2,1)S(1)} %pad_maximum_fusion.1.refs_0_), channel_id=1, source_target_pairs={{0,12},{2,14},{4,0},{6,2},{8,4},{10,6},{12,8},{14,10},{1,13},{3,15... | collective-permute-start | bytes 589832 | tf_op jit(solution)/shard_map/ppermute | solution.py:150
  40.4 13.1 %collective-permute-start.6 = (bf16[384,256]{1,0:T(8,128)(2,1)S(1)}, bf16[384,256]{1,0:T(8,128)(2,1)S(1)}, u32[]{:S(2)}, u32[]{:S(2)}) collective-permute-start(bf16[384,256]{1,0:T(8,128)(2,1)S(1)} %pad_maximum_fusion.1.refs_0_), channel_id=1, source_target_pairs={{0,4},{2,6},{4,8},{6,10},{8,12},{10,14},{12,0},{14,2},{1,5},{3,7},... | collective-permute-start | bytes 589832 | tf_op jit(solution)/shard_map/ppermute | solution.py:150
  42.3 16.6 %collective-permute-start.5 = (bf16[384,256]{1,0:T(8,128)(2,1)S(1)}, bf16[384,256]{1,0:T(8,128)(2,1)S(1)}, u32[]{:S(2)}, u32[]{:S(2)}) collective-permute-start(bf16[384,256]{1,0:T(8,128)(2,1)S(1)} %pad_maximum_fusion.1.refs_0_), channel_id=1, source_target_pairs={{0,14},{2,0},{4,2},{6,4},{8,6},{10,8},{12,10},{14,12},{1,15},{3,1}... | collective-permute-start | bytes 589832 | tf_op jit(solution)/shard_map/ppermute | solution.py:150
  47.0 11.9 %collective-permute-start.4 = (bf16[384,256]{1,0:T(8,128)(2,1)S(1)}, bf16[384,256]{1,0:T(8,128)(2,1)S(1)}, u32[]{:S(2)}, u32[]{:S(2)}) collective-permute-start(bf16[384,256]{1,0:T(8,128)(2,1)S(1)} %pad_maximum_fusion.1.refs_0_), channel_id=1, source_target_pairs={{0,2},{2,4},{4,6},{6,8},{8,10},{10,12},{12,14},{14,0},{1,3},{3,5},... | collective-permute-start | bytes 589832 | tf_op jit(solution)/shard_map/ppermute | solution.py:150
  48.9 10.0 %collective-permute-start.9 = (bf16[384,256]{1,0:T(8,128)(2,1)S(1)}, bf16[384,256]{1,0:T(8,128)(2,1)S(1)}, u32[]{:S(2)}, u32[]{:S(2)}) collective-permute-start(bf16[384,256]{1,0:T(8,128)(2,1)S(1)} %collective-permute-done.7.refs_4_), channel_id=1, source_target_pairs={{0,14},{2,0},{4,2},{6,4},{8,6},{10,8},{12,10},{14,12},{1,15},{3,1}... | collective-permute-start | bytes 589832 | tf_op jit(solution)/shard_map/ppermute | solution.py:150
  53.5 10.6 %collective-permute-start.10 = (bf16[384,256]{1,0:T(8,128)(2,1)S(1)}, bf16[384,256]{1,0:T(8,128)(2,1)S(1)}, u32[]{:S(2)}, u32[]{:S(2)}) collective-permute-start(bf16[384,256]{1,0:T(8,128)(2,1)S(1)} %collective-permute-done.6.refs_3_), channel_id=1, source_target_pairs={{0,4},{2,6},{4,8},{6,10},{8,12},{10,14},{12,0},{14,2},{1,5},{3,7},... | collective-permute-start | bytes 589832 | tf_op jit(solution)/shard_map/ppermute | solution.py:150
  55.5 12.9 %collective-permute-start.8 = (bf16[384,256]{1,0:T(8,128)(2,1)S(1)}, bf16[384,256]{1,0:T(8,128)(2,1)S(1)}, u32[]{:S(2)}, u32[]{:S(2)}) collective-permute-start(bf16[384,256]{1,0:T(8,128)(2,1)S(1)} %collective-permute-done.6.refs_3_), channel_id=1, source_target_pairs={{0,2},{2,4},{4,6},{6,8},{8,10},{10,12},{12,14},{14,0},{1,3},{3,5},... | collective-permute-start | bytes 589832 | tf_op jit(solution)/shard_map/ppermute | solution.py:150
  73.3 23.1 %copy-start = (bf16[2,4,4,96,256]{4,3,2,1,0:T(8,128)(2,1)}, bf16[2,4,4,96,256]{4,3,2,1,0:T(8,128)(2,1)S(1)}, u32[]{:S(2)}) copy-start(bf16[2,4,4,96,256]{4,3,2,1,0:T(8,128)(2,1)S(1)} %get-tuple-element.30.refs_4_) | copy-start | bytes 4718596
  73.3 7.4 %collective-permute-start.11 = (bf16[16,96,256]{2,1,0:T(8,128)(2,1)S(1)}, bf16[16,96,256]{2,1,0:T(8,128)(2,1)S(1)}, u32[]{:S(2)}, u32[]{:S(2)}) collective-permute-start(bf16[16,96,256]{2,1,0:T(8,128)(2,1)S(1)} %get-tuple-element.25), channel_id=1, source_target_pairs={{0,16},{16,0},{1,17},{17,1},{2,18},{18,2},{3,19},{19,3},{4,20},{20... | collective-permute-start | bytes 2359304 | tf_op jit(solution)/shard_map/ppermute | solution.py:164
  81.0 61.4 %copy-start.1 = (bf16[256,3072]{1,0:T(8,128)(2,1)S(1)}, bf16[256,3072]{1,0:T(8,128)(2,1)}, u32[]{:S(2)}) copy-start(bf16[256,3072]{1,0:T(8,128)(2,1)} %get-tuple-element.29.refs_3_) | copy-start | bytes 4718596
  96.5 9.3 %collective-permute-start.14 = (bf16[384,256]{1,0:T(8,128)(2,1)S(1)}, bf16[384,256]{1,0:T(8,128)(2,1)S(1)}, u32[]{:S(2)}, u32[]{:S(2)}) collective-permute-start(bf16[384,256]{1,0:T(8,128)(2,1)S(1)} %shard_map.56.refs_0_), channel_id=1, source_target_pairs={{0,384},{128,256},{256,128},{384,0},{1,385},{129,257},{257,129},{3... | collective-permute-start | bytes 589832 | tf_op jit(solution)/shard_map/ppermute | solution.py:173
  98.6 17.0 %collective-permute-start.13 = (bf16[384,256]{1,0:T(8,128)(2,1)S(1)}, bf16[384,256]{1,0:T(8,128)(2,1)S(1)}, u32[]{:S(2)}, u32[]{:S(2)}) collective-permute-start(bf16[384,256]{1,0:T(8,128)(2,1)S(1)} %shard_map.56.refs_0_), channel_id=1, source_target_pairs={{0,256},{128,384},{256,0},{384,128},{1,257},{129,385},{257,1},{385... | collective-permute-start | bytes 589832 | tf_op jit(solution)/shard_map/ppermute | solution.py:173
  100.6 15.1 %collective-permute-start.12 = (bf16[384,256]{1,0:T(8,128)(2,1)S(1)}, bf16[384,256]{1,0:T(8,128)(2,1)S(1)}, u32[]{:S(2)}, u32[]{:S(2)}) collective-permute-start(bf16[384,256]{1,0:T(8,128)(2,1)S(1)} %shard_map.56.refs_0_), channel_id=1, source_target_pairs={{0,128},{128,0},{256,384},{384,256},{1,129},{129,1},{257,385},{385... | collective-permute-start | bytes 589832 | tf_op jit(solution)/shard_map/ppermute | solution.py:173
  142.4 1.4 copy-start.2
  147.6 4.5 %collective-permute-start.15 = (bf16[16,96,256]{2,1,0:T(8,128)(2,1)S(1)}, bf16[16,96,256]{2,1,0:T(8,128)(2,1)S(1)}, u32[]{:S(2)}, u32[]{:S(2)}) collective-permute-start(bf16[16,96,256]{2,1,0:T(8,128)(2,1)S(1)} %get-tuple-element.32), channel_id=1, source_target_pairs={{0,16},{16,0},{1,17},{17,1},{2,18},{18,2},{3,19},{19,3},{4,20},{20... | collective-permute-start | bytes 2359304 | tf_op jit(solution)/shard_map/ppermute | solution.py:164
Sparse Core Ops, SparseCore 0:
  33.7 28.3 all-gather.4
  116.6 23.3 all-gather.6

commit v6 on v5

--- a/solution.py
+++ b/solution.py
@@ -12,8 +12,8 @@
 EPS = 1e-06
 F32 = jnp.float32
 BF16 = jnp.bfloat16
-AXES = ("zl", "x", "core", "y", "zh")
-SIZES = (4, 4, 2, 8, 2)
+AXES = ("z2", "z1", "x", "core", "y", "zh")
+SIZES = (2, 2, 4, 2, 8, 2)
 STEPS = (0, -1, 1, -2, 2, -3, 3, -4)
 
 
@@ -58,15 +58,17 @@
         copy.wait()
 
 
-def by_zl(src_ref, dst_ref):
-    zl = lax.axis_index("zl")
-    return [(src_ref.at[:, k, :ROWS], dst_ref.at[:, jnp.bitwise_xor(zl, k)]) for k in range(4)]
+def by_z(src_ref, dst_ref):
+    z1, z2 = lax.axis_index("z1"), lax.axis_index("z2")
+    return [
+        (src_ref.at[:, k], dst_ref.at[:, jnp.bitwise_xor(z1, k % 2), jnp.bitwise_xor(z2, k // 2)]) for k in range(4)
+    ]
 
 
 def first_kernel(scale, *refs):
     toks, refs = refs[:8], refs[8:]
     w_any, sides_any, normt_ref, normed_ref, query_ref, keep_ref, send_ref, w_ref, sides_ref, sems = refs
-    copies = fetch(by_zl(w_any, w_ref) + [(sides_any, sides_ref)], sems)
+    copies = fetch(by_z(w_any, w_ref) + [(sides_any, sides_ref)], sems)
     y, zh = lax.axis_index("y"), lax.axis_index("zh")
     width = normed_ref.shape[1]
     total = jnp.zeros((1, normt_ref.shape[-1]), F32)
@@ -83,7 +85,7 @@
         from_y = lax.rem(y + (step + 8), 8)
         for part in range(4):
             x = 2 * lax.rem(from_y, 2) + jnp.bitwise_xor(zh, part // 2)
-            normt_ref[part % 2, x, from_y // 2] = block[part * ROWS:(part + 1) * ROWS]
+            normt_ref[part % 2, x, lax.rem(from_y // 2, 2), from_y // 4] = block[part * ROWS:(part + 1) * ROWS]
     run = 4 * ROWS
     for x in range(4):
         for c in range(2):
@@ -107,11 +109,18 @@
     out_ref[...] = jnp.sum(parts_ref[...].astype(F32), 0).astype(BF16)
 
 
-def last_sum_kernel(*refs):
-    parts, (first_ref, square_ref) = refs[:4], refs[4:]
-    total = sum(ref[...].astype(F32) for ref in parts)
-    first_ref[...] = total.astype(BF16)
-    square = jnp.sum((total * total).reshape(-1, 8, total.shape[1]), 0)
+def half_sums_kernel(parts_ref, own_ref, give_ref):
+    z2 = lax.axis_index("z2")
+    own_ref[...] = jnp.sum(parts_ref[:, z2].astype(F32), 0)
+    give_ref[...] = jnp.sum(parts_ref[:, 1 - z2].astype(F32), 0).astype(BF16)
+
+
+def pair_kernel(mine_ref, theirs_ref, first_ref, square_ref):
+    z1 = lax.axis_index("z1")
+    first_ref[z1] = mine_ref[...]
+    first_ref[1 - z1] = theirs_ref[...]
+    mine, theirs = mine_ref[...].astype(F32), theirs_ref[...].astype(F32)
+    square = jnp.sum((mine * mine + theirs * theirs).reshape(-1, 8, mine.shape[1]), 0)
     square_ref[...] = square[:, :HEAD] + square[:, HEAD:]
 
 
@@ -160,9 +169,14 @@
     return block, back1, ahead1, back2, ahead2, back3, ahead3, back4
 
 
-def sum_core(keep, send):
-    got = lax.ppermute(send, "core", swap(2, 1))
-    return (keep.astype(F32) + got.astype(F32)).astype(BF16)
+def add(a, b):
+    return (a.astype(F32) + b.astype(F32)).astype(BF16)
+
+
+def scatter_parts(keep, send):
+    both = add(keep, lax.ppermute(send, "core", swap(2, 1)))
+    pieces = both.reshape(8, 2 * ROWS, both.shape[-1])
+    return lax.all_to_all(pieces, ("x", "z1"), 0, 0, tiled=True)
 
 
 def everywhere(value, axes, size):
@@ -170,7 +184,7 @@
 
 
 def along_z(block):
-    return [block] + [lax.ppermute(block, "zl", swap(4, k)) for k in (1, 2, 3)]
+    return [block] + [lax.ppermute(block, ("z2", "z1"), swap(4, k)) for k in (1, 2, 3)]
 
 
 def gather_chips(blocks):
@@ -184,8 +198,8 @@
     model_width = feats * 16
     scale = 1.0 / math.sqrt(count * 32)
     radius = 0.3 * math.sqrt(model_width + cols * 16)
-    whole, half = (8, 4, ROWS, cols), (16, ROWS, cols)
-    normt_like = (2, 4, 4, ROWS, count)
+    whole, half = (8, 2, 2, ROWS, cols), (16, ROWS, cols)
+    normt_like = (2, 4, 2, 2, ROWS, count)
     sides = jnp.stack([keys, values, cotangent])
 
     other = lax.ppermute(tok, "zh", swap(2, 1))
@@ -203,10 +217,11 @@
         scratch=(pltpu.VMEM(whole, BF16), pltpu.VMEM(sides.shape, BF16), pltpu.SemaphoreType.DMA((5,))),
     )(*blocks, weight, sides)
 
-    quarter = (4 * ROWS, cols)
-    parts = lax.all_to_all(sum_core(keep, send).reshape(4, *quarter), "x", 0, 0, tiled=True)
-    partial = call(sum_kernel, [(quarter, BF16)], 48)(parts)[0]
-    first, square = call(last_sum_kernel, [(quarter, BF16), ((8, HEAD), F32)], 48)(*along_z(partial))
+    pair = (2 * ROWS, cols)
+    partial = call(sum_kernel, [(pair, BF16)], 48)(scatter_parts(keep, send))[0]
+    mine = add(partial, lax.ppermute(partial, "z2", swap(2, 1)))
+    theirs = lax.ppermute(mine, "z1", swap(2, 1))
+    first, square = call(pair_kernel, [((2, *pair), BF16), ((8, HEAD), F32)], 48)(mine, theirs)
     first_all = gather_chips(first)
     square = jnp.sum(everywhere(square, ("zh", "y"), 16), 0)
     square = everywhere(square, ("x", "core"), 8)
@@ -217,11 +232,12 @@
         anywhere=(4,),
         scratch=(pltpu.VMEM(normt_like, BF16), pltpu.SemaphoreType.DMA((1,))),
     )(square, query, first_all, normed, normt, sides)
-    parts = lax.all_to_all(sum_core(keep, send), ("x", "zl"), 0, 0, tiled=True)
-    return jnp.sum(parts.astype(F32), 0)
+    parts = scatter_parts(keep, send).reshape(8, 2, ROWS, cols)
+    own, give = call(half_sums_kernel, [((ROWS, cols), F32), ((ROWS, cols), BF16)], 48)(parts)
+    return own + lax.ppermute(give, "z2", swap(2, 1)).astype(F32)
 
 
 def solution(mesh):
     cut = Mesh(mesh.devices.reshape(SIZES), AXES)
-    spec = P(("zl", "x", "core"), ("y", "zh"))
+    spec = P(AXES[:4], AXES[4:])
     return jax.shard_map(shards, mesh=cut, in_specs=(spec,) * 5, out_specs=spec, check_vma=False)

time: 186 us -> 179 us (0.962)
  blocking collectives: 65.9 us -> 59.5 us
  starting transfers between devices: 61.4 us -> 59.1 us
  waiting for transfers between devices: 27.9 us -> 30 us
    all_to_all x2, blocking collectives: 40.1 us -> 31 us  [scatter_parts(): return lax.all_to_all(pieces, ('x', 'z1'), 0, 0, tiled=True)]
    all_to_all x2, blocking collectives: 25.8 us -> 28.5 us  [everywhere(): lax.all_to_all(jnp.broadcast_to(value, (size, *value.shape)), axes, 0, 0,...]
    ppermute x8, starting transfers between devices: 26.7 us -> 24.4 us  [the longest x3 9.27 us: along_z(): lax.ppermute(block, ('z2', 'z1'), swap(4, k))]
    ppermute x8, waiting for transfers between devices: 18.4 us -> 20.5 us  [the longest x1 5.15 us: shards(): mine = add(partial, lax.ppermute(partial, 'z2', swap(2, 1)))]
    pallas_call x4 -> x5, Pallas kernels: 9.62 us -> 9.64 us  [run(): pl.pallas_call(kernel, out_shape=[jax.ShapeDtypeStruct(s, d) for s, d in...]
  transfers between devices with their start and end apart: 18 -> 18, of which waited for: 6 -> 8; matrix products, arithmetic and copies ran while one was open for 1% -> 1% of each run, Pallas kernels for 0% -> 0%
where the time goes in v6:
time: 179 us; the launch traced here: 178 us
  blocking collectives  59.5 us (33%)
  starting transfers between devices  59.1 us (33%)
  waiting for transfers between devices  30 us (17%)
  between operations  13.7 us (8%)
  Pallas kernels  9.64 us (5%)
  other arithmetic  4.66 us (3%)
    all_to_all x2, blocking collectives, scatter_parts(): return lax.all_to_all(pieces, ('x', 'z1'), 0, 0, tiled=True)  31 us
    all_to_all x2, blocking collectives, everywhere(): lax.all_to_all(jnp.broadcast_to(value, (size, *value.shape)), axes, 0, 0,...  28.5 us
    ppermute x7, starting transfers between devices, turn(): return lax.ppermute(value, 'y', [(i, (i + step) % 8) for i in range(8)])  23.2 us
    ppermute x1, starting transfers between devices, shards(): other = lax.ppermute(tok, 'zh', swap(2, 1))  11.5 us
    pallas_call x5, Pallas kernels, run(): pl.pallas_call(kernel, out_shape=[jax.ShapeDtypeStruct(s, d) for s, d in...  9.64 us
    ppermute x7, waiting for transfers between devices, turn(): return lax.ppermute(value, 'y', [(i, (i + step) % 8) for i in range(8)])  9.47 us
    ppermute x3, starting transfers between devices, along_z(): lax.ppermute(block, ('z2', 'z1'), swap(4, k))  9.27 us
    ppermute x2, starting transfers between devices, scatter_parts(): both = add(keep, lax.ppermute(send, 'core', swap(2, 1)))  8.17 us
  transfers between devices with their start and end apart: 18, of which 8 were waited for; matrix products, arithmetic and copies ran while one was open for 1% of the time, Pallas kernels for 0%

profile of v6, /device:TPU:1, one launch (start us, length us, event | category | flops | bytes accessed | tf_op | source)
XLA Modules:
  0.0 178.0 jit_solution(3257334836979889723)
XLA Ops:
  6.5 11.5 %collective-permute-start.3 = (bf16[192,256]{1,0:T(8,128)(2,1)}, bf16[192,256]{1,0:T(8,128)(2,1)S(1)}, u32[]{:S(2)}, u32[]{:S(2)}) collective-permute-start(bf16[192,256]{1,0:T(8,128)(2,1)} %bitcast.21), channel_id=1, source_target_pairs={{0,1},{1,0},{2,3},{3,2},{4,5},{5,4},{6,7},{7,6},{8,9},{9,8},{10,11... | collective-permute-start | bytes 294920 | tf_op jit(solution)/shard_map/ppermute | solution.py:205
  18.0 4.0 %collective-permute-start.1 = (bf16[96,256]{1,0:T(8,128)(2,1)}, bf16[96,256]{1,0:T(8,128)(2,1)S(1)}, u32[]{:S(2)}, u32[]{:S(2)}) collective-permute-start(bf16[96,256]{1,0:T(8,128)(2,1)} %param.9), channel_id=1, source_target_pairs={{0,256},{128,384},{256,0},{384,128},{1,257},{129,385},{257,1},{385... | collective-permute-start | bytes 147464 | tf_op jit(solution)/shard_map/ppermute | solution.py:187
  22.0 3.1 %collective-permute-start = (bf16[96,256]{1,0:T(8,128)(2,1)}, bf16[96,256]{1,0:T(8,128)(2,1)S(1)}, u32[]{:S(2)}, u32[]{:S(2)}) collective-permute-start(bf16[96,256]{1,0:T(8,128)(2,1)} %param.9), channel_id=1, source_target_pairs={{0,128},{128,0},{256,384},{384,256},{1,129},{129,1},{257,385},{385... | collective-permute-start | bytes 147464 | tf_op jit(solution)/shard_map/ppermute | solution.py:187
  25.1 2.2 %collective-permute-start.2 = (bf16[96,256]{1,0:T(8,128)(2,1)}, bf16[96,256]{1,0:T(8,128)(2,1)S(1)}, u32[]{:S(2)}, u32[]{:S(2)}) collective-permute-start(bf16[96,256]{1,0:T(8,128)(2,1)} %param.9), channel_id=1, source_target_pairs={{0,384},{128,256},{256,128},{384,0},{1,385},{129,257},{257,129},{3... | collective-permute-start | bytes 147464 | tf_op jit(solution)/shard_map/ppermute | solution.py:187
  27.3 4.7 %collective-permute-done.2 = bf16[96,256]{1,0:T(8,128)(2,1)S(1)} collective-permute-done((bf16[96,256]{1,0:T(8,128)(2,1)}, bf16[96,256]{1,0:T(8,128)(2,1)S(1)}, u32[]{:S(2)}, u32[]{:S(2)}) %collective-permute-start.2) | collective-permute-done | bytes 49184 | tf_op jit(solution)/shard_map/ppermute | solution.py:187
  32.0 1.5 pad_maximum_fusion.2
  34.5 5.9 %collective-permute-start.7 = (bf16[384,256]{1,0:T(8,128)(2,1)S(1)}, bf16[384,256]{1,0:T(8,128)(2,1)S(1)}, u32[]{:S(2)}, u32[]{:S(2)}) collective-permute-start(bf16[384,256]{1,0:T(8,128)(2,1)S(1)} %pad_maximum_fusion.1.refs_0_), channel_id=1, source_target_pairs={{0,12},{2,14},{4,0},{6,2},{8,4},{10,6},{12,8},{14,10},{1,13},{3,15... | collective-permute-start | bytes 589832 | tf_op jit(solution)/shard_map/ppermute | solution.py:159
  40.4 1.9 %collective-permute-start.6 = (bf16[384,256]{1,0:T(8,128)(2,1)S(1)}, bf16[384,256]{1,0:T(8,128)(2,1)S(1)}, u32[]{:S(2)}, u32[]{:S(2)}) collective-permute-start(bf16[384,256]{1,0:T(8,128)(2,1)S(1)} %pad_maximum_fusion.1.refs_0_), channel_id=1, source_target_pairs={{0,4},{2,6},{4,8},{6,10},{8,12},{10,14},{12,0},{14,2},{1,5},{3,7},... | collective-permute-start | bytes 589832 | tf_op jit(solution)/shard_map/ppermute | solution.py:159
  42.3 4.7 %collective-permute-start.5 = (bf16[384,256]{1,0:T(8,128)(2,1)S(1)}, bf16[384,256]{1,0:T(8,128)(2,1)S(1)}, u32[]{:S(2)}, u32[]{:S(2)}) collective-permute-start(bf16[384,256]{1,0:T(8,128)(2,1)S(1)} %pad_maximum_fusion.1.refs_0_), channel_id=1, source_target_pairs={{0,14},{2,0},{4,2},{6,4},{8,6},{10,8},{12,10},{14,12},{1,15},{3,1}... | collective-permute-start | bytes 589832 | tf_op jit(solution)/shard_map/ppermute | solution.py:159
  47.0 1.9 %collective-permute-start.4 = (bf16[384,256]{1,0:T(8,128)(2,1)S(1)}, bf16[384,256]{1,0:T(8,128)(2,1)S(1)}, u32[]{:S(2)}, u32[]{:S(2)}) collective-permute-start(bf16[384,256]{1,0:T(8,128)(2,1)S(1)} %pad_maximum_fusion.1.refs_0_), channel_id=1, source_target_pairs={{0,2},{2,4},{4,6},{6,8},{8,10},{10,12},{12,14},{14,0},{1,3},{3,5},... | collective-permute-start | bytes 589832 | tf_op jit(solution)/shard_map/ppermute | solution.py:159
  49.0 4.6 %collective-permute-start.9 = (bf16[384,256]{1,0:T(8,128)(2,1)S(1)}, bf16[384,256]{1,0:T(8,128)(2,1)S(1)}, u32[]{:S(2)}, u32[]{:S(2)}) collective-permute-start(bf16[384,256]{1,0:T(8,128)(2,1)S(1)} %collective-permute-done.7.refs_4_), channel_id=1, source_target_pairs={{0,14},{2,0},{4,2},{6,4},{8,6},{10,8},{12,10},{14,12},{1,15},{3,1}... | collective-permute-start | bytes 589832 | tf_op jit(solution)/shard_map/ppermute | solution.py:159
  53.5 1.9 %collective-permute-start.10 = (bf16[384,256]{1,0:T(8,128)(2,1)S(1)}, bf16[384,256]{1,0:T(8,128)(2,1)S(1)}, u32[]{:S(2)}, u32[]{:S(2)}) collective-permute-start(bf16[384,256]{1,0:T(8,128)(2,1)S(1)} %collective-permute-done.6.refs_3_), channel_id=1, source_target_pairs={{0,4},{2,6},{4,8},{6,10},{8,12},{10,14},{12,0},{14,2},{1,5},{3,7},... | collective-permute-start | bytes 589832 | tf_op jit(solution)/shard_map/ppermute | solution.py:159
  55.5 2.3 %collective-permute-start.8 = (bf16[384,256]{1,0:T(8,128)(2,1)S(1)}, bf16[384,256]{1,0:T(8,128)(2,1)S(1)}, u32[]{:S(2)}, u32[]{:S(2)}) collective-permute-start(bf16[384,256]{1,0:T(8,128)(2,1)S(1)} %collective-permute-done.6.refs_3_), channel_id=1, source_target_pairs={{0,2},{2,4},{4,6},{6,8},{8,10},{10,12},{12,14},{14,0},{1,3},{3,5},... | collective-permute-start | bytes 589832 | tf_op jit(solution)/shard_map/ppermute | solution.py:159
  58.9 5.2 %collective-permute-done.10.refs_7_ = bf16[384,256]{1,0:T(8,128)(2,1)S(1)} collective-permute-done((bf16[384,256]{1,0:T(8,128)(2,1)S(1)}, bf16[384,256]{1,0:T(8,128)(2,1)S(1)}, u32[]{:S(2)}, u32[]{:S(2)}) %collective-permute-start.10) | collective-permute-done | bytes 196640 | tf_op jit(solution)/shard_map/ppermute | solution.py:159
  64.1 4.3 %collective-permute-done.8.refs_5_ = bf16[384,256]{1,0:T(8,128)(2,1)S(1)} collective-permute-done((bf16[384,256]{1,0:T(8,128)(2,1)S(1)}, bf16[384,256]{1,0:T(8,128)(2,1)S(1)}, u32[]{:S(2)}, u32[]{:S(2)}) %collective-permute-start.8) | collective-permute-done | bytes 196640 | tf_op jit(solution)/shard_map/ppermute | solution.py:159
  68.4 4.9 %shard_map.55 = (bf16[2,4,2,2,96,256]{5,4,3,2,1,0:T(8,128)(2,1)S(1)}, bf16[256,3072]{1,0:T(8,128)(2,1)}, f32[256,256]{1,0:T(8,128)S(1)}, bf16[16,96,256]{2,1,0:T(8,128)(2,1)S(1)}, bf16[16,96,256]{2,1,0:T(8,128)(2,1)S(1)}) custom-call(bf16[384,256]{1,0:T(8,128)(2,1)S(1)} %pad_maximum_fusion.1.refs_0_, bf16[384,256]{1,0:T(8,128)(2,1)S(1)} %collective-permute-done.4.refs_1_, ...), custom_call_target="tpu_custom_call" | custom-call | tf_op jit(solution)/shard_map/pallas_call | solution.py:142
  73.3 5.5 %collective-permute-start.11 = (bf16[16,96,256]{2,1,0:T(8,128)(2,1)S(1)}, bf16[16,96,256]{2,1,0:T(8,128)(2,1)S(1)}, u32[]{:S(2)}, u32[]{:S(2)}) collective-permute-start(bf16[16,96,256]{2,1,0:T(8,128)(2,1)S(1)} %get-tuple-element.27), channel_id=1, source_target_pairs={{0,16},{16,0},{1,17},{17,1},{2,18},{18,2},{3,19},{19,3},{4,20},{20... | collective-permute-start | bytes 2359304 | tf_op jit(solution)/shard_map/ppermute | solution.py:177
  78.9 1.9 %collective-permute-done.11 = bf16[16,96,256]{2,1,0:T(8,128)(2,1)S(1)} collective-permute-done((bf16[16,96,256]{2,1,0:T(8,128)(2,1)S(1)}, bf16[16,96,256]{2,1,0:T(8,128)(2,1)S(1)}, u32[]{:S(2)}, u32[]{:S(2)}) %collective-permute-start.11) | collective-permute-done | bytes 786464 | tf_op jit(solution)/shard_map/ppermute | solution.py:177
  81.0 16.0 %all_to_all.20.parts_ref = bf16[8,192,256]{2,1,0:T(8,128)(2,1)S(1)} all-to-all(bf16[8,192,256]{2,1,0:T(8,128)(2,1)S(1)} %bitcast.15), channel_id=1, replica_groups=mesh['z2'=2,'z1'=2,'x'=4,'core'=2,'y'=8,'zh'=2] {'x','z1'}, dimensions={0} | all-to-all | bytes 1572864 | tf_op jit(solution)/shard_map/all_to_all | solution.py:179
  97.1 2.2 %collective-permute-start.12 = (bf16[192,256]{1,0:T(8,128)(2,1)S(1)}, bf16[192,256]{1,0:T(8,128)(2,1)S(1)}, u32[]{:S(2)}, u32[]{:S(2)}) collective-permute-start(bf16[192,256]{1,0:T(8,128)(2,1)S(1)} %shard_map.56), channel_id=1, source_target_pairs={{0,256},{256,0},{1,257},{257,1},{2,258},{258,2},{3,259},{259,3},{4... | collective-permute-start | bytes 294920 | tf_op jit(solution)/shard_map/ppermute | solution.py:222
  99.3 5.1 %collective-permute-done.12 = bf16[192,256]{1,0:T(8,128)(2,1)S(1)} collective-permute-done((bf16[192,256]{1,0:T(8,128)(2,1)S(1)}, bf16[192,256]{1,0:T(8,128)(2,1)S(1)}, u32[]{:S(2)}, u32[]{:S(2)}) %collective-permute-start.12) | collective-permute-done | bytes 98336 | tf_op jit(solution)/shard_map/ppermute | solution.py:222
  104.4 1.9 %collective-permute-start.13 = (bf16[192,256]{1,0:T(8,128)(2,1)S(1)}, bf16[192,256]{1,0:T(8,128)(2,1)S(1)}, u32[]{:S(2)}, u32[]{:S(2)}) collective-permute-start(bf16[192,256]{1,0:T(8,128)(2,1)S(1)} %add_convert_fusion.2.mine_ref), channel_id=1, source_target_pairs={{0,128},{128,0},{1,129},{129,1},{2,130},{130,2},{3,131},{131,3},{4... | collective-permute-start | bytes 294920 | tf_op jit(solution)/shard_map/ppermute | solution.py:223
  106.4 3.4 %collective-permute-done.13.theirs_ref = bf16[192,256]{1,0:T(8,128)(2,1)S(1)} collective-permute-done((bf16[192,256]{1,0:T(8,128)(2,1)S(1)}, bf16[192,256]{1,0:T(8,128)(2,1)S(1)}, u32[]{:S(2)}, u32[]{:S(2)}) %collective-permute-start.13) | collective-permute-done | bytes 98336 | tf_op jit(solution)/shard_map/ppermute | solution.py:223
  110.5 15.9 %all_to_all.21 = f32[16,8,128]{2,1,0:T(8,128)S(1)} all-to-all(f32[16,8,128]{2,1,0:T(8,128)S(1)} %broadcast_in_dim.6), channel_id=1, replica_groups=mesh['z2'=2,'z1'=2,'x'=4,'core'=2,'y'=8,'zh'=2] {'zh','y'}, dimensions={0} | all-to-all | bytes 131072 | tf_op jit(solution)/shard_map/all_to_all | solution.py:183
  126.4 12.6 %all_to_all.22.refs_0_ = f32[8,8,128]{2,1,0:T(8,128)S(1)} all-to-all(f32[8,8,128]{2,1,0:T(8,128)S(1)} %broadcast_in_dim.7), channel_id=1, replica_groups=mesh['z2'=2,'z1'=2,'x'=4,'core'=2,'y'=8,'zh'=2] {'x','core'}, dimensions={0} | all-to-all | bytes 65536 | tf_op jit(solution)/shard_map/all_to_all | solution.py:183
  139.1 1.4 copy-done.2
  140.5 3.8 %shard_map.58 = (bf16[16,96,256]{2,1,0:T(8,128)(2,1)S(1)}, bf16[16,96,256]{2,1,0:T(8,128)(2,1)S(1)}) custom-call(f32[8,8,128]{2,1,0:T(8,128)S(1)} %all_to_all.22.refs_0_, f32[256,256]{1,0:T(8,128)S(1)} %get-tuple-element.29.refs_1_, bf16[8,2,192,256]{3,2,1,0:T(8,128)(2,1)S(1)} %bitcast.14, bf16[256,3072]{1,0:T(8,128)(2,1)S(1)} %copy-done.1, ...), custom_call_target="tpu_custom_call" | custom-call | tf_op jit(solution)/shard_map/pallas_call | solution.py:142
  144.3 2.6 %collective-permute-start.14 = (bf16[16,96,256]{2,1,0:T(8,128)(2,1)S(1)}, bf16[16,96,256]{2,1,0:T(8,128)(2,1)S(1)}, u32[]{:S(2)}, u32[]{:S(2)}) collective-permute-start(bf16[16,96,256]{2,1,0:T(8,128)(2,1)S(1)} %get-tuple-element.34), channel_id=1, source_target_pairs={{0,16},{16,0},{1,17},{17,1},{2,18},{18,2},{3,19},{19,3},{4,20},{20... | collective-permute-start | bytes 2359304 | tf_op jit(solution)/shard_map/ppermute | solution.py:177
  146.9 1.9 %collective-permute-done.14 = bf16[16,96,256]{2,1,0:T(8,128)(2,1)S(1)} collective-permute-done((bf16[16,96,256]{2,1,0:T(8,128)(2,1)S(1)}, bf16[16,96,256]{2,1,0:T(8,128)(2,1)S(1)}, u32[]{:S(2)}, u32[]{:S(2)}) %collective-permute-start.14) | collective-permute-done | bytes 786464 | tf_op jit(solution)/shard_map/ppermute | solution.py:177
  149.1 15.1 %all_to_all.23 = bf16[8,192,256]{2,1,0:T(8,128)(2,1)S(1)} all-to-all(bf16[8,192,256]{2,1,0:T(8,128)(2,1)S(1)} %bitcast.16), channel_id=1, replica_groups=mesh['z2'=2,'z1'=2,'x'=4,'core'=2,'y'=8,'zh'=2] {'x','z1'}, dimensions={0} | all-to-all | bytes 1572864 | tf_op jit(solution)/shard_map/all_to_all | solution.py:179
  164.2 2.8 %collective-permute-start.15 = (bf16[96,256]{1,0:T(8,128)(2,1)S(1)}, bf16[96,256]{1,0:T(8,128)(2,1)S(1)}, u32[]{:S(2)}, u32[]{:S(2)}) collective-permute-start(bf16[96,256]{1,0:T(8,128)(2,1)S(1)} %get-tuple-element.36), channel_id=1, source_target_pairs={{0,256},{256,0},{1,257},{257,1},{2,258},{258,2},{3,259},{259,3},{4... | collective-permute-start | bytes 147464 | tf_op jit(solution)/shard_map/ppermute | solution.py:237
  167.1 3.4 %collective-permute-done.15 = bf16[96,256]{1,0:T(8,128)(2,1)S(1)} collective-permute-done((bf16[96,256]{1,0:T(8,128)(2,1)S(1)}, bf16[96,256]{1,0:T(8,128)(2,1)S(1)}, u32[]{:S(2)}, u32[]{:S(2)}) %collective-permute-start.15) | collective-permute-done | bytes 49184 | tf_op jit(solution)/shard_map/ppermute | solution.py:237
  (31 shorter events, 4.2 us)
Async XLA Ops:
  6.5 61.9 %all-gather.5.cloned.1.call-start = ((), (), s32[]{:S(2)}) async-start(), calls=%async_computation.4 | async-start | bytes 1769472 | tf_op jit(solution)/shard_map/all_gather | solution.py:191
  6.5 25.5 %collective-permute-start.3 = (bf16[192,256]{1,0:T(8,128)(2,1)}, bf16[192,256]{1,0:T(8,128)(2,1)S(1)}, u32[]{:S(2)}, u32[]{:S(2)}) collective-permute-start(bf16[192,256]{1,0:T(8,128)(2,1)} %bitcast.21), channel_id=1, source_target_pairs={{0,1},{1,0},{2,3},{3,2},{4,5},{5,4},{6,7},{7,6},{8,9},{9,8},{10,11... | collective-permute-start | bytes 294920 | tf_op jit(solution)/shard_map/ppermute | solution.py:205
  18.0 9.3 %collective-permute-start.1 = (bf16[96,256]{1,0:T(8,128)(2,1)}, bf16[96,256]{1,0:T(8,128)(2,1)S(1)}, u32[]{:S(2)}, u32[]{:S(2)}) collective-permute-start(bf16[96,256]{1,0:T(8,128)(2,1)} %param.9), channel_id=1, source_target_pairs={{0,256},{128,384},{256,0},{384,128},{1,257},{129,385},{257,1},{385... | collective-permute-start | bytes 147464 | tf_op jit(solution)/shard_map/ppermute | solution.py:187
  22.0 5.3 %collective-permute-start = (bf16[96,256]{1,0:T(8,128)(2,1)}, bf16[96,256]{1,0:T(8,128)(2,1)S(1)}, u32[]{:S(2)}, u32[]{:S(2)}) collective-permute-start(bf16[96,256]{1,0:T(8,128)(2,1)} %param.9), channel_id=1, source_target_pairs={{0,128},{128,0},{256,384},{384,256},{1,129},{129,1},{257,385},{385... | collective-permute-start | bytes 147464 | tf_op jit(solution)/shard_map/ppermute | solution.py:187
  25.1 6.9 %collective-permute-start.2 = (bf16[96,256]{1,0:T(8,128)(2,1)}, bf16[96,256]{1,0:T(8,128)(2,1)S(1)}, u32[]{:S(2)}, u32[]{:S(2)}) collective-permute-start(bf16[96,256]{1,0:T(8,128)(2,1)} %param.9), channel_id=1, source_target_pairs={{0,384},{128,256},{256,128},{384,0},{1,385},{129,257},{257,129},{3... | collective-permute-start | bytes 147464 | tf_op jit(solution)/shard_map/ppermute | solution.py:187
  33.5 105.5 %all-gather.7.cloned.1.call-start = ((), (), s32[]{:S(2)}) async-start(), calls=%async_computation.5 | async-start | bytes 1769472 | tf_op jit(solution)/shard_map/all_gather | solution.py:191
  34.5 14.4 %collective-permute-start.7 = (bf16[384,256]{1,0:T(8,128)(2,1)S(1)}, bf16[384,256]{1,0:T(8,128)(2,1)S(1)}, u32[]{:S(2)}, u32[]{:S(2)}) collective-permute-start(bf16[384,256]{1,0:T(8,128)(2,1)S(1)} %pad_maximum_fusion.1.refs_0_), channel_id=1, source_target_pairs={{0,12},{2,14},{4,0},{6,2},{8,4},{10,6},{12,8},{14,10},{1,13},{3,15... | collective-permute-start | bytes 589832 | tf_op jit(solution)/shard_map/ppermute | solution.py:159
  40.4 13.1 %collective-permute-start.6 = (bf16[384,256]{1,0:T(8,128)(2,1)S(1)}, bf16[384,256]{1,0:T(8,128)(2,1)S(1)}, u32[]{:S(2)}, u32[]{:S(2)}) collective-permute-start(bf16[384,256]{1,0:T(8,128)(2,1)S(1)} %pad_maximum_fusion.1.refs_0_), channel_id=1, source_target_pairs={{0,4},{2,6},{4,8},{6,10},{8,12},{10,14},{12,0},{14,2},{1,5},{3,7},... | collective-permute-start | bytes 589832 | tf_op jit(solution)/shard_map/ppermute | solution.py:159
  42.3 16.6 %collective-permute-start.5 = (bf16[384,256]{1,0:T(8,128)(2,1)S(1)}, bf16[384,256]{1,0:T(8,128)(2,1)S(1)}, u32[]{:S(2)}, u32[]{:S(2)}) collective-permute-start(bf16[384,256]{1,0:T(8,128)(2,1)S(1)} %pad_maximum_fusion.1.refs_0_), channel_id=1, source_target_pairs={{0,14},{2,0},{4,2},{6,4},{8,6},{10,8},{12,10},{14,12},{1,15},{3,1}... | collective-permute-start | bytes 589832 | tf_op jit(solution)/shard_map/ppermute | solution.py:159
  47.0 11.9 %collective-permute-start.4 = (bf16[384,256]{1,0:T(8,128)(2,1)S(1)}, bf16[384,256]{1,0:T(8,128)(2,1)S(1)}, u32[]{:S(2)}, u32[]{:S(2)}) collective-permute-start(bf16[384,256]{1,0:T(8,128)(2,1)S(1)} %pad_maximum_fusion.1.refs_0_), channel_id=1, source_target_pairs={{0,2},{2,4},{4,6},{6,8},{8,10},{10,12},{12,14},{14,0},{1,3},{3,5},... | collective-permute-start | bytes 589832 | tf_op jit(solution)/shard_map/ppermute | solution.py:159
  49.0 10.0 %collective-permute-start.9 = (bf16[384,256]{1,0:T(8,128)(2,1)S(1)}, bf16[384,256]{1,0:T(8,128)(2,1)S(1)}, u32[]{:S(2)}, u32[]{:S(2)}) collective-permute-start(bf16[384,256]{1,0:T(8,128)(2,1)S(1)} %collective-permute-done.7.refs_4_), channel_id=1, source_target_pairs={{0,14},{2,0},{4,2},{6,4},{8,6},{10,8},{12,10},{14,12},{1,15},{3,1}... | collective-permute-start | bytes 589832 | tf_op jit(solution)/shard_map/ppermute | solution.py:159
  53.5 10.6 %collective-permute-start.10 = (bf16[384,256]{1,0:T(8,128)(2,1)S(1)}, bf16[384,256]{1,0:T(8,128)(2,1)S(1)}, u32[]{:S(2)}, u32[]{:S(2)}) collective-permute-start(bf16[384,256]{1,0:T(8,128)(2,1)S(1)} %collective-permute-done.6.refs_3_), channel_id=1, source_target_pairs={{0,4},{2,6},{4,8},{6,10},{8,12},{10,14},{12,0},{14,2},{1,5},{3,7},... | collective-permute-start | bytes 589832 | tf_op jit(solution)/shard_map/ppermute | solution.py:159
  55.5 12.9 %collective-permute-start.8 = (bf16[384,256]{1,0:T(8,128)(2,1)S(1)}, bf16[384,256]{1,0:T(8,128)(2,1)S(1)}, u32[]{:S(2)}, u32[]{:S(2)}) collective-permute-start(bf16[384,256]{1,0:T(8,128)(2,1)S(1)} %collective-permute-done.6.refs_3_), channel_id=1, source_target_pairs={{0,2},{2,4},{4,6},{6,8},{8,10},{10,12},{12,14},{14,0},{1,3},{3,5},... | collective-permute-start | bytes 589832 | tf_op jit(solution)/shard_map/ppermute | solution.py:159
  73.3 23.7 %copy-start = (bf16[2,4,2,2,96,256]{5,4,3,2,1,0:T(8,128)(2,1)}, bf16[2,4,2,2,96,256]{5,4,3,2,1,0:T(8,128)(2,1)S(1)}, u32[]{:S(2)}) copy-start(bf16[2,4,2,2,96,256]{5,4,3,2,1,0:T(8,128)(2,1)S(1)} %get-tuple-element.32.refs_4_) | copy-start | bytes 4718596
  73.3 7.4 %collective-permute-start.11 = (bf16[16,96,256]{2,1,0:T(8,128)(2,1)S(1)}, bf16[16,96,256]{2,1,0:T(8,128)(2,1)S(1)}, u32[]{:S(2)}, u32[]{:S(2)}) collective-permute-start(bf16[16,96,256]{2,1,0:T(8,128)(2,1)S(1)} %get-tuple-element.27), channel_id=1, source_target_pairs={{0,16},{16,0},{1,17},{17,1},{2,18},{18,2},{3,19},{19,3},{4,20},{20... | collective-permute-start | bytes 2359304 | tf_op jit(solution)/shard_map/ppermute | solution.py:177
  81.0 58.1 %copy-start.1 = (bf16[256,3072]{1,0:T(8,128)(2,1)S(1)}, bf16[256,3072]{1,0:T(8,128)(2,1)}, u32[]{:S(2)}) copy-start(bf16[256,3072]{1,0:T(8,128)(2,1)} %get-tuple-element.31.refs_3_) | copy-start | bytes 4718596
  97.1 7.3 %collective-permute-start.12 = (bf16[192,256]{1,0:T(8,128)(2,1)S(1)}, bf16[192,256]{1,0:T(8,128)(2,1)S(1)}, u32[]{:S(2)}, u32[]{:S(2)}) collective-permute-start(bf16[192,256]{1,0:T(8,128)(2,1)S(1)} %shard_map.56), channel_id=1, source_target_pairs={{0,256},{256,0},{1,257},{257,1},{2,258},{258,2},{3,259},{259,3},{4... | collective-permute-start | bytes 294920 | tf_op jit(solution)/shard_map/ppermute | solution.py:222
  104.4 5.4 %collective-permute-start.13 = (bf16[192,256]{1,0:T(8,128)(2,1)S(1)}, bf16[192,256]{1,0:T(8,128)(2,1)S(1)}, u32[]{:S(2)}, u32[]{:S(2)}) collective-permute-start(bf16[192,256]{1,0:T(8,128)(2,1)S(1)} %add_convert_fusion.2.mine_ref), channel_id=1, source_target_pairs={{0,128},{128,0},{1,129},{129,1},{2,130},{130,2},{3,131},{131,3},{4... | collective-permute-start | bytes 294920 | tf_op jit(solution)/shard_map/ppermute | solution.py:223
  139.1 1.4 copy-start.2
  144.3 4.5 %collective-permute-start.14 = (bf16[16,96,256]{2,1,0:T(8,128)(2,1)S(1)}, bf16[16,96,256]{2,1,0:T(8,128)(2,1)S(1)}, u32[]{:S(2)}, u32[]{:S(2)}) collective-permute-start(bf16[16,96,256]{2,1,0:T(8,128)(2,1)S(1)} %get-tuple-element.34), channel_id=1, source_target_pairs={{0,16},{16,0},{1,17},{17,1},{2,18},{18,2},{3,19},{19,3},{4,20},{20... | collective-permute-start | bytes 2359304 | tf_op jit(solution)/shard_map/ppermute | solution.py:177
  164.2 6.3 %collective-permute-start.15 = (bf16[96,256]{1,0:T(8,128)(2,1)S(1)}, bf16[96,256]{1,0:T(8,128)(2,1)S(1)}, u32[]{:S(2)}, u32[]{:S(2)}) collective-permute-start(bf16[96,256]{1,0:T(8,128)(2,1)S(1)} %get-tuple-element.36), channel_id=1, source_target_pairs={{0,256},{256,0},{1,257},{257,1},{2,258},{258,2},{3,259},{259,3},{4... | collective-permute-start | bytes 147464 | tf_op jit(solution)/shard_map/ppermute | solution.py:237
Sparse Core Ops, SparseCore 0:
  33.7 28.3 all-gather.4
  110.7 26.3 all-gather.6

commit v7 on v6

--- a/solution.py
+++ b/solution.py
@@ -14,7 +14,7 @@
 BF16 = jnp.bfloat16
 AXES = ("z2", "z1", "x", "core", "y", "zh")
 SIZES = (2, 2, 4, 2, 8, 2)
-STEPS = (0, -1, 1, -2, 2, -3, 3, -4)
+STEPS = (0, -1, 1, -2, 2, -3, 3, 4)
 
 
 def mm(a, b, dims=((1,), (0,))):
@@ -165,8 +165,8 @@
 
 def gather_tokens(block):
     back1, ahead1, back2, ahead2 = turn(block, 1), turn(block, 7), turn(block, 2), turn(block, 6)
-    back3, ahead3, back4 = turn(back2, 1), turn(ahead2, 7), turn(back2, 2)
-    return block, back1, ahead1, back2, ahead2, back3, ahead3, back4
+    back3, ahead3, ahead4 = turn(back2, 1), turn(ahead2, 7), turn(ahead2, 6)
+    return block, back1, ahead1, back2, ahead2, back3, ahead3, ahead4
 
 
 def add(a, b):

time: 179 us -> 176 us (0.983)
  waiting for transfers between devices: 30 us -> 27 us
    ppermute x7, waiting for transfers between devices: 9.47 us -> 5.8 us  [turn(): return lax.ppermute(value, 'y', [(i, (i + step) % 8) for i in range(8)])]
  transfers between devices with their start and end apart: 18 -> 18, of which waited for: 8 -> 7; matrix products, arithmetic and copies ran while one was open for 1% -> 1% of each run, Pallas kernels for 0% -> 0%
where the time goes in v7:
time: 176 us; the launch traced here: 175 us
  blocking collectives  59.9 us (34%)
  starting transfers between devices  58.5 us (33%)
  waiting for transfers between devices  27 us (15%)
  between operations  13.7 us (8%)
  Pallas kernels  9.64 us (5%)
  other arithmetic  4.66 us (3%)
    all_to_all x2, blocking collectives, scatter_parts(): return lax.all_to_all(pieces, ('x', 'z1'), 0, 0, tiled=True)  31 us
    all_to_all x2, blocking collectives, everywhere(): lax.all_to_all(jnp.broadcast_to(value, (size, *value.shape)), axes, 0, 0,...  28.9 us
    ppermute x7, starting transfers between devices, turn(): return lax.ppermute(value, 'y', [(i, (i + step) % 8) for i in range(8)])  24.4 us
    ppermute x1, starting transfers between devices, shards(): other = lax.ppermute(tok, 'zh', swap(2, 1))  11.5 us
    pallas_call x5, Pallas kernels, run(): pl.pallas_call(kernel, out_shape=[jax.ShapeDtypeStruct(s, d) for s, d in...  9.64 us
    ppermute x3, starting transfers between devices, along_z(): lax.ppermute(block, ('z2', 'z1'), swap(4, k))  9.27 us
    ppermute x2, starting transfers between devices, scatter_parts(): both = add(keep, lax.ppermute(send, 'core', swap(2, 1)))  7.13 us
    ppermute x7, waiting for transfers between devices, turn(): return lax.ppermute(value, 'y', [(i, (i + step) % 8) for i in range(8)])  5.8 us
  transfers between devices with their start and end apart: 18, of which 7 were waited for; matrix products, arithmetic and copies ran while one was open for 1% of the time, Pallas kernels for 0%

profile of v7, /device:TPU:1, one launch (start us, length us, event | category | flops | bytes accessed | tf_op | source)
XLA Modules:
  0.0 174.8 jit_solution(17451692519851623142)
XLA Ops:
  6.5 11.5 %collective-permute-start.3 = (bf16[192,256]{1,0:T(8,128)(2,1)}, bf16[192,256]{1,0:T(8,128)(2,1)S(1)}, u32[]{:S(2)}, u32[]{:S(2)}) collective-permute-start(bf16[192,256]{1,0:T(8,128)(2,1)} %bitcast.21), channel_id=1, source_target_pairs={{0,1},{1,0},{2,3},{3,2},{4,5},{5,4},{6,7},{7,6},{8,9},{9,8},{10,11... | collective-permute-start | bytes 294920 | tf_op jit(solution)/shard_map/ppermute | solution.py:205
  18.0 4.0 %collective-permute-start.1 = (bf16[96,256]{1,0:T(8,128)(2,1)}, bf16[96,256]{1,0:T(8,128)(2,1)S(1)}, u32[]{:S(2)}, u32[]{:S(2)}) collective-permute-start(bf16[96,256]{1,0:T(8,128)(2,1)} %param.9), channel_id=1, source_target_pairs={{0,256},{128,384},{256,0},{384,128},{1,257},{129,385},{257,1},{385... | collective-permute-start | bytes 147464 | tf_op jit(solution)/shard_map/ppermute | solution.py:187
  22.0 3.1 %collective-permute-start = (bf16[96,256]{1,0:T(8,128)(2,1)}, bf16[96,256]{1,0:T(8,128)(2,1)S(1)}, u32[]{:S(2)}, u32[]{:S(2)}) collective-permute-start(bf16[96,256]{1,0:T(8,128)(2,1)} %param.9), channel_id=1, source_target_pairs={{0,128},{128,0},{256,384},{384,256},{1,129},{129,1},{257,385},{385... | collective-permute-start | bytes 147464 | tf_op jit(solution)/shard_map/ppermute | solution.py:187
  25.1 2.2 %collective-permute-start.2 = (bf16[96,256]{1,0:T(8,128)(2,1)}, bf16[96,256]{1,0:T(8,128)(2,1)S(1)}, u32[]{:S(2)}, u32[]{:S(2)}) collective-permute-start(bf16[96,256]{1,0:T(8,128)(2,1)} %param.9), channel_id=1, source_target_pairs={{0,384},{128,256},{256,128},{384,0},{1,385},{129,257},{257,129},{3... | collective-permute-start | bytes 147464 | tf_op jit(solution)/shard_map/ppermute | solution.py:187
  27.3 4.7 %collective-permute-done.2 = bf16[96,256]{1,0:T(8,128)(2,1)S(1)} collective-permute-done((bf16[96,256]{1,0:T(8,128)(2,1)}, bf16[96,256]{1,0:T(8,128)(2,1)S(1)}, u32[]{:S(2)}, u32[]{:S(2)}) %collective-permute-start.2) | collective-permute-done | bytes 49184 | tf_op jit(solution)/shard_map/ppermute | solution.py:187
  32.0 1.5 pad_maximum_fusion.2
  34.5 5.9 %collective-permute-start.7 = (bf16[384,256]{1,0:T(8,128)(2,1)S(1)}, bf16[384,256]{1,0:T(8,128)(2,1)S(1)}, u32[]{:S(2)}, u32[]{:S(2)}) collective-permute-start(bf16[384,256]{1,0:T(8,128)(2,1)S(1)} %pad_maximum_fusion.1.refs_0_), channel_id=1, source_target_pairs={{0,12},{2,14},{4,0},{6,2},{8,4},{10,6},{12,8},{14,10},{1,13},{3,15... | collective-permute-start | bytes 589832 | tf_op jit(solution)/shard_map/ppermute | solution.py:159
  40.4 1.9 %collective-permute-start.6 = (bf16[384,256]{1,0:T(8,128)(2,1)S(1)}, bf16[384,256]{1,0:T(8,128)(2,1)S(1)}, u32[]{:S(2)}, u32[]{:S(2)}) collective-permute-start(bf16[384,256]{1,0:T(8,128)(2,1)S(1)} %pad_maximum_fusion.1.refs_0_), channel_id=1, source_target_pairs={{0,4},{2,6},{4,8},{6,10},{8,12},{10,14},{12,0},{14,2},{1,5},{3,7},... | collective-permute-start | bytes 589832 | tf_op jit(solution)/shard_map/ppermute | solution.py:159
  42.3 4.7 %collective-permute-start.5 = (bf16[384,256]{1,0:T(8,128)(2,1)S(1)}, bf16[384,256]{1,0:T(8,128)(2,1)S(1)}, u32[]{:S(2)}, u32[]{:S(2)}) collective-permute-start(bf16[384,256]{1,0:T(8,128)(2,1)S(1)} %pad_maximum_fusion.1.refs_0_), channel_id=1, source_target_pairs={{0,14},{2,0},{4,2},{6,4},{8,6},{10,8},{12,10},{14,12},{1,15},{3,1}... | collective-permute-start | bytes 589832 | tf_op jit(solution)/shard_map/ppermute | solution.py:159
  47.0 1.9 %collective-permute-start.4 = (bf16[384,256]{1,0:T(8,128)(2,1)S(1)}, bf16[384,256]{1,0:T(8,128)(2,1)S(1)}, u32[]{:S(2)}, u32[]{:S(2)}) collective-permute-start(bf16[384,256]{1,0:T(8,128)(2,1)S(1)} %pad_maximum_fusion.1.refs_0_), channel_id=1, source_target_pairs={{0,2},{2,4},{4,6},{6,8},{8,10},{10,12},{12,14},{14,0},{1,3},{3,5},... | collective-permute-start | bytes 589832 | tf_op jit(solution)/shard_map/ppermute | solution.py:159
  49.0 4.7 %collective-permute-start.10 = (bf16[384,256]{1,0:T(8,128)(2,1)S(1)}, bf16[384,256]{1,0:T(8,128)(2,1)S(1)}, u32[]{:S(2)}, u32[]{:S(2)}) collective-permute-start(bf16[384,256]{1,0:T(8,128)(2,1)S(1)} %collective-permute-done.7.refs_4_), channel_id=1, source_target_pairs={{0,12},{2,14},{4,0},{6,2},{8,4},{10,6},{12,8},{14,10},{1,13},{3,15... | collective-permute-start | bytes 589832 | tf_op jit(solution)/shard_map/ppermute | solution.py:159
  53.6 1.9 %collective-permute-start.9 = (bf16[384,256]{1,0:T(8,128)(2,1)S(1)}, bf16[384,256]{1,0:T(8,128)(2,1)S(1)}, u32[]{:S(2)}, u32[]{:S(2)}) collective-permute-start(bf16[384,256]{1,0:T(8,128)(2,1)S(1)} %collective-permute-done.7.refs_4_), channel_id=1, source_target_pairs={{0,14},{2,0},{4,2},{6,4},{8,6},{10,8},{12,10},{14,12},{1,15},{3,1}... | collective-permute-start | bytes 589832 | tf_op jit(solution)/shard_map/ppermute | solution.py:159
  55.6 3.4 %collective-permute-start.8 = (bf16[384,256]{1,0:T(8,128)(2,1)S(1)}, bf16[384,256]{1,0:T(8,128)(2,1)S(1)}, u32[]{:S(2)}, u32[]{:S(2)}) collective-permute-start(bf16[384,256]{1,0:T(8,128)(2,1)S(1)} %collective-permute-done.6.refs_3_), channel_id=1, source_target_pairs={{0,2},{2,4},{4,6},{6,8},{8,10},{10,12},{12,14},{14,0},{1,3},{3,5},... | collective-permute-start | bytes 589832 | tf_op jit(solution)/shard_map/ppermute | solution.py:159
  58.9 1.1 pad_maximum_fusion.refs_9_.refs_5_
  60.1 5.8 %collective-permute-done.9.refs_6_ = bf16[384,256]{1,0:T(8,128)(2,1)S(1)} collective-permute-done((bf16[384,256]{1,0:T(8,128)(2,1)S(1)}, bf16[384,256]{1,0:T(8,128)(2,1)S(1)}, u32[]{:S(2)}, u32[]{:S(2)}) %collective-permute-start.9) | collective-permute-done | bytes 196640 | tf_op jit(solution)/shard_map/ppermute | solution.py:159
  65.9 4.9 %shard_map.55 = (bf16[2,4,2,2,96,256]{5,4,3,2,1,0:T(8,128)(2,1)S(1)}, bf16[256,3072]{1,0:T(8,128)(2,1)}, f32[256,256]{1,0:T(8,128)S(1)}, bf16[16,96,256]{2,1,0:T(8,128)(2,1)S(1)}, bf16[16,96,256]{2,1,0:T(8,128)(2,1)S(1)}) custom-call(bf16[384,256]{1,0:T(8,128)(2,1)S(1)} %pad_maximum_fusion.1.refs_0_, bf16[384,256]{1,0:T(8,128)(2,1)S(1)} %collective-permute-done.4.refs_1_, ...), custom_call_target="tpu_custom_call" | custom-call | tf_op jit(solution)/shard_map/pallas_call | solution.py:142
  70.8 4.5 %collective-permute-start.11 = (bf16[16,96,256]{2,1,0:T(8,128)(2,1)S(1)}, bf16[16,96,256]{2,1,0:T(8,128)(2,1)S(1)}, u32[]{:S(2)}, u32[]{:S(2)}) collective-permute-start(bf16[16,96,256]{2,1,0:T(8,128)(2,1)S(1)} %get-tuple-element.27), channel_id=1, source_target_pairs={{0,16},{16,0},{1,17},{17,1},{2,18},{18,2},{3,19},{19,3},{4,20},{20... | collective-permute-start | bytes 2359304 | tf_op jit(solution)/shard_map/ppermute | solution.py:177
  75.3 1.9 %collective-permute-done.11 = bf16[16,96,256]{2,1,0:T(8,128)(2,1)S(1)} collective-permute-done((bf16[16,96,256]{2,1,0:T(8,128)(2,1)S(1)}, bf16[16,96,256]{2,1,0:T(8,128)(2,1)S(1)}, u32[]{:S(2)}, u32[]{:S(2)}) %collective-permute-start.11) | collective-permute-done | bytes 786464 | tf_op jit(solution)/shard_map/ppermute | solution.py:177
  77.4 16.0 %all_to_all.20.parts_ref = bf16[8,192,256]{2,1,0:T(8,128)(2,1)S(1)} all-to-all(bf16[8,192,256]{2,1,0:T(8,128)(2,1)S(1)} %bitcast.15), channel_id=1, replica_groups=mesh['z2'=2,'z1'=2,'x'=4,'core'=2,'y'=8,'zh'=2] {'x','z1'}, dimensions={0} | all-to-all | bytes 1572864 | tf_op jit(solution)/shard_map/all_to_all | solution.py:179
  93.5 2.2 %collective-permute-start.12 = (bf16[192,256]{1,0:T(8,128)(2,1)S(1)}, bf16[192,256]{1,0:T(8,128)(2,1)S(1)}, u32[]{:S(2)}, u32[]{:S(2)}) collective-permute-start(bf16[192,256]{1,0:T(8,128)(2,1)S(1)} %shard_map.56), channel_id=1, source_target_pairs={{0,256},{256,0},{1,257},{257,1},{2,258},{258,2},{3,259},{259,3},{4... | collective-permute-start | bytes 294920 | tf_op jit(solution)/shard_map/ppermute | solution.py:222
  95.7 5.1 %collective-permute-done.12 = bf16[192,256]{1,0:T(8,128)(2,1)S(1)} collective-permute-done((bf16[192,256]{1,0:T(8,128)(2,1)S(1)}, bf16[192,256]{1,0:T(8,128)(2,1)S(1)}, u32[]{:S(2)}, u32[]{:S(2)}) %collective-permute-start.12) | collective-permute-done | bytes 98336 | tf_op jit(solution)/shard_map/ppermute | solution.py:222
  100.9 1.9 %collective-permute-start.13 = (bf16[192,256]{1,0:T(8,128)(2,1)S(1)}, bf16[192,256]{1,0:T(8,128)(2,1)S(1)}, u32[]{:S(2)}, u32[]{:S(2)}) collective-permute-start(bf16[192,256]{1,0:T(8,128)(2,1)S(1)} %add_convert_fusion.2.mine_ref), channel_id=1, source_target_pairs={{0,128},{128,0},{1,129},{129,1},{2,130},{130,2},{3,131},{131,3},{4... | collective-permute-start | bytes 294920 | tf_op jit(solution)/shard_map/ppermute | solution.py:223
  102.8 3.4 %collective-permute-done.13.theirs_ref = bf16[192,256]{1,0:T(8,128)(2,1)S(1)} collective-permute-done((bf16[192,256]{1,0:T(8,128)(2,1)S(1)}, bf16[192,256]{1,0:T(8,128)(2,1)S(1)}, u32[]{:S(2)}, u32[]{:S(2)}) %collective-permute-start.13) | collective-permute-done | bytes 98336 | tf_op jit(solution)/shard_map/ppermute | solution.py:223
  107.0 16.4 %all_to_all.21 = f32[16,8,128]{2,1,0:T(8,128)S(1)} all-to-all(f32[16,8,128]{2,1,0:T(8,128)S(1)} %broadcast_in_dim.6), channel_id=1, replica_groups=mesh['z2'=2,'z1'=2,'x'=4,'core'=2,'y'=8,'zh'=2] {'zh','y'}, dimensions={0} | all-to-all | bytes 131072 | tf_op jit(solution)/shard_map/all_to_all | solution.py:183
  123.4 12.5 %all_to_all.22.refs_0_ = f32[8,8,128]{2,1,0:T(8,128)S(1)} all-to-all(f32[8,8,128]{2,1,0:T(8,128)S(1)} %broadcast_in_dim.7), channel_id=1, replica_groups=mesh['z2'=2,'z1'=2,'x'=4,'core'=2,'y'=8,'zh'=2] {'x','core'}, dimensions={0} | all-to-all | bytes 65536 | tf_op jit(solution)/shard_map/all_to_all | solution.py:183
  135.9 1.4 copy-done.2
  137.3 3.8 %shard_map.58 = (bf16[16,96,256]{2,1,0:T(8,128)(2,1)S(1)}, bf16[16,96,256]{2,1,0:T(8,128)(2,1)S(1)}) custom-call(f32[8,8,128]{2,1,0:T(8,128)S(1)} %all_to_all.22.refs_0_, f32[256,256]{1,0:T(8,128)S(1)} %get-tuple-element.29.refs_1_, bf16[8,2,192,256]{3,2,1,0:T(8,128)(2,1)S(1)} %bitcast.14, bf16[256,3072]{1,0:T(8,128)(2,1)S(1)} %copy-done.1, ...), custom_call_target="tpu_custom_call" | custom-call | tf_op jit(solution)/shard_map/pallas_call | solution.py:142
  141.1 2.6 %collective-permute-start.14 = (bf16[16,96,256]{2,1,0:T(8,128)(2,1)S(1)}, bf16[16,96,256]{2,1,0:T(8,128)(2,1)S(1)}, u32[]{:S(2)}, u32[]{:S(2)}) collective-permute-start(bf16[16,96,256]{2,1,0:T(8,128)(2,1)S(1)} %get-tuple-element.34), channel_id=1, source_target_pairs={{0,16},{16,0},{1,17},{17,1},{2,18},{18,2},{3,19},{19,3},{4,20},{20... | collective-permute-start | bytes 2359304 | tf_op jit(solution)/shard_map/ppermute | solution.py:177
  143.8 1.9 %collective-permute-done.14 = bf16[16,96,256]{2,1,0:T(8,128)(2,1)S(1)} collective-permute-done((bf16[16,96,256]{2,1,0:T(8,128)(2,1)S(1)}, bf16[16,96,256]{2,1,0:T(8,128)(2,1)S(1)}, u32[]{:S(2)}, u32[]{:S(2)}) %collective-permute-start.14) | collective-permute-done | bytes 786464 | tf_op jit(solution)/shard_map/ppermute | solution.py:177
  145.9 15.1 %all_to_all.23 = bf16[8,192,256]{2,1,0:T(8,128)(2,1)S(1)} all-to-all(bf16[8,192,256]{2,1,0:T(8,128)(2,1)S(1)} %bitcast.16), channel_id=1, replica_groups=mesh['z2'=2,'z1'=2,'x'=4,'core'=2,'y'=8,'zh'=2] {'x','z1'}, dimensions={0} | all-to-all | bytes 1572864 | tf_op jit(solution)/shard_map/all_to_all | solution.py:179
  161.1 2.2 %collective-permute-start.15 = (bf16[96,256]{1,0:T(8,128)(2,1)S(1)}, bf16[96,256]{1,0:T(8,128)(2,1)S(1)}, u32[]{:S(2)}, u32[]{:S(2)}) collective-permute-start(bf16[96,256]{1,0:T(8,128)(2,1)S(1)} %get-tuple-element.36), channel_id=1, source_target_pairs={{0,256},{256,0},{1,257},{257,1},{2,258},{258,2},{3,259},{259,3},{4... | collective-permute-start | bytes 147464 | tf_op jit(solution)/shard_map/ppermute | solution.py:237
  163.2 4.1 %collective-permute-done.15 = bf16[96,256]{1,0:T(8,128)(2,1)S(1)} collective-permute-done((bf16[96,256]{1,0:T(8,128)(2,1)S(1)}, bf16[96,256]{1,0:T(8,128)(2,1)S(1)}, u32[]{:S(2)}, u32[]{:S(2)}) %collective-permute-start.15) | collective-permute-done | bytes 49184 | tf_op jit(solution)/shard_map/ppermute | solution.py:237
  (31 shorter events, 3.1 us)
Async XLA Ops:
  6.5 59.3 %all-gather.5.cloned.1.call-start = ((), (), s32[]{:S(2)}) async-start(), calls=%async_computation.4 | async-start | bytes 1769472 | tf_op jit(solution)/shard_map/all_gather | solution.py:191
  6.5 25.5 %collective-permute-start.3 = (bf16[192,256]{1,0:T(8,128)(2,1)}, bf16[192,256]{1,0:T(8,128)(2,1)S(1)}, u32[]{:S(2)}, u32[]{:S(2)}) collective-permute-start(bf16[192,256]{1,0:T(8,128)(2,1)} %bitcast.21), channel_id=1, source_target_pairs={{0,1},{1,0},{2,3},{3,2},{4,5},{5,4},{6,7},{7,6},{8,9},{9,8},{10,11... | collective-permute-start | bytes 294920 | tf_op jit(solution)/shard_map/ppermute | solution.py:205
  18.0 9.3 %collective-permute-start.1 = (bf16[96,256]{1,0:T(8,128)(2,1)}, bf16[96,256]{1,0:T(8,128)(2,1)S(1)}, u32[]{:S(2)}, u32[]{:S(2)}) collective-permute-start(bf16[96,256]{1,0:T(8,128)(2,1)} %param.9), channel_id=1, source_target_pairs={{0,256},{128,384},{256,0},{384,128},{1,257},{129,385},{257,1},{385... | collective-permute-start | bytes 147464 | tf_op jit(solution)/shard_map/ppermute | solution.py:187
  22.0 5.3 %collective-permute-start = (bf16[96,256]{1,0:T(8,128)(2,1)}, bf16[96,256]{1,0:T(8,128)(2,1)S(1)}, u32[]{:S(2)}, u32[]{:S(2)}) collective-permute-start(bf16[96,256]{1,0:T(8,128)(2,1)} %param.9), channel_id=1, source_target_pairs={{0,128},{128,0},{256,384},{384,256},{1,129},{129,1},{257,385},{385... | collective-permute-start | bytes 147464 | tf_op jit(solution)/shard_map/ppermute | solution.py:187
  25.1 6.9 %collective-permute-start.2 = (bf16[96,256]{1,0:T(8,128)(2,1)}, bf16[96,256]{1,0:T(8,128)(2,1)S(1)}, u32[]{:S(2)}, u32[]{:S(2)}) collective-permute-start(bf16[96,256]{1,0:T(8,128)(2,1)} %param.9), channel_id=1, source_target_pairs={{0,384},{128,256},{256,128},{384,0},{1,385},{129,257},{257,129},{3... | collective-permute-start | bytes 147464 | tf_op jit(solution)/shard_map/ppermute | solution.py:187
  33.5 102.3 %all-gather.7.cloned.1.call-start = ((), (), s32[]{:S(2)}) async-start(), calls=%async_computation.5 | async-start | bytes 1769472 | tf_op jit(solution)/shard_map/all_gather | solution.py:191
  34.5 14.4 %collective-permute-start.7 = (bf16[384,256]{1,0:T(8,128)(2,1)S(1)}, bf16[384,256]{1,0:T(8,128)(2,1)S(1)}, u32[]{:S(2)}, u32[]{:S(2)}) collective-permute-start(bf16[384,256]{1,0:T(8,128)(2,1)S(1)} %pad_maximum_fusion.1.refs_0_), channel_id=1, source_target_pairs={{0,12},{2,14},{4,0},{6,2},{8,4},{10,6},{12,8},{14,10},{1,13},{3,15... | collective-permute-start | bytes 589832 | tf_op jit(solution)/shard_map/ppermute | solution.py:159
  40.4 15.2 %collective-permute-start.6 = (bf16[384,256]{1,0:T(8,128)(2,1)S(1)}, bf16[384,256]{1,0:T(8,128)(2,1)S(1)}, u32[]{:S(2)}, u32[]{:S(2)}) collective-permute-start(bf16[384,256]{1,0:T(8,128)(2,1)S(1)} %pad_maximum_fusion.1.refs_0_), channel_id=1, source_target_pairs={{0,4},{2,6},{4,8},{6,10},{8,12},{10,14},{12,0},{14,2},{1,5},{3,7},... | collective-permute-start | bytes 589832 | tf_op jit(solution)/shard_map/ppermute | solution.py:159
  42.3 17.7 %collective-permute-start.5 = (bf16[384,256]{1,0:T(8,128)(2,1)S(1)}, bf16[384,256]{1,0:T(8,128)(2,1)S(1)}, u32[]{:S(2)}, u32[]{:S(2)}) collective-permute-start(bf16[384,256]{1,0:T(8,128)(2,1)S(1)} %pad_maximum_fusion.1.refs_0_), channel_id=1, source_target_pairs={{0,14},{2,0},{4,2},{6,4},{8,6},{10,8},{12,10},{14,12},{1,15},{3,1}... | collective-permute-start | bytes 589832 | tf_op jit(solution)/shard_map/ppermute | solution.py:159
  47.0 13.0 %collective-permute-start.4 = (bf16[384,256]{1,0:T(8,128)(2,1)S(1)}, bf16[384,256]{1,0:T(8,128)(2,1)S(1)}, u32[]{:S(2)}, u32[]{:S(2)}) collective-permute-start(bf16[384,256]{1,0:T(8,128)(2,1)S(1)} %pad_maximum_fusion.1.refs_0_), channel_id=1, source_target_pairs={{0,2},{2,4},{4,6},{6,8},{8,10},{10,12},{12,14},{14,0},{1,3},{3,5},... | collective-permute-start | bytes 589832 | tf_op jit(solution)/shard_map/ppermute | solution.py:159
  49.0 11.1 %collective-permute-start.10 = (bf16[384,256]{1,0:T(8,128)(2,1)S(1)}, bf16[384,256]{1,0:T(8,128)(2,1)S(1)}, u32[]{:S(2)}, u32[]{:S(2)}) collective-permute-start(bf16[384,256]{1,0:T(8,128)(2,1)S(1)} %collective-permute-done.7.refs_4_), channel_id=1, source_target_pairs={{0,12},{2,14},{4,0},{6,2},{8,4},{10,6},{12,8},{14,10},{1,13},{3,15... | collective-permute-start | bytes 589832 | tf_op jit(solution)/shard_map/ppermute | solution.py:159
  53.6 12.2 %collective-permute-start.9 = (bf16[384,256]{1,0:T(8,128)(2,1)S(1)}, bf16[384,256]{1,0:T(8,128)(2,1)S(1)}, u32[]{:S(2)}, u32[]{:S(2)}) collective-permute-start(bf16[384,256]{1,0:T(8,128)(2,1)S(1)} %collective-permute-done.7.refs_4_), channel_id=1, source_target_pairs={{0,14},{2,0},{4,2},{6,4},{8,6},{10,8},{12,10},{14,12},{1,15},{3,1}... | collective-permute-start | bytes 589832 | tf_op jit(solution)/shard_map/ppermute | solution.py:159
  55.6 10.3 %collective-permute-start.8 = (bf16[384,256]{1,0:T(8,128)(2,1)S(1)}, bf16[384,256]{1,0:T(8,128)(2,1)S(1)}, u32[]{:S(2)}, u32[]{:S(2)}) collective-permute-start(bf16[384,256]{1,0:T(8,128)(2,1)S(1)} %collective-permute-done.6.refs_3_), channel_id=1, source_target_pairs={{0,2},{2,4},{4,6},{6,8},{8,10},{10,12},{12,14},{14,0},{1,3},{3,5},... | collective-permute-start | bytes 589832 | tf_op jit(solution)/shard_map/ppermute | solution.py:159
  70.8 22.6 %copy-start = (bf16[2,4,2,2,96,256]{5,4,3,2,1,0:T(8,128)(2,1)}, bf16[2,4,2,2,96,256]{5,4,3,2,1,0:T(8,128)(2,1)S(1)}, u32[]{:S(2)}) copy-start(bf16[2,4,2,2,96,256]{5,4,3,2,1,0:T(8,128)(2,1)S(1)} %get-tuple-element.32.refs_4_) | copy-start | bytes 4718596
  70.8 6.4 %collective-permute-start.11 = (bf16[16,96,256]{2,1,0:T(8,128)(2,1)S(1)}, bf16[16,96,256]{2,1,0:T(8,128)(2,1)S(1)}, u32[]{:S(2)}, u32[]{:S(2)}) collective-permute-start(bf16[16,96,256]{2,1,0:T(8,128)(2,1)S(1)} %get-tuple-element.27), channel_id=1, source_target_pairs={{0,16},{16,0},{1,17},{17,1},{2,18},{18,2},{3,19},{19,3},{4,20},{20... | collective-permute-start | bytes 2359304 | tf_op jit(solution)/shard_map/ppermute | solution.py:177
  77.4 58.5 %copy-start.1 = (bf16[256,3072]{1,0:T(8,128)(2,1)S(1)}, bf16[256,3072]{1,0:T(8,128)(2,1)}, u32[]{:S(2)}) copy-start(bf16[256,3072]{1,0:T(8,128)(2,1)} %get-tuple-element.31.refs_3_) | copy-start | bytes 4718596
  93.5 7.3 %collective-permute-start.12 = (bf16[192,256]{1,0:T(8,128)(2,1)S(1)}, bf16[192,256]{1,0:T(8,128)(2,1)S(1)}, u32[]{:S(2)}, u32[]{:S(2)}) collective-permute-start(bf16[192,256]{1,0:T(8,128)(2,1)S(1)} %shard_map.56), channel_id=1, source_target_pairs={{0,256},{256,0},{1,257},{257,1},{2,258},{258,2},{3,259},{259,3},{4... | collective-permute-start | bytes 294920 | tf_op jit(solution)/shard_map/ppermute | solution.py:222
  100.9 5.4 %collective-permute-start.13 = (bf16[192,256]{1,0:T(8,128)(2,1)S(1)}, bf16[192,256]{1,0:T(8,128)(2,1)S(1)}, u32[]{:S(2)}, u32[]{:S(2)}) collective-permute-start(bf16[192,256]{1,0:T(8,128)(2,1)S(1)} %add_convert_fusion.2.mine_ref), channel_id=1, source_target_pairs={{0,128},{128,0},{1,129},{129,1},{2,130},{130,2},{3,131},{131,3},{4... | collective-permute-start | bytes 294920 | tf_op jit(solution)/shard_map/ppermute | solution.py:223
  135.9 1.4 copy-start.2
  141.1 4.5 %collective-permute-start.14 = (bf16[16,96,256]{2,1,0:T(8,128)(2,1)S(1)}, bf16[16,96,256]{2,1,0:T(8,128)(2,1)S(1)}, u32[]{:S(2)}, u32[]{:S(2)}) collective-permute-start(bf16[16,96,256]{2,1,0:T(8,128)(2,1)S(1)} %get-tuple-element.34), channel_id=1, source_target_pairs={{0,16},{16,0},{1,17},{17,1},{2,18},{18,2},{3,19},{19,3},{4,20},{20... | collective-permute-start | bytes 2359304 | tf_op jit(solution)/shard_map/ppermute | solution.py:177
  161.1 6.3 %collective-permute-start.15 = (bf16[96,256]{1,0:T(8,128)(2,1)S(1)}, bf16[96,256]{1,0:T(8,128)(2,1)S(1)}, u32[]{:S(2)}, u32[]{:S(2)}) collective-permute-start(bf16[96,256]{1,0:T(8,128)(2,1)S(1)} %get-tuple-element.36), channel_id=1, source_target_pairs={{0,256},{256,0},{1,257},{257,1},{2,258},{258,2},{3,259},{259,3},{4... | collective-permute-start | bytes 147464 | tf_op jit(solution)/shard_map/ppermute | solution.py:237
Sparse Core Ops, SparseCore 0:
  33.7 28.3 all-gather.4
  107.1 26.2 all-gather.6

commit v8 on v7

--- a/solution.py
+++ b/solution.py
@@ -115,11 +115,12 @@
     give_ref[...] = jnp.sum(parts_ref[:, 1 - z2].astype(F32), 0).astype(BF16)
 
 
-def pair_kernel(mine_ref, theirs_ref, first_ref, square_ref):
+def pair_kernel(mine_ref, theirs_ref, mine_far_ref, theirs_far_ref, first_ref, square_ref):
     z1 = lax.axis_index("z1")
-    first_ref[z1] = mine_ref[...]
-    first_ref[1 - z1] = theirs_ref[...]
-    mine, theirs = mine_ref[...].astype(F32), theirs_ref[...].astype(F32)
+    mine = mine_ref[...].astype(F32) + mine_far_ref[...].astype(F32)
+    theirs = theirs_ref[...].astype(F32) + theirs_far_ref[...].astype(F32)
+    first_ref[z1] = mine.astype(BF16)
+    first_ref[1 - z1] = theirs.astype(BF16)
     square = jnp.sum((mine * mine + theirs * theirs).reshape(-1, 8, mine.shape[1]), 0)
     square_ref[...] = square[:, :HEAD] + square[:, HEAD:]
 
@@ -204,10 +205,10 @@
 
     other = lax.ppermute(tok, "zh", swap(2, 1))
     weight_z = along_z(query_weight)
-    *weight_z, other = lax.optimization_barrier((*weight_z, other))
+    *weight_z, block = lax.optimization_barrier((*weight_z, jnp.concatenate([tok, other], 0)))
     weight_z = jnp.stack(weight_z)
     weight = gather_chips(weight_z)
-    blocks = gather_tokens(jnp.concatenate([tok, other], 0))
+    blocks = gather_tokens(block)
 
     normt, normed, query, keep, send = call(
         lambda *refs: first_kernel(scale, *refs),
@@ -219,9 +220,7 @@
 
     pair = (2 * ROWS, cols)
     partial = call(sum_kernel, [(pair, BF16)], 48)(scatter_parts(keep, send))[0]
-    mine = add(partial, lax.ppermute(partial, "z2", swap(2, 1)))
-    theirs = lax.ppermute(mine, "z1", swap(2, 1))
-    first, square = call(pair_kernel, [((2, *pair), BF16), ((8, HEAD), F32)], 48)(mine, theirs)
+    first, square = call(pair_kernel, [((2, *pair), BF16), ((8, HEAD), F32)], 48)(*along_z(partial))
     first_all = gather_chips(first)
     square = jnp.sum(everywhere(square, ("zh", "y"), 16), 0)
     square = everywhere(square, ("x", "core"), 8)

time: 176 us -> 175 us (level)
  waiting for transfers between devices: 27 us -> 20.6 us
  starting transfers between devices: 58.5 us -> 64.2 us
  blocking collectives: 59.9 us -> 58.1 us
    ppermute x3 -> x6, starting transfers between devices: 9.27 us -> 18.6 us  [along_z(): lax.ppermute(block, ('z2', 'z1'), swap(4, k))]
    ppermute x2 -> x0, waiting for transfers between devices: 8.56 us -> none  [the longest x1 5.13 us: shards(): mine = add(partial, lax.ppermute(partial, 'z2', swap(2, 1)))]
    ppermute x2 -> x0, starting transfers between devices: 4.1 us -> none  [the longest x1 2.18 us: shards(): mine = add(partial, lax.ppermute(partial, 'z2', swap(2, 1)))]
    ppermute x3 -> x6, waiting for transfers between devices: 4.7 us -> 7.99 us  [along_z(): lax.ppermute(block, ('z2', 'z1'), swap(4, k))]
  transfers between devices with their start and end apart: 18 -> 19, of which waited for: 7 -> 6; matrix products, arithmetic and copies ran while one was open for 1% -> 1% of each run, Pallas kernels for 0% -> 0%
where the time goes in v8:
time: 175 us; the launch traced here: 172 us
  starting transfers between devices  64.2 us (37%)
  blocking collectives  58.1 us (33%)
  waiting for transfers between devices  20.6 us (12%)
  between operations  13.7 us (8%)
  Pallas kernels  9.69 us (6%)
  other arithmetic  4.62 us (3%)
    all_to_all x2, blocking collectives, scatter_parts(): return lax.all_to_all(pieces, ('x', 'z1'), 0, 0, tiled=True)  30.5 us
    all_to_all x2, blocking collectives, everywhere(): lax.all_to_all(jnp.broadcast_to(value, (size, *value.shape)), axes, 0, 0,...  27.6 us
    ppermute x7, starting transfers between devices, turn(): return lax.ppermute(value, 'y', [(i, (i + step) % 8) for i in range(8)])  24.4 us
    ppermute x6, starting transfers between devices, along_z(): lax.ppermute(block, ('z2', 'z1'), swap(4, k))  18.6 us
    ppermute x1, starting transfers between devices, shards(): other = lax.ppermute(tok, 'zh', swap(2, 1))  11.5 us
    pallas_call x5, Pallas kernels, run(): pl.pallas_call(kernel, out_shape=[jax.ShapeDtypeStruct(s, d) for s, d in...  9.69 us
    ppermute x6, waiting for transfers between devices, along_z(): lax.ppermute(block, ('z2', 'z1'), swap(4, k))  7.99 us
    ppermute x2, starting transfers between devices, scatter_parts(): both = add(keep, lax.ppermute(send, 'core', swap(2, 1)))  7.13 us
  transfers between devices with their start and end apart: 19, of which 6 were waited for; matrix products, arithmetic and copies ran while one was open for 1% of the time, Pallas kernels for 0%

profile of v8, /device:TPU:1, one launch (start us, length us, event | category | flops | bytes accessed | tf_op | source)
XLA Modules:
  0.0 172.4 jit_solution(8171806201728390424)
XLA Ops:
  6.5 11.5 %collective-permute-start.3 = (bf16[192,256]{1,0:T(8,128)(2,1)}, bf16[192,256]{1,0:T(8,128)(2,1)S(1)}, u32[]{:S(2)}, u32[]{:S(2)}) collective-permute-start(bf16[192,256]{1,0:T(8,128)(2,1)} %bitcast.21), channel_id=1, source_target_pairs={{0,1},{1,0},{2,3},{3,2},{4,5},{5,4},{6,7},{7,6},{8,9},{9,8},{10,11... | collective-permute-start | bytes 294920 | tf_op jit(solution)/shard_map/ppermute | solution.py:206
  18.0 4.0 %collective-permute-start.1 = (bf16[96,256]{1,0:T(8,128)(2,1)}, bf16[96,256]{1,0:T(8,128)(2,1)S(1)}, u32[]{:S(2)}, u32[]{:S(2)}) collective-permute-start(bf16[96,256]{1,0:T(8,128)(2,1)} %param.9), channel_id=1, source_target_pairs={{0,256},{128,384},{256,0},{384,128},{1,257},{129,385},{257,1},{385... | collective-permute-start | bytes 147464 | tf_op jit(solution)/shard_map/ppermute | solution.py:188
  22.0 3.1 %collective-permute-start = (bf16[96,256]{1,0:T(8,128)(2,1)}, bf16[96,256]{1,0:T(8,128)(2,1)S(1)}, u32[]{:S(2)}, u32[]{:S(2)}) collective-permute-start(bf16[96,256]{1,0:T(8,128)(2,1)} %param.9), channel_id=1, source_target_pairs={{0,128},{128,0},{256,384},{384,256},{1,129},{129,1},{257,385},{385... | collective-permute-start | bytes 147464 | tf_op jit(solution)/shard_map/ppermute | solution.py:188
  25.1 2.2 %collective-permute-start.2 = (bf16[96,256]{1,0:T(8,128)(2,1)}, bf16[96,256]{1,0:T(8,128)(2,1)S(1)}, u32[]{:S(2)}, u32[]{:S(2)}) collective-permute-start(bf16[96,256]{1,0:T(8,128)(2,1)} %param.9), channel_id=1, source_target_pairs={{0,384},{128,256},{256,128},{384,0},{1,385},{129,257},{257,129},{3... | collective-permute-start | bytes 147464 | tf_op jit(solution)/shard_map/ppermute | solution.py:188
  28.2 3.8 %collective-permute-done.2 = bf16[96,256]{1,0:T(8,128)(2,1)S(1)} collective-permute-done((bf16[96,256]{1,0:T(8,128)(2,1)}, bf16[96,256]{1,0:T(8,128)(2,1)S(1)}, u32[]{:S(2)}, u32[]{:S(2)}) %collective-permute-start.2) | collective-permute-done | bytes 49184 | tf_op jit(solution)/shard_map/ppermute | solution.py:188
  32.0 1.5 pad_maximum_fusion.2
  33.6 5.9 %collective-permute-start.7 = (bf16[384,256]{1,0:T(8,128)(2,1)S(1)}, bf16[384,256]{1,0:T(8,128)(2,1)S(1)}, u32[]{:S(2)}, u32[]{:S(2)}) collective-permute-start(bf16[384,256]{1,0:T(8,128)(2,1)S(1)} %pad_maximum_fusion.1.refs_0_), channel_id=1, source_target_pairs={{0,12},{2,14},{4,0},{6,2},{8,4},{10,6},{12,8},{14,10},{1,13},{3,15... | collective-permute-start | bytes 589832 | tf_op jit(solution)/shard_map/ppermute | solution.py:160
  39.5 1.9 %collective-permute-start.6 = (bf16[384,256]{1,0:T(8,128)(2,1)S(1)}, bf16[384,256]{1,0:T(8,128)(2,1)S(1)}, u32[]{:S(2)}, u32[]{:S(2)}) collective-permute-start(bf16[384,256]{1,0:T(8,128)(2,1)S(1)} %pad_maximum_fusion.1.refs_0_), channel_id=1, source_target_pairs={{0,4},{2,6},{4,8},{6,10},{8,12},{10,14},{12,0},{14,2},{1,5},{3,7},... | collective-permute-start | bytes 589832 | tf_op jit(solution)/shard_map/ppermute | solution.py:160
  41.4 4.7 %collective-permute-start.5 = (bf16[384,256]{1,0:T(8,128)(2,1)S(1)}, bf16[384,256]{1,0:T(8,128)(2,1)S(1)}, u32[]{:S(2)}, u32[]{:S(2)}) collective-permute-start(bf16[384,256]{1,0:T(8,128)(2,1)S(1)} %pad_maximum_fusion.1.refs_0_), channel_id=1, source_target_pairs={{0,14},{2,0},{4,2},{6,4},{8,6},{10,8},{12,10},{14,12},{1,15},{3,1}... | collective-permute-start | bytes 589832 | tf_op jit(solution)/shard_map/ppermute | solution.py:160
  46.1 1.9 %collective-permute-start.4 = (bf16[384,256]{1,0:T(8,128)(2,1)S(1)}, bf16[384,256]{1,0:T(8,128)(2,1)S(1)}, u32[]{:S(2)}, u32[]{:S(2)}) collective-permute-start(bf16[384,256]{1,0:T(8,128)(2,1)S(1)} %pad_maximum_fusion.1.refs_0_), channel_id=1, source_target_pairs={{0,2},{2,4},{4,6},{6,8},{8,10},{10,12},{12,14},{14,0},{1,3},{3,5},... | collective-permute-start | bytes 589832 | tf_op jit(solution)/shard_map/ppermute | solution.py:160
  48.0 4.7 %collective-permute-start.10 = (bf16[384,256]{1,0:T(8,128)(2,1)S(1)}, bf16[384,256]{1,0:T(8,128)(2,1)S(1)}, u32[]{:S(2)}, u32[]{:S(2)}) collective-permute-start(bf16[384,256]{1,0:T(8,128)(2,1)S(1)} %collective-permute-done.7.refs_4_), channel_id=1, source_target_pairs={{0,12},{2,14},{4,0},{6,2},{8,4},{10,6},{12,8},{14,10},{1,13},{3,15... | collective-permute-start | bytes 589832 | tf_op jit(solution)/shard_map/ppermute | solution.py:160
  52.7 1.9 %collective-permute-start.9 = (bf16[384,256]{1,0:T(8,128)(2,1)S(1)}, bf16[384,256]{1,0:T(8,128)(2,1)S(1)}, u32[]{:S(2)}, u32[]{:S(2)}) collective-permute-start(bf16[384,256]{1,0:T(8,128)(2,1)S(1)} %collective-permute-done.7.refs_4_), channel_id=1, source_target_pairs={{0,14},{2,0},{4,2},{6,4},{8,6},{10,8},{12,10},{14,12},{1,15},{3,1}... | collective-permute-start | bytes 589832 | tf_op jit(solution)/shard_map/ppermute | solution.py:160
  54.6 3.4 %collective-permute-start.8 = (bf16[384,256]{1,0:T(8,128)(2,1)S(1)}, bf16[384,256]{1,0:T(8,128)(2,1)S(1)}, u32[]{:S(2)}, u32[]{:S(2)}) collective-permute-start(bf16[384,256]{1,0:T(8,128)(2,1)S(1)} %collective-permute-done.6.refs_3_), channel_id=1, source_target_pairs={{0,2},{2,4},{4,6},{6,8},{8,10},{10,12},{12,14},{14,0},{1,3},{3,5},... | collective-permute-start | bytes 589832 | tf_op jit(solution)/shard_map/ppermute | solution.py:160
  58.0 1.1 pad_maximum_fusion.refs_9_.refs_5_
  59.1 5.8 %collective-permute-done.9.refs_6_ = bf16[384,256]{1,0:T(8,128)(2,1)S(1)} collective-permute-done((bf16[384,256]{1,0:T(8,128)(2,1)S(1)}, bf16[384,256]{1,0:T(8,128)(2,1)S(1)}, u32[]{:S(2)}, u32[]{:S(2)}) %collective-permute-start.9) | collective-permute-done | bytes 196640 | tf_op jit(solution)/shard_map/ppermute | solution.py:160
  64.9 4.9 %shard_map.55 = (bf16[2,4,2,2,96,256]{5,4,3,2,1,0:T(8,128)(2,1)S(1)}, bf16[256,3072]{1,0:T(8,128)(2,1)}, f32[256,256]{1,0:T(8,128)S(1)}, bf16[16,96,256]{2,1,0:T(8,128)(2,1)S(1)}, bf16[16,96,256]{2,1,0:T(8,128)(2,1)S(1)}) custom-call(bf16[384,256]{1,0:T(8,128)(2,1)S(1)} %pad_maximum_fusion.1.refs_0_, bf16[384,256]{1,0:T(8,128)(2,1)S(1)} %collective-permute-done.4.refs_1_, ...), custom_call_target="tpu_custom_call" | custom-call | tf_op jit(solution)/shard_map/pallas_call | solution.py:143
  69.9 4.5 %collective-permute-start.11 = (bf16[16,96,256]{2,1,0:T(8,128)(2,1)S(1)}, bf16[16,96,256]{2,1,0:T(8,128)(2,1)S(1)}, u32[]{:S(2)}, u32[]{:S(2)}) collective-permute-start(bf16[16,96,256]{2,1,0:T(8,128)(2,1)S(1)} %get-tuple-element.27), channel_id=1, source_target_pairs={{0,16},{16,0},{1,17},{17,1},{2,18},{18,2},{3,19},{19,3},{4,20},{20... | collective-permute-start | bytes 2359304 | tf_op jit(solution)/shard_map/ppermute | solution.py:178
  74.4 1.9 %collective-permute-done.11 = bf16[16,96,256]{2,1,0:T(8,128)(2,1)S(1)} collective-permute-done((bf16[16,96,256]{2,1,0:T(8,128)(2,1)S(1)}, bf16[16,96,256]{2,1,0:T(8,128)(2,1)S(1)}, u32[]{:S(2)}, u32[]{:S(2)}) %collective-permute-start.11) | collective-permute-done | bytes 786464 | tf_op jit(solution)/shard_map/ppermute | solution.py:178
  76.5 16.0 %all_to_all.20.parts_ref = bf16[8,192,256]{2,1,0:T(8,128)(2,1)S(1)} all-to-all(bf16[8,192,256]{2,1,0:T(8,128)(2,1)S(1)} %bitcast.15), channel_id=1, replica_groups=mesh['z2'=2,'z1'=2,'x'=4,'core'=2,'y'=8,'zh'=2] {'x','z1'}, dimensions={0} | all-to-all | bytes 1572864 | tf_op jit(solution)/shard_map/all_to_all | solution.py:180
  92.6 2.7 %collective-permute-start.14 = (bf16[192,256]{1,0:T(8,128)(2,1)S(1)}, bf16[192,256]{1,0:T(8,128)(2,1)S(1)}, u32[]{:S(2)}, u32[]{:S(2)}) collective-permute-start(bf16[192,256]{1,0:T(8,128)(2,1)S(1)} %shard_map.56.mine_ref), channel_id=1, source_target_pairs={{0,384},{128,256},{256,128},{384,0},{1,385},{129,257},{257,129},{3... | collective-permute-start | bytes 294920 | tf_op jit(solution)/shard_map/ppermute | solution.py:188
  95.3 3.1 %collective-permute-start.13 = (bf16[192,256]{1,0:T(8,128)(2,1)S(1)}, bf16[192,256]{1,0:T(8,128)(2,1)S(1)}, u32[]{:S(2)}, u32[]{:S(2)}) collective-permute-start(bf16[192,256]{1,0:T(8,128)(2,1)S(1)} %shard_map.56.mine_ref), channel_id=1, source_target_pairs={{0,256},{128,384},{256,0},{384,128},{1,257},{129,385},{257,1},{385... | collective-permute-start | bytes 294920 | tf_op jit(solution)/shard_map/ppermute | solution.py:188
  98.5 3.4 %collective-permute-start.12 = (bf16[192,256]{1,0:T(8,128)(2,1)S(1)}, bf16[192,256]{1,0:T(8,128)(2,1)S(1)}, u32[]{:S(2)}, u32[]{:S(2)}) collective-permute-start(bf16[192,256]{1,0:T(8,128)(2,1)S(1)} %shard_map.56.mine_ref), channel_id=1, source_target_pairs={{0,128},{128,0},{256,384},{384,256},{1,129},{129,1},{257,385},{385... | collective-permute-start | bytes 294920 | tf_op jit(solution)/shard_map/ppermute | solution.py:188
  101.9 4.2 %collective-permute-done.13.mine_far_ref = bf16[192,256]{1,0:T(8,128)(2,1)S(1)} collective-permute-done((bf16[192,256]{1,0:T(8,128)(2,1)S(1)}, bf16[192,256]{1,0:T(8,128)(2,1)S(1)}, u32[]{:S(2)}, u32[]{:S(2)}) %collective-permute-start.13) | collective-permute-done | bytes 98336 | tf_op jit(solution)/shard_map/ppermute | solution.py:188
  106.9 17.6 %all_to_all.21 = f32[16,8,128]{2,1,0:T(8,128)S(1)} all-to-all(f32[16,8,128]{2,1,0:T(8,128)S(1)} %broadcast_in_dim.6), channel_id=1, replica_groups=mesh['z2'=2,'z1'=2,'x'=4,'core'=2,'y'=8,'zh'=2] {'zh','y'}, dimensions={0} | all-to-all | bytes 131072 | tf_op jit(solution)/shard_map/all_to_all | solution.py:184
  124.5 10.0 %all_to_all.22.refs_0_ = f32[8,8,128]{2,1,0:T(8,128)S(1)} all-to-all(f32[8,8,128]{2,1,0:T(8,128)S(1)} %broadcast_in_dim.7), channel_id=1, replica_groups=mesh['z2'=2,'z1'=2,'x'=4,'core'=2,'y'=8,'zh'=2] {'x','core'}, dimensions={0} | all-to-all | bytes 65536 | tf_op jit(solution)/shard_map/all_to_all | solution.py:184
  134.5 1.4 copy-done.2
  135.9 3.8 %shard_map.58 = (bf16[16,96,256]{2,1,0:T(8,128)(2,1)S(1)}, bf16[16,96,256]{2,1,0:T(8,128)(2,1)S(1)}) custom-call(f32[8,8,128]{2,1,0:T(8,128)S(1)} %all_to_all.22.refs_0_, f32[256,256]{1,0:T(8,128)S(1)} %get-tuple-element.29.refs_1_, bf16[8,2,192,256]{3,2,1,0:T(8,128)(2,1)S(1)} %bitcast.14, bf16[256,3072]{1,0:T(8,128)(2,1)S(1)} %copy-done.1, ...), custom_call_target="tpu_custom_call" | custom-call | tf_op jit(solution)/shard_map/pallas_call | solution.py:143
  139.7 2.6 %collective-permute-start.15 = (bf16[16,96,256]{2,1,0:T(8,128)(2,1)S(1)}, bf16[16,96,256]{2,1,0:T(8,128)(2,1)S(1)}, u32[]{:S(2)}, u32[]{:S(2)}) collective-permute-start(bf16[16,96,256]{2,1,0:T(8,128)(2,1)S(1)} %get-tuple-element.34), channel_id=1, source_target_pairs={{0,16},{16,0},{1,17},{17,1},{2,18},{18,2},{3,19},{19,3},{4,20},{20... | collective-permute-start | bytes 2359304 | tf_op jit(solution)/shard_map/ppermute | solution.py:178
  142.4 1.9 %collective-permute-done.15 = bf16[16,96,256]{2,1,0:T(8,128)(2,1)S(1)} collective-permute-done((bf16[16,96,256]{2,1,0:T(8,128)(2,1)S(1)}, bf16[16,96,256]{2,1,0:T(8,128)(2,1)S(1)}, u32[]{:S(2)}, u32[]{:S(2)}) %collective-permute-start.15) | collective-permute-done | bytes 786464 | tf_op jit(solution)/shard_map/ppermute | solution.py:178
  144.5 14.6 %all_to_all.23 = bf16[8,192,256]{2,1,0:T(8,128)(2,1)S(1)} all-to-all(bf16[8,192,256]{2,1,0:T(8,128)(2,1)S(1)} %bitcast.16), channel_id=1, replica_groups=mesh['z2'=2,'z1'=2,'x'=4,'core'=2,'y'=8,'zh'=2] {'x','z1'}, dimensions={0} | all-to-all | bytes 1572864 | tf_op jit(solution)/shard_map/all_to_all | solution.py:180
  159.2 2.7 %collective-permute-start.16 = (bf16[96,256]{1,0:T(8,128)(2,1)S(1)}, bf16[96,256]{1,0:T(8,128)(2,1)S(1)}, u32[]{:S(2)}, u32[]{:S(2)}) collective-permute-start(bf16[96,256]{1,0:T(8,128)(2,1)S(1)} %get-tuple-element.36), channel_id=1, source_target_pairs={{0,256},{256,0},{1,257},{257,1},{2,258},{258,2},{3,259},{259,3},{4... | collective-permute-start | bytes 147464 | tf_op jit(solution)/shard_map/ppermute | solution.py:236
  161.9 3.0 %collective-permute-done.16 = bf16[96,256]{1,0:T(8,128)(2,1)S(1)} collective-permute-done((bf16[96,256]{1,0:T(8,128)(2,1)S(1)}, bf16[96,256]{1,0:T(8,128)(2,1)S(1)}, u32[]{:S(2)}, u32[]{:S(2)}) %collective-permute-start.16) | collective-permute-done | bytes 49184 | tf_op jit(solution)/shard_map/ppermute | solution.py:236
  (32 shorter events, 3.1 us)
Async XLA Ops:
  6.5 58.4 %all-gather.5.cloned.1.call-start = ((), (), s32[]{:S(2)}) async-start(), calls=%async_computation.4 | async-start | bytes 1769472 | tf_op jit(solution)/shard_map/all_gather | solution.py:192
  6.5 20.8 %collective-permute-start.3 = (bf16[192,256]{1,0:T(8,128)(2,1)}, bf16[192,256]{1,0:T(8,128)(2,1)S(1)}, u32[]{:S(2)}, u32[]{:S(2)}) collective-permute-start(bf16[192,256]{1,0:T(8,128)(2,1)} %bitcast.21), channel_id=1, source_target_pairs={{0,1},{1,0},{2,3},{3,2},{4,5},{5,4},{6,7},{7,6},{8,9},{9,8},{10,11... | collective-permute-start | bytes 294920 | tf_op jit(solution)/shard_map/ppermute | solution.py:206
  18.0 10.2 %collective-permute-start.1 = (bf16[96,256]{1,0:T(8,128)(2,1)}, bf16[96,256]{1,0:T(8,128)(2,1)S(1)}, u32[]{:S(2)}, u32[]{:S(2)}) collective-permute-start(bf16[96,256]{1,0:T(8,128)(2,1)} %param.9), channel_id=1, source_target_pairs={{0,256},{128,384},{256,0},{384,128},{1,257},{129,385},{257,1},{385... | collective-permute-start | bytes 147464 | tf_op jit(solution)/shard_map/ppermute | solution.py:188
  22.0 6.2 %collective-permute-start = (bf16[96,256]{1,0:T(8,128)(2,1)}, bf16[96,256]{1,0:T(8,128)(2,1)S(1)}, u32[]{:S(2)}, u32[]{:S(2)}) collective-permute-start(bf16[96,256]{1,0:T(8,128)(2,1)} %param.9), channel_id=1, source_target_pairs={{0,128},{128,0},{256,384},{384,256},{1,129},{129,1},{257,385},{385... | collective-permute-start | bytes 147464 | tf_op jit(solution)/shard_map/ppermute | solution.py:188
  25.1 6.9 %collective-permute-start.2 = (bf16[96,256]{1,0:T(8,128)(2,1)}, bf16[96,256]{1,0:T(8,128)(2,1)S(1)}, u32[]{:S(2)}, u32[]{:S(2)}) collective-permute-start(bf16[96,256]{1,0:T(8,128)(2,1)} %param.9), channel_id=1, source_target_pairs={{0,384},{128,256},{256,128},{384,0},{1,385},{129,257},{257,129},{3... | collective-permute-start | bytes 147464 | tf_op jit(solution)/shard_map/ppermute | solution.py:188
  33.5 101.0 %all-gather.7.cloned.1.call-start = ((), (), s32[]{:S(2)}) async-start(), calls=%async_computation.5 | async-start | bytes 1769472 | tf_op jit(solution)/shard_map/all_gather | solution.py:192
  33.6 14.4 %collective-permute-start.7 = (bf16[384,256]{1,0:T(8,128)(2,1)S(1)}, bf16[384,256]{1,0:T(8,128)(2,1)S(1)}, u32[]{:S(2)}, u32[]{:S(2)}) collective-permute-start(bf16[384,256]{1,0:T(8,128)(2,1)S(1)} %pad_maximum_fusion.1.refs_0_), channel_id=1, source_target_pairs={{0,12},{2,14},{4,0},{6,2},{8,4},{10,6},{12,8},{14,10},{1,13},{3,15... | collective-permute-start | bytes 589832 | tf_op jit(solution)/shard_map/ppermute | solution.py:160
  39.5 15.2 %collective-permute-start.6 = (bf16[384,256]{1,0:T(8,128)(2,1)S(1)}, bf16[384,256]{1,0:T(8,128)(2,1)S(1)}, u32[]{:S(2)}, u32[]{:S(2)}) collective-permute-start(bf16[384,256]{1,0:T(8,128)(2,1)S(1)} %pad_maximum_fusion.1.refs_0_), channel_id=1, source_target_pairs={{0,4},{2,6},{4,8},{6,10},{8,12},{10,14},{12,0},{14,2},{1,5},{3,7},... | collective-permute-start | bytes 589832 | tf_op jit(solution)/shard_map/ppermute | solution.py:160
  41.4 17.7 %collective-permute-start.5 = (bf16[384,256]{1,0:T(8,128)(2,1)S(1)}, bf16[384,256]{1,0:T(8,128)(2,1)S(1)}, u32[]{:S(2)}, u32[]{:S(2)}) collective-permute-start(bf16[384,256]{1,0:T(8,128)(2,1)S(1)} %pad_maximum_fusion.1.refs_0_), channel_id=1, source_target_pairs={{0,14},{2,0},{4,2},{6,4},{8,6},{10,8},{12,10},{14,12},{1,15},{3,1}... | collective-permute-start | bytes 589832 | tf_op jit(solution)/shard_map/ppermute | solution.py:160
  46.1 13.0 %collective-permute-start.4 = (bf16[384,256]{1,0:T(8,128)(2,1)S(1)}, bf16[384,256]{1,0:T(8,128)(2,1)S(1)}, u32[]{:S(2)}, u32[]{:S(2)}) collective-permute-start(bf16[384,256]{1,0:T(8,128)(2,1)S(1)} %pad_maximum_fusion.1.refs_0_), channel_id=1, source_target_pairs={{0,2},{2,4},{4,6},{6,8},{8,10},{10,12},{12,14},{14,0},{1,3},{3,5},... | collective-permute-start | bytes 589832 | tf_op jit(solution)/shard_map/ppermute | solution.py:160
  48.0 11.1 %collective-permute-start.10 = (bf16[384,256]{1,0:T(8,128)(2,1)S(1)}, bf16[384,256]{1,0:T(8,128)(2,1)S(1)}, u32[]{:S(2)}, u32[]{:S(2)}) collective-permute-start(bf16[384,256]{1,0:T(8,128)(2,1)S(1)} %collective-permute-done.7.refs_4_), channel_id=1, source_target_pairs={{0,12},{2,14},{4,0},{6,2},{8,4},{10,6},{12,8},{14,10},{1,13},{3,15... | collective-permute-start | bytes 589832 | tf_op jit(solution)/shard_map/ppermute | solution.py:160
  52.7 12.2 %collective-permute-start.9 = (bf16[384,256]{1,0:T(8,128)(2,1)S(1)}, bf16[384,256]{1,0:T(8,128)(2,1)S(1)}, u32[]{:S(2)}, u32[]{:S(2)}) collective-permute-start(bf16[384,256]{1,0:T(8,128)(2,1)S(1)} %collective-permute-done.7.refs_4_), channel_id=1, source_target_pairs={{0,14},{2,0},{4,2},{6,4},{8,6},{10,8},{12,10},{14,12},{1,15},{3,1}... | collective-permute-start | bytes 589832 | tf_op jit(solution)/shard_map/ppermute | solution.py:160
  54.6 10.3 %collective-permute-start.8 = (bf16[384,256]{1,0:T(8,128)(2,1)S(1)}, bf16[384,256]{1,0:T(8,128)(2,1)S(1)}, u32[]{:S(2)}, u32[]{:S(2)}) collective-permute-start(bf16[384,256]{1,0:T(8,128)(2,1)S(1)} %collective-permute-done.6.refs_3_), channel_id=1, source_target_pairs={{0,2},{2,4},{4,6},{6,8},{8,10},{10,12},{12,14},{14,0},{1,3},{3,5},... | collective-permute-start | bytes 589832 | tf_op jit(solution)/shard_map/ppermute | solution.py:160
  69.9 22.6 %copy-start = (bf16[2,4,2,2,96,256]{5,4,3,2,1,0:T(8,128)(2,1)}, bf16[2,4,2,2,96,256]{5,4,3,2,1,0:T(8,128)(2,1)S(1)}, u32[]{:S(2)}) copy-start(bf16[2,4,2,2,96,256]{5,4,3,2,1,0:T(8,128)(2,1)S(1)} %get-tuple-element.32.refs_4_) | copy-start | bytes 4718596
  69.9 6.4 %collective-permute-start.11 = (bf16[16,96,256]{2,1,0:T(8,128)(2,1)S(1)}, bf16[16,96,256]{2,1,0:T(8,128)(2,1)S(1)}, u32[]{:S(2)}, u32[]{:S(2)}) collective-permute-start(bf16[16,96,256]{2,1,0:T(8,128)(2,1)S(1)} %get-tuple-element.27), channel_id=1, source_target_pairs={{0,16},{16,0},{1,17},{17,1},{2,18},{18,2},{3,19},{19,3},{4,20},{20... | collective-permute-start | bytes 2359304 | tf_op jit(solution)/shard_map/ppermute | solution.py:178
  76.5 58.0 %copy-start.1 = (bf16[256,3072]{1,0:T(8,128)(2,1)S(1)}, bf16[256,3072]{1,0:T(8,128)(2,1)}, u32[]{:S(2)}) copy-start(bf16[256,3072]{1,0:T(8,128)(2,1)} %get-tuple-element.31.refs_3_) | copy-start | bytes 4718596
  92.6 9.3 %collective-permute-start.14 = (bf16[192,256]{1,0:T(8,128)(2,1)S(1)}, bf16[192,256]{1,0:T(8,128)(2,1)S(1)}, u32[]{:S(2)}, u32[]{:S(2)}) collective-permute-start(bf16[192,256]{1,0:T(8,128)(2,1)S(1)} %shard_map.56.mine_ref), channel_id=1, source_target_pairs={{0,384},{128,256},{256,128},{384,0},{1,385},{129,257},{257,129},{3... | collective-permute-start | bytes 294920 | tf_op jit(solution)/shard_map/ppermute | solution.py:188
  95.3 10.8 %collective-permute-start.13 = (bf16[192,256]{1,0:T(8,128)(2,1)S(1)}, bf16[192,256]{1,0:T(8,128)(2,1)S(1)}, u32[]{:S(2)}, u32[]{:S(2)}) collective-permute-start(bf16[192,256]{1,0:T(8,128)(2,1)S(1)} %shard_map.56.mine_ref), channel_id=1, source_target_pairs={{0,256},{128,384},{256,0},{384,128},{1,257},{129,385},{257,1},{385... | collective-permute-start | bytes 294920 | tf_op jit(solution)/shard_map/ppermute | solution.py:188
  98.5 7.7 %collective-permute-start.12 = (bf16[192,256]{1,0:T(8,128)(2,1)S(1)}, bf16[192,256]{1,0:T(8,128)(2,1)S(1)}, u32[]{:S(2)}, u32[]{:S(2)}) collective-permute-start(bf16[192,256]{1,0:T(8,128)(2,1)S(1)} %shard_map.56.mine_ref), channel_id=1, source_target_pairs={{0,128},{128,0},{256,384},{384,256},{1,129},{129,1},{257,385},{385... | collective-permute-start | bytes 294920 | tf_op jit(solution)/shard_map/ppermute | solution.py:188
  134.5 1.4 copy-start.2
  139.7 4.5 %collective-permute-start.15 = (bf16[16,96,256]{2,1,0:T(8,128)(2,1)S(1)}, bf16[16,96,256]{2,1,0:T(8,128)(2,1)S(1)}, u32[]{:S(2)}, u32[]{:S(2)}) collective-permute-start(bf16[16,96,256]{2,1,0:T(8,128)(2,1)S(1)} %get-tuple-element.34), channel_id=1, source_target_pairs={{0,16},{16,0},{1,17},{17,1},{2,18},{18,2},{3,19},{19,3},{4,20},{20... | collective-permute-start | bytes 2359304 | tf_op jit(solution)/shard_map/ppermute | solution.py:178
  159.2 5.7 %collective-permute-start.16 = (bf16[96,256]{1,0:T(8,128)(2,1)S(1)}, bf16[96,256]{1,0:T(8,128)(2,1)S(1)}, u32[]{:S(2)}, u32[]{:S(2)}) collective-permute-start(bf16[96,256]{1,0:T(8,128)(2,1)S(1)} %get-tuple-element.36), channel_id=1, source_target_pairs={{0,256},{256,0},{1,257},{257,1},{2,258},{258,2},{3,259},{259,3},{4... | collective-permute-start | bytes 147464 | tf_op jit(solution)/shard_map/ppermute | solution.py:236
Sparse Core Ops, SparseCore 0:
  33.7 28.1 all-gather.4
  107.0 25.0 all-gather.6

commit v9 on v8

--- a/solution.py
+++ b/solution.py
@@ -46,8 +46,8 @@
     return jnp.concatenate(heads, axis=1)
 
 
-def fetch(pairs, sems):
-    copies = [pltpu.make_async_copy(src, dst, sems.at[i]) for i, (src, dst) in enumerate(pairs)]
+def fetch(pairs, sems, first=0):
+    copies = [pltpu.make_async_copy(src, dst, sems.at[first + i]) for i, (src, dst) in enumerate(pairs)]
     for copy in copies:
         copy.start()
     return copies
@@ -125,14 +125,27 @@
     square_ref[...] = square[:, :HEAD] + square[:, HEAD:]
 
 
-def second_kernel(scale, radius, square_ref, query_ref, first_ref, normed_ref, normt_any, sides_ref,
-                  keep_ref, send_ref, normt_ref, sems):
-    copies = fetch([(normt_any, normt_ref)], sems)
+def second_kernel(scale, radius, square_any, query_any, first_any, normed_any, normt_any, sides_any,
+                  keep_ref, send_ref, square_ref, query_ref, first_ref, normed_ref, normt_ref, sides_ref, sems):
+    cuts = 4
+    chips, run = first_ref.shape[0] // cuts, normed_ref.shape[1] // cuts
+    pairs = []
+    for i in range(cuts):
+        rows, cols = pl.ds(i * chips, chips), pl.ds(i * run, run)
+        pairs += [(first_any.at[rows], first_ref.at[rows]), (normed_any.at[:, cols], normed_ref.at[:, cols])]
+    pairs += [(square_any, square_ref), (query_any, query_ref), (sides_any, sides_ref)]
+    copies = fetch(pairs, sems)
+    move = jnp.zeros(query_ref.shape, F32)
+    for i in range(cuts):
+        wait(copies[2 * i:2 * i + 2])
+        rows = first_ref[i * chips:(i + 1) * chips].reshape(run, first_ref.shape[-1])
+        move += mm(normed_ref[:, i * run:(i + 1) * run], rows)
+    late = fetch([(normt_any, normt_ref)], sems, len(copies))
+    wait(copies[2 * cuts:])
     norm = jnp.sqrt(jnp.sum(jnp.sum(square_ref[...], 0), keepdims=True))
-    move = mm(normed_ref[...], first_ref[...].reshape(normed_ref.shape[1], first_ref.shape[-1]))
     query = query_ref[...] + (radius / norm) * move
     dq = query_grad(query, sides_ref[0], sides_ref[1], sides_ref[2])
-    wait(copies)
+    wait(late)
     term(scale, normt_ref, dq, keep_ref, send_ref)
 
 
@@ -224,13 +237,14 @@
     first_all = gather_chips(first)
     square = jnp.sum(everywhere(square, ("zh", "y"), 16), 0)
     square = everywhere(square, ("x", "core"), 8)
+    args = (square, query, first_all, normed, normt, sides)
     keep, send = call(
         lambda *refs: second_kernel(scale, radius, *refs),
         [(half, BF16), (half, BF16)],
-        48,
-        anywhere=(4,),
-        scratch=(pltpu.VMEM(normt_like, BF16), pltpu.SemaphoreType.DMA((1,))),
-    )(square, query, first_all, normed, normt, sides)
+        51,
+        anywhere=range(len(args)),
+        scratch=[pltpu.VMEM(arg.shape, arg.dtype) for arg in args] + [pltpu.SemaphoreType.DMA((12,))],
+    )(*args)
     parts = scatter_parts(keep, send).reshape(8, 2, ROWS, cols)
     own, give = call(half_sums_kernel, [((ROWS, cols), F32), ((ROWS, cols), BF16)], 48)(parts)
     return own + lax.ppermute(give, "z2", swap(2, 1)).astype(F32)

time: 175 us -> 174 us (level)
  no operation moved by 1% of the time
where the time goes in v9:
time: 174 us; the launch traced here: 172 us
  starting transfers between devices  64.2 us (37%)
  blocking collectives  58 us (33%)
  waiting for transfers between devices  20.6 us (12%)
  between operations  13.7 us (8%)
  Pallas kernels  10.5 us (6%)
  other arithmetic  4.63 us (3%)
    all_to_all x2, blocking collectives, scatter_parts(): return lax.all_to_all(pieces, ('x', 'z1'), 0, 0, tiled=True)  30.4 us
    all_to_all x2, blocking collectives, everywhere(): lax.all_to_all(jnp.broadcast_to(value, (size, *value.shape)), axes, 0, 0,...  27.6 us
    ppermute x7, starting transfers between devices, turn(): return lax.ppermute(value, 'y', [(i, (i + step) % 8) for i in range(8)])  24.4 us
    ppermute x6, starting transfers between devices, along_z(): lax.ppermute(block, ('z2', 'z1'), swap(4, k))  18.6 us
    ppermute x1, starting transfers between devices, shards(): other = lax.ppermute(tok, 'zh', swap(2, 1))  11.5 us
    pallas_call x5, Pallas kernels, run(): pl.pallas_call(kernel, out_shape=[jax.ShapeDtypeStruct(s, d) for s, d in...  10.5 us
    ppermute x6, waiting for transfers between devices, along_z(): lax.ppermute(block, ('z2', 'z1'), swap(4, k))  7.98 us
    ppermute x2, starting transfers between devices, scatter_parts(): both = add(keep, lax.ppermute(send, 'core', swap(2, 1)))  7.13 us
  transfers between devices with their start and end apart: 19, of which 6 were waited for; matrix products, arithmetic and copies ran while one was open for 1% of the time, Pallas kernels for 0%

profile of v9, /device:TPU:1, one launch (start us, length us, event | category | flops | bytes accessed | tf_op | source)
XLA Modules:
  0.0 171.6 jit_solution(7134692652710353033)
XLA Ops:
  6.5 11.5 %collective-permute-start.3 = (bf16[192,256]{1,0:T(8,128)(2,1)}, bf16[192,256]{1,0:T(8,128)(2,1)S(1)}, u32[]{:S(2)}, u32[]{:S(2)}) collective-permute-start(bf16[192,256]{1,0:T(8,128)(2,1)} %bitcast.21), channel_id=1, source_target_pairs={{0,1},{1,0},{2,3},{3,2},{4,5},{5,4},{6,7},{7,6},{8,9},{9,8},{10,11... | collective-permute-start | bytes 294920 | tf_op jit(solution)/shard_map/ppermute | solution.py:219
  18.0 4.0 %collective-permute-start.1 = (bf16[96,256]{1,0:T(8,128)(2,1)}, bf16[96,256]{1,0:T(8,128)(2,1)S(1)}, u32[]{:S(2)}, u32[]{:S(2)}) collective-permute-start(bf16[96,256]{1,0:T(8,128)(2,1)} %param.9), channel_id=1, source_target_pairs={{0,256},{128,384},{256,0},{384,128},{1,257},{129,385},{257,1},{385... | collective-permute-start | bytes 147464 | tf_op jit(solution)/shard_map/ppermute | solution.py:201
  22.0 3.1 %collective-permute-start = (bf16[96,256]{1,0:T(8,128)(2,1)}, bf16[96,256]{1,0:T(8,128)(2,1)S(1)}, u32[]{:S(2)}, u32[]{:S(2)}) collective-permute-start(bf16[96,256]{1,0:T(8,128)(2,1)} %param.9), channel_id=1, source_target_pairs={{0,128},{128,0},{256,384},{384,256},{1,129},{129,1},{257,385},{385... | collective-permute-start | bytes 147464 | tf_op jit(solution)/shard_map/ppermute | solution.py:201
  25.1 2.2 %collective-permute-start.2 = (bf16[96,256]{1,0:T(8,128)(2,1)}, bf16[96,256]{1,0:T(8,128)(2,1)S(1)}, u32[]{:S(2)}, u32[]{:S(2)}) collective-permute-start(bf16[96,256]{1,0:T(8,128)(2,1)} %param.9), channel_id=1, source_target_pairs={{0,384},{128,256},{256,128},{384,0},{1,385},{129,257},{257,129},{3... | collective-permute-start | bytes 147464 | tf_op jit(solution)/shard_map/ppermute | solution.py:201
  27.3 0.9 pad_maximum_fusion.1.refs_0_
  28.2 3.8 %collective-permute-done.2 = bf16[96,256]{1,0:T(8,128)(2,1)S(1)} collective-permute-done((bf16[96,256]{1,0:T(8,128)(2,1)}, bf16[96,256]{1,0:T(8,128)(2,1)S(1)}, u32[]{:S(2)}, u32[]{:S(2)}) %collective-permute-start.2) | collective-permute-done | bytes 49184 | tf_op jit(solution)/shard_map/ppermute | solution.py:201
  32.0 1.5 pad_maximum_fusion.2
  33.6 5.9 %collective-permute-start.7 = (bf16[384,256]{1,0:T(8,128)(2,1)S(1)}, bf16[384,256]{1,0:T(8,128)(2,1)S(1)}, u32[]{:S(2)}, u32[]{:S(2)}) collective-permute-start(bf16[384,256]{1,0:T(8,128)(2,1)S(1)} %pad_maximum_fusion.1.refs_0_), channel_id=1, source_target_pairs={{0,12},{2,14},{4,0},{6,2},{8,4},{10,6},{12,8},{14,10},{1,13},{3,15... | collective-permute-start | bytes 589832 | tf_op jit(solution)/shard_map/ppermute | solution.py:173
  39.5 1.9 %collective-permute-start.6 = (bf16[384,256]{1,0:T(8,128)(2,1)S(1)}, bf16[384,256]{1,0:T(8,128)(2,1)S(1)}, u32[]{:S(2)}, u32[]{:S(2)}) collective-permute-start(bf16[384,256]{1,0:T(8,128)(2,1)S(1)} %pad_maximum_fusion.1.refs_0_), channel_id=1, source_target_pairs={{0,4},{2,6},{4,8},{6,10},{8,12},{10,14},{12,0},{14,2},{1,5},{3,7},... | collective-permute-start | bytes 589832 | tf_op jit(solution)/shard_map/ppermute | solution.py:173
  41.4 4.7 %collective-permute-start.5 = (bf16[384,256]{1,0:T(8,128)(2,1)S(1)}, bf16[384,256]{1,0:T(8,128)(2,1)S(1)}, u32[]{:S(2)}, u32[]{:S(2)}) collective-permute-start(bf16[384,256]{1,0:T(8,128)(2,1)S(1)} %pad_maximum_fusion.1.refs_0_), channel_id=1, source_target_pairs={{0,14},{2,0},{4,2},{6,4},{8,6},{10,8},{12,10},{14,12},{1,15},{3,1}... | collective-permute-start | bytes 589832 | tf_op jit(solution)/shard_map/ppermute | solution.py:173
  46.1 1.9 %collective-permute-start.4 = (bf16[384,256]{1,0:T(8,128)(2,1)S(1)}, bf16[384,256]{1,0:T(8,128)(2,1)S(1)}, u32[]{:S(2)}, u32[]{:S(2)}) collective-permute-start(bf16[384,256]{1,0:T(8,128)(2,1)S(1)} %pad_maximum_fusion.1.refs_0_), channel_id=1, source_target_pairs={{0,2},{2,4},{4,6},{6,8},{8,10},{10,12},{12,14},{14,0},{1,3},{3,5},... | collective-permute-start | bytes 589832 | tf_op jit(solution)/shard_map/ppermute | solution.py:173
  48.0 4.7 %collective-permute-start.10 = (bf16[384,256]{1,0:T(8,128)(2,1)S(1)}, bf16[384,256]{1,0:T(8,128)(2,1)S(1)}, u32[]{:S(2)}, u32[]{:S(2)}) collective-permute-start(bf16[384,256]{1,0:T(8,128)(2,1)S(1)} %collective-permute-done.7.refs_4_), channel_id=1, source_target_pairs={{0,12},{2,14},{4,0},{6,2},{8,4},{10,6},{12,8},{14,10},{1,13},{3,15... | collective-permute-start | bytes 589832 | tf_op jit(solution)/shard_map/ppermute | solution.py:173
  52.7 1.9 %collective-permute-start.9 = (bf16[384,256]{1,0:T(8,128)(2,1)S(1)}, bf16[384,256]{1,0:T(8,128)(2,1)S(1)}, u32[]{:S(2)}, u32[]{:S(2)}) collective-permute-start(bf16[384,256]{1,0:T(8,128)(2,1)S(1)} %collective-permute-done.7.refs_4_), channel_id=1, source_target_pairs={{0,14},{2,0},{4,2},{6,4},{8,6},{10,8},{12,10},{14,12},{1,15},{3,1}... | collective-permute-start | bytes 589832 | tf_op jit(solution)/shard_map/ppermute | solution.py:173
  54.7 3.4 %collective-permute-start.8 = (bf16[384,256]{1,0:T(8,128)(2,1)S(1)}, bf16[384,256]{1,0:T(8,128)(2,1)S(1)}, u32[]{:S(2)}, u32[]{:S(2)}) collective-permute-start(bf16[384,256]{1,0:T(8,128)(2,1)S(1)} %collective-permute-done.6.refs_3_), channel_id=1, source_target_pairs={{0,2},{2,4},{4,6},{6,8},{8,10},{10,12},{12,14},{14,0},{1,3},{3,5},... | collective-permute-start | bytes 589832 | tf_op jit(solution)/shard_map/ppermute | solution.py:173
  58.0 1.1 pad_maximum_fusion.refs_9_.refs_5_
  59.1 5.8 %collective-permute-done.9.refs_6_ = bf16[384,256]{1,0:T(8,128)(2,1)S(1)} collective-permute-done((bf16[384,256]{1,0:T(8,128)(2,1)S(1)}, bf16[384,256]{1,0:T(8,128)(2,1)S(1)}, u32[]{:S(2)}, u32[]{:S(2)}) %collective-permute-start.9) | collective-permute-done | bytes 196640 | tf_op jit(solution)/shard_map/ppermute | solution.py:173
  64.9 4.9 %shard_map.55 = (bf16[2,4,2,2,96,256]{5,4,3,2,1,0:T(8,128)(2,1)S(1)}, bf16[256,3072]{1,0:T(8,128)(2,1)}, f32[256,256]{1,0:T(8,128)S(1)}, bf16[16,96,256]{2,1,0:T(8,128)(2,1)S(1)}, bf16[16,96,256]{2,1,0:T(8,128)(2,1)S(1)}) custom-call(bf16[384,256]{1,0:T(8,128)(2,1)S(1)} %pad_maximum_fusion.1.refs_0_, bf16[384,256]{1,0:T(8,128)(2,1)S(1)} %collective-permute-done.4.refs_1_, ...), custom_call_target="tpu_custom_call" | custom-call | tf_op jit(solution)/shard_map/pallas_call | solution.py:156
  69.9 4.5 %collective-permute-start.11 = (bf16[16,96,256]{2,1,0:T(8,128)(2,1)S(1)}, bf16[16,96,256]{2,1,0:T(8,128)(2,1)S(1)}, u32[]{:S(2)}, u32[]{:S(2)}) collective-permute-start(bf16[16,96,256]{2,1,0:T(8,128)(2,1)S(1)} %get-tuple-element.27), channel_id=1, source_target_pairs={{0,16},{16,0},{1,17},{17,1},{2,18},{18,2},{3,19},{19,3},{4,20},{20... | collective-permute-start | bytes 2359304 | tf_op jit(solution)/shard_map/ppermute | solution.py:191
  74.4 1.9 %collective-permute-done.11 = bf16[16,96,256]{2,1,0:T(8,128)(2,1)S(1)} collective-permute-done((bf16[16,96,256]{2,1,0:T(8,128)(2,1)S(1)}, bf16[16,96,256]{2,1,0:T(8,128)(2,1)S(1)}, u32[]{:S(2)}, u32[]{:S(2)}) %collective-permute-start.11) | collective-permute-done | bytes 786464 | tf_op jit(solution)/shard_map/ppermute | solution.py:191
  76.5 15.8 %all_to_all.20.parts_ref = bf16[8,192,256]{2,1,0:T(8,128)(2,1)S(1)} all-to-all(bf16[8,192,256]{2,1,0:T(8,128)(2,1)S(1)} %bitcast.14), channel_id=1, replica_groups=mesh['z2'=2,'z1'=2,'x'=4,'core'=2,'y'=8,'zh'=2] {'x','z1'}, dimensions={0} | all-to-all | bytes 1572864 | tf_op jit(solution)/shard_map/all_to_all | solution.py:193
  92.5 2.7 %collective-permute-start.14 = (bf16[192,256]{1,0:T(8,128)(2,1)S(1)}, bf16[192,256]{1,0:T(8,128)(2,1)S(1)}, u32[]{:S(2)}, u32[]{:S(2)}) collective-permute-start(bf16[192,256]{1,0:T(8,128)(2,1)S(1)} %shard_map.56.mine_ref), channel_id=1, source_target_pairs={{0,384},{128,256},{256,128},{384,0},{1,385},{129,257},{257,129},{3... | collective-permute-start | bytes 294920 | tf_op jit(solution)/shard_map/ppermute | solution.py:201
  95.2 3.1 %collective-permute-start.13 = (bf16[192,256]{1,0:T(8,128)(2,1)S(1)}, bf16[192,256]{1,0:T(8,128)(2,1)S(1)}, u32[]{:S(2)}, u32[]{:S(2)}) collective-permute-start(bf16[192,256]{1,0:T(8,128)(2,1)S(1)} %shard_map.56.mine_ref), channel_id=1, source_target_pairs={{0,256},{128,384},{256,0},{384,128},{1,257},{129,385},{257,1},{385... | collective-permute-start | bytes 294920 | tf_op jit(solution)/shard_map/ppermute | solution.py:201
  98.3 3.4 %collective-permute-start.12 = (bf16[192,256]{1,0:T(8,128)(2,1)S(1)}, bf16[192,256]{1,0:T(8,128)(2,1)S(1)}, u32[]{:S(2)}, u32[]{:S(2)}) collective-permute-start(bf16[192,256]{1,0:T(8,128)(2,1)S(1)} %shard_map.56.mine_ref), channel_id=1, source_target_pairs={{0,128},{128,0},{256,384},{384,256},{1,129},{129,1},{257,385},{385... | collective-permute-start | bytes 294920 | tf_op jit(solution)/shard_map/ppermute | solution.py:201
  101.8 4.2 %collective-permute-done.13.mine_far_ref = bf16[192,256]{1,0:T(8,128)(2,1)S(1)} collective-permute-done((bf16[192,256]{1,0:T(8,128)(2,1)S(1)}, bf16[192,256]{1,0:T(8,128)(2,1)S(1)}, u32[]{:S(2)}, u32[]{:S(2)}) %collective-permute-start.13) | collective-permute-done | bytes 98336 | tf_op jit(solution)/shard_map/ppermute | solution.py:201
  106.8 17.6 %all_to_all.21 = f32[16,8,128]{2,1,0:T(8,128)S(1)} all-to-all(f32[16,8,128]{2,1,0:T(8,128)S(1)} %broadcast_in_dim.6), channel_id=1, replica_groups=mesh['z2'=2,'z1'=2,'x'=4,'core'=2,'y'=8,'zh'=2] {'zh','y'}, dimensions={0} | all-to-all | bytes 131072 | tf_op jit(solution)/shard_map/all_to_all | solution.py:197
  124.4 10.0 %all_to_all.22.refs_0_ = f32[8,8,128]{2,1,0:T(8,128)S(1)} all-to-all(f32[8,8,128]{2,1,0:T(8,128)S(1)} %broadcast_in_dim.7), channel_id=1, replica_groups=mesh['z2'=2,'z1'=2,'x'=4,'core'=2,'y'=8,'zh'=2] {'x','core'}, dimensions={0} | all-to-all | bytes 65536 | tf_op jit(solution)/shard_map/all_to_all | solution.py:197
  134.4 4.6 %shard_map.58 = (bf16[16,96,256]{2,1,0:T(8,128)(2,1)S(1)}, bf16[16,96,256]{2,1,0:T(8,128)(2,1)S(1)}) custom-call(f32[8,8,128]{2,1,0:T(8,128)S(1)} %all_to_all.22.refs_0_, f32[256,256]{1,0:T(8,128)S(1)} %get-tuple-element.29.refs_1_, bf16[8,2,192,256]{3,2,1,0:T(8,128)(2,1)} %bitcast.17, bf16[256,3072]{1,0:T(8,128)(2,1)} %get-tuple-element.31.refs_3_, ...), custom_call_target="tpu_custom_call" | custom-call | tf_op jit(solution)/shard_map/pallas_call | solution.py:156
  139.0 2.6 %collective-permute-start.15 = (bf16[16,96,256]{2,1,0:T(8,128)(2,1)S(1)}, bf16[16,96,256]{2,1,0:T(8,128)(2,1)S(1)}, u32[]{:S(2)}, u32[]{:S(2)}) collective-permute-start(bf16[16,96,256]{2,1,0:T(8,128)(2,1)S(1)} %get-tuple-element.34), channel_id=1, source_target_pairs={{0,16},{16,0},{1,17},{17,1},{2,18},{18,2},{3,19},{19,3},{4,20},{20... | collective-permute-start | bytes 2359304 | tf_op jit(solution)/shard_map/ppermute | solution.py:191
  141.6 1.9 %collective-permute-done.15 = bf16[16,96,256]{2,1,0:T(8,128)(2,1)S(1)} collective-permute-done((bf16[16,96,256]{2,1,0:T(8,128)(2,1)S(1)}, bf16[16,96,256]{2,1,0:T(8,128)(2,1)S(1)}, u32[]{:S(2)}, u32[]{:S(2)}) %collective-permute-start.15) | collective-permute-done | bytes 786464 | tf_op jit(solution)/shard_map/ppermute | solution.py:191
  143.7 14.6 %all_to_all.23 = bf16[8,192,256]{2,1,0:T(8,128)(2,1)S(1)} all-to-all(bf16[8,192,256]{2,1,0:T(8,128)(2,1)S(1)} %bitcast.15), channel_id=1, replica_groups=mesh['z2'=2,'z1'=2,'x'=4,'core'=2,'y'=8,'zh'=2] {'x','z1'}, dimensions={0} | all-to-all | bytes 1572864 | tf_op jit(solution)/shard_map/all_to_all | solution.py:193
  158.4 2.7 %collective-permute-start.16 = (bf16[96,256]{1,0:T(8,128)(2,1)S(1)}, bf16[96,256]{1,0:T(8,128)(2,1)S(1)}, u32[]{:S(2)}, u32[]{:S(2)}) collective-permute-start(bf16[96,256]{1,0:T(8,128)(2,1)S(1)} %get-tuple-element.36), channel_id=1, source_target_pairs={{0,256},{256,0},{1,257},{257,1},{2,258},{258,2},{3,259},{259,3},{4... | collective-permute-start | bytes 147464 | tf_op jit(solution)/shard_map/ppermute | solution.py:250
  161.1 3.0 %collective-permute-done.16 = bf16[96,256]{1,0:T(8,128)(2,1)S(1)} collective-permute-done((bf16[96,256]{1,0:T(8,128)(2,1)S(1)}, bf16[96,256]{1,0:T(8,128)(2,1)S(1)}, u32[]{:S(2)}, u32[]{:S(2)}) %collective-permute-start.16) | collective-permute-done | bytes 49184 | tf_op jit(solution)/shard_map/ppermute | solution.py:250
  (28 shorter events, 2.2 us)
Async XLA Ops:
  6.5 58.4 %all-gather.5.cloned.1.call-start = ((), (), s32[]{:S(2)}) async-start(), calls=%async_computation.4 | async-start | bytes 1769472 | tf_op jit(solution)/shard_map/all_gather | solution.py:205
  6.5 20.8 %collective-permute-start.3 = (bf16[192,256]{1,0:T(8,128)(2,1)}, bf16[192,256]{1,0:T(8,128)(2,1)S(1)}, u32[]{:S(2)}, u32[]{:S(2)}) collective-permute-start(bf16[192,256]{1,0:T(8,128)(2,1)} %bitcast.21), channel_id=1, source_target_pairs={{0,1},{1,0},{2,3},{3,2},{4,5},{5,4},{6,7},{7,6},{8,9},{9,8},{10,11... | collective-permute-start | bytes 294920 | tf_op jit(solution)/shard_map/ppermute | solution.py:219
  18.0 10.2 %collective-permute-start.1 = (bf16[96,256]{1,0:T(8,128)(2,1)}, bf16[96,256]{1,0:T(8,128)(2,1)S(1)}, u32[]{:S(2)}, u32[]{:S(2)}) collective-permute-start(bf16[96,256]{1,0:T(8,128)(2,1)} %param.9), channel_id=1, source_target_pairs={{0,256},{128,384},{256,0},{384,128},{1,257},{129,385},{257,1},{385... | collective-permute-start | bytes 147464 | tf_op jit(solution)/shard_map/ppermute | solution.py:201
  22.0 6.2 %collective-permute-start = (bf16[96,256]{1,0:T(8,128)(2,1)}, bf16[96,256]{1,0:T(8,128)(2,1)S(1)}, u32[]{:S(2)}, u32[]{:S(2)}) collective-permute-start(bf16[96,256]{1,0:T(8,128)(2,1)} %param.9), channel_id=1, source_target_pairs={{0,128},{128,0},{256,384},{384,256},{1,129},{129,1},{257,385},{385... | collective-permute-start | bytes 147464 | tf_op jit(solution)/shard_map/ppermute | solution.py:201
  25.1 6.9 %collective-permute-start.2 = (bf16[96,256]{1,0:T(8,128)(2,1)}, bf16[96,256]{1,0:T(8,128)(2,1)S(1)}, u32[]{:S(2)}, u32[]{:S(2)}) collective-permute-start(bf16[96,256]{1,0:T(8,128)(2,1)} %param.9), channel_id=1, source_target_pairs={{0,384},{128,256},{256,128},{384,0},{1,385},{129,257},{257,129},{3... | collective-permute-start | bytes 147464 | tf_op jit(solution)/shard_map/ppermute | solution.py:201
  33.5 100.8 %all-gather.7.cloned.1.call-start = ((), (), s32[]{:S(2)}) async-start(), calls=%async_computation.5 | async-start | bytes 1769472 | tf_op jit(solution)/shard_map/all_gather | solution.py:205
  33.6 14.4 %collective-permute-start.7 = (bf16[384,256]{1,0:T(8,128)(2,1)S(1)}, bf16[384,256]{1,0:T(8,128)(2,1)S(1)}, u32[]{:S(2)}, u32[]{:S(2)}) collective-permute-start(bf16[384,256]{1,0:T(8,128)(2,1)S(1)} %pad_maximum_fusion.1.refs_0_), channel_id=1, source_target_pairs={{0,12},{2,14},{4,0},{6,2},{8,4},{10,6},{12,8},{14,10},{1,13},{3,15... | collective-permute-start | bytes 589832 | tf_op jit(solution)/shard_map/ppermute | solution.py:173
  39.5 15.2 %collective-permute-start.6 = (bf16[384,256]{1,0:T(8,128)(2,1)S(1)}, bf16[384,256]{1,0:T(8,128)(2,1)S(1)}, u32[]{:S(2)}, u32[]{:S(2)}) collective-permute-start(bf16[384,256]{1,0:T(8,128)(2,1)S(1)} %pad_maximum_fusion.1.refs_0_), channel_id=1, source_target_pairs={{0,4},{2,6},{4,8},{6,10},{8,12},{10,14},{12,0},{14,2},{1,5},{3,7},... | collective-permute-start | bytes 589832 | tf_op jit(solution)/shard_map/ppermute | solution.py:173
  41.4 17.7 %collective-permute-start.5 = (bf16[384,256]{1,0:T(8,128)(2,1)S(1)}, bf16[384,256]{1,0:T(8,128)(2,1)S(1)}, u32[]{:S(2)}, u32[]{:S(2)}) collective-permute-start(bf16[384,256]{1,0:T(8,128)(2,1)S(1)} %pad_maximum_fusion.1.refs_0_), channel_id=1, source_target_pairs={{0,14},{2,0},{4,2},{6,4},{8,6},{10,8},{12,10},{14,12},{1,15},{3,1}... | collective-permute-start | bytes 589832 | tf_op jit(solution)/shard_map/ppermute | solution.py:173
  46.1 13.0 %collective-permute-start.4 = (bf16[384,256]{1,0:T(8,128)(2,1)S(1)}, bf16[384,256]{1,0:T(8,128)(2,1)S(1)}, u32[]{:S(2)}, u32[]{:S(2)}) collective-permute-start(bf16[384,256]{1,0:T(8,128)(2,1)S(1)} %pad_maximum_fusion.1.refs_0_), channel_id=1, source_target_pairs={{0,2},{2,4},{4,6},{6,8},{8,10},{10,12},{12,14},{14,0},{1,3},{3,5},... | collective-permute-start | bytes 589832 | tf_op jit(solution)/shard_map/ppermute | solution.py:173
  48.0 11.1 %collective-permute-start.10 = (bf16[384,256]{1,0:T(8,128)(2,1)S(1)}, bf16[384,256]{1,0:T(8,128)(2,1)S(1)}, u32[]{:S(2)}, u32[]{:S(2)}) collective-permute-start(bf16[384,256]{1,0:T(8,128)(2,1)S(1)} %collective-permute-done.7.refs_4_), channel_id=1, source_target_pairs={{0,12},{2,14},{4,0},{6,2},{8,4},{10,6},{12,8},{14,10},{1,13},{3,15... | collective-permute-start | bytes 589832 | tf_op jit(solution)/shard_map/ppermute | solution.py:173
  52.7 12.2 %collective-permute-start.9 = (bf16[384,256]{1,0:T(8,128)(2,1)S(1)}, bf16[384,256]{1,0:T(8,128)(2,1)S(1)}, u32[]{:S(2)}, u32[]{:S(2)}) collective-permute-start(bf16[384,256]{1,0:T(8,128)(2,1)S(1)} %collective-permute-done.7.refs_4_), channel_id=1, source_target_pairs={{0,14},{2,0},{4,2},{6,4},{8,6},{10,8},{12,10},{14,12},{1,15},{3,1}... | collective-permute-start | bytes 589832 | tf_op jit(solution)/shard_map/ppermute | solution.py:173
  54.7 10.3 %collective-permute-start.8 = (bf16[384,256]{1,0:T(8,128)(2,1)S(1)}, bf16[384,256]{1,0:T(8,128)(2,1)S(1)}, u32[]{:S(2)}, u32[]{:S(2)}) collective-permute-start(bf16[384,256]{1,0:T(8,128)(2,1)S(1)} %collective-permute-done.6.refs_3_), channel_id=1, source_target_pairs={{0,2},{2,4},{4,6},{6,8},{8,10},{10,12},{12,14},{14,0},{1,3},{3,5},... | collective-permute-start | bytes 589832 | tf_op jit(solution)/shard_map/ppermute | solution.py:173
  69.9 22.5 %copy-start = (bf16[2,4,2,2,96,256]{5,4,3,2,1,0:T(8,128)(2,1)}, bf16[2,4,2,2,96,256]{5,4,3,2,1,0:T(8,128)(2,1)S(1)}, u32[]{:S(2)}) copy-start(bf16[2,4,2,2,96,256]{5,4,3,2,1,0:T(8,128)(2,1)S(1)} %get-tuple-element.32.refs_4_) | copy-start | bytes 4718596
  69.9 6.4 %collective-permute-start.11 = (bf16[16,96,256]{2,1,0:T(8,128)(2,1)S(1)}, bf16[16,96,256]{2,1,0:T(8,128)(2,1)S(1)}, u32[]{:S(2)}, u32[]{:S(2)}) collective-permute-start(bf16[16,96,256]{2,1,0:T(8,128)(2,1)S(1)} %get-tuple-element.27), channel_id=1, source_target_pairs={{0,16},{16,0},{1,17},{17,1},{2,18},{18,2},{3,19},{19,3},{4,20},{20... | collective-permute-start | bytes 2359304 | tf_op jit(solution)/shard_map/ppermute | solution.py:191
  92.5 9.3 %collective-permute-start.14 = (bf16[192,256]{1,0:T(8,128)(2,1)S(1)}, bf16[192,256]{1,0:T(8,128)(2,1)S(1)}, u32[]{:S(2)}, u32[]{:S(2)}) collective-permute-start(bf16[192,256]{1,0:T(8,128)(2,1)S(1)} %shard_map.56.mine_ref), channel_id=1, source_target_pairs={{0,384},{128,256},{256,128},{384,0},{1,385},{129,257},{257,129},{3... | collective-permute-start | bytes 294920 | tf_op jit(solution)/shard_map/ppermute | solution.py:201
  95.2 10.8 %collective-permute-start.13 = (bf16[192,256]{1,0:T(8,128)(2,1)S(1)}, bf16[192,256]{1,0:T(8,128)(2,1)S(1)}, u32[]{:S(2)}, u32[]{:S(2)}) collective-permute-start(bf16[192,256]{1,0:T(8,128)(2,1)S(1)} %shard_map.56.mine_ref), channel_id=1, source_target_pairs={{0,256},{128,384},{256,0},{384,128},{1,257},{129,385},{257,1},{385... | collective-permute-start | bytes 294920 | tf_op jit(solution)/shard_map/ppermute | solution.py:201
  98.3 7.7 %collective-permute-start.12 = (bf16[192,256]{1,0:T(8,128)(2,1)S(1)}, bf16[192,256]{1,0:T(8,128)(2,1)S(1)}, u32[]{:S(2)}, u32[]{:S(2)}) collective-permute-start(bf16[192,256]{1,0:T(8,128)(2,1)S(1)} %shard_map.56.mine_ref), channel_id=1, source_target_pairs={{0,128},{128,0},{256,384},{384,256},{1,129},{129,1},{257,385},{385... | collective-permute-start | bytes 294920 | tf_op jit(solution)/shard_map/ppermute | solution.py:201
  139.0 4.5 %collective-permute-start.15 = (bf16[16,96,256]{2,1,0:T(8,128)(2,1)S(1)}, bf16[16,96,256]{2,1,0:T(8,128)(2,1)S(1)}, u32[]{:S(2)}, u32[]{:S(2)}) collective-permute-start(bf16[16,96,256]{2,1,0:T(8,128)(2,1)S(1)} %get-tuple-element.34), channel_id=1, source_target_pairs={{0,16},{16,0},{1,17},{17,1},{2,18},{18,2},{3,19},{19,3},{4,20},{20... | collective-permute-start | bytes 2359304 | tf_op jit(solution)/shard_map/ppermute | solution.py:191
  158.4 5.7 %collective-permute-start.16 = (bf16[96,256]{1,0:T(8,128)(2,1)S(1)}, bf16[96,256]{1,0:T(8,128)(2,1)S(1)}, u32[]{:S(2)}, u32[]{:S(2)}) collective-permute-start(bf16[96,256]{1,0:T(8,128)(2,1)S(1)} %get-tuple-element.36), channel_id=1, source_target_pairs={{0,256},{256,0},{1,257},{257,1},{2,258},{258,2},{3,259},{259,3},{4... | collective-permute-start | bytes 147464 | tf_op jit(solution)/shard_map/ppermute | solution.py:250
Sparse Core Ops, SparseCore 0:
  33.7 28.1 all-gather.4
  106.9 25.0 all-gather.6

commit v10 on v9

--- a/solution.py
+++ b/solution.py
@@ -44,6 +44,33 @@
         )
         heads.append(dq.astype(BF16))
     return jnp.concatenate(heads, axis=1)
+
+
+def by_head(array):
+    return [array[:, h * HEAD:(h + 1) * HEAD] for h in range(array.shape[1] // HEAD)]
+
+
+def prob_grads(sides_ref):
+    return [mm(cot, value, ((1,), (1,))) for cot, value in zip(by_head(sides_ref[2]), by_head(sides_ref[1]))]
+
+
+def query_grad_beside(query, keys, dprobs):
+    temper = 1.0 / math.sqrt(HEAD)
+    keys = by_head(keys)
+    centers = [q - jnp.mean(q, -1, keepdims=True) for q in by_head(query)]
+    inverses = [lax.rsqrt(jnp.mean(center * center, -1, keepdims=True) + EPS) for center in centers]
+    qns = [center * inverse for center, inverse in zip(centers, inverses)]
+    scores = [mm(qn.astype(BF16), key, ((1,), (1,))) * temper for qn, key in zip(qns, keys)]
+    expons = [jnp.exp(score) for score in scores]
+    attends = [expon * (1.0 / jnp.sum(expon, -1, keepdims=True)) for expon in expons]
+    means = [jnp.sum(attend * dprob, -1, keepdims=True) for attend, dprob in zip(attends, dprobs)]
+    dscores = [attend * (dprob - mean) for attend, dprob, mean in zip(attends, dprobs, means)]
+    dqns = [mm(dscore.astype(BF16), key) * temper for dscore, key in zip(dscores, keys)]
+    dqs = [
+        inverse * (dqn - jnp.mean(dqn, -1, keepdims=True) - qn * jnp.mean(dqn * qn, -1, keepdims=True))
+        for inverse, dqn, qn in zip(inverses, dqns, qns)
+    ]
+    return jnp.concatenate([dq.astype(BF16) for dq in dqs], axis=1)
 
 
 def fetch(pairs, sems, first=0):
@@ -129,22 +156,25 @@
                   keep_ref, send_ref, square_ref, query_ref, first_ref, normed_ref, normt_ref, sides_ref, sems):
     cuts = 4
     chips, run = first_ref.shape[0] // cuts, normed_ref.shape[1] // cuts
-    pairs = []
+    pairs = [(sides_any, sides_ref)]
     for i in range(cuts):
         rows, cols = pl.ds(i * chips, chips), pl.ds(i * run, run)
         pairs += [(first_any.at[rows], first_ref.at[rows]), (normed_any.at[:, cols], normed_ref.at[:, cols])]
-    pairs += [(square_any, square_ref), (query_any, query_ref), (sides_any, sides_ref)]
+    pairs += [(square_any, square_ref), (query_any, query_ref)]
     copies = fetch(pairs, sems)
+    wait(copies[:1])
+    dprobs = prob_grads(sides_ref)
+    copies = copies[1:]
     move = jnp.zeros(query_ref.shape, F32)
     for i in range(cuts):
         wait(copies[2 * i:2 * i + 2])
         rows = first_ref[i * chips:(i + 1) * chips].reshape(run, first_ref.shape[-1])
         move += mm(normed_ref[:, i * run:(i + 1) * run], rows)
-    late = fetch([(normt_any, normt_ref)], sems, len(copies))
+    late = fetch([(normt_any, normt_ref)], sems, len(pairs))
     wait(copies[2 * cuts:])
     norm = jnp.sqrt(jnp.sum(jnp.sum(square_ref[...], 0), keepdims=True))
     query = query_ref[...] + (radius / norm) * move
-    dq = query_grad(query, sides_ref[0], sides_ref[1], sides_ref[2])
+    dq = query_grad_beside(query, sides_ref[0], dprobs)
     wait(late)
     term(scale, normt_ref, dq, keep_ref, send_ref)
 

time: 174 us -> 174 us (level)
  no operation moved by 1% of the time
where the time goes in v10:
time: 174 us; the launch traced here: 172 us
  starting transfers between devices  64.2 us (37%)
  blocking collectives  58 us (33%)
  waiting for transfers between devices  20.6 us (12%)
  between operations  13.7 us (8%)
  Pallas kernels  10.5 us (6%)
  other arithmetic  4.63 us (3%)
    all_to_all x2, blocking collectives, scatter_parts(): return lax.all_to_all(pieces, ('x', 'z1'), 0, 0, tiled=True)  30.4 us
    all_to_all x2, blocking collectives, everywhere(): lax.all_to_all(jnp.broadcast_to(value, (size, *value.shape)), axes, 0, 0,...  27.6 us
    ppermute x7, starting transfers between devices, turn(): return lax.ppermute(value, 'y', [(i, (i + step) % 8) for i in range(8)])  24.4 us
    ppermute x6, starting transfers between devices, along_z(): lax.ppermute(block, ('z2', 'z1'), swap(4, k))  18.6 us
    ppermute x1, starting transfers between devices, shards(): other = lax.ppermute(tok, 'zh', swap(2, 1))  11.5 us
    pallas_call x5, Pallas kernels, run(): pl.pallas_call(kernel, out_shape=[jax.ShapeDtypeStruct(s, d) for s, d in...  10.5 us
    ppermute x6, waiting for transfers between devices, along_z(): lax.ppermute(block, ('z2', 'z1'), swap(4, k))  7.98 us
    ppermute x2, starting transfers between devices, scatter_parts(): both = add(keep, lax.ppermute(send, 'core', swap(2, 1)))  7.13 us
  transfers between devices with their start and end apart: 19, of which 6 were waited for; matrix products, arithmetic and copies ran while one was open for 1% of the time, Pallas kernels for 0%

profile of v10, /device:TPU:1, one launch (start us, length us, event | category | flops | bytes accessed | tf_op | source)
XLA Modules:
  0.0 171.6 jit_solution(10992144236098853995)
XLA Ops:
  6.5 11.5 %collective-permute-start.3 = (bf16[192,256]{1,0:T(8,128)(2,1)}, bf16[192,256]{1,0:T(8,128)(2,1)S(1)}, u32[]{:S(2)}, u32[]{:S(2)}) collective-permute-start(bf16[192,256]{1,0:T(8,128)(2,1)} %bitcast.21), channel_id=1, source_target_pairs={{0,1},{1,0},{2,3},{3,2},{4,5},{5,4},{6,7},{7,6},{8,9},{9,8},{10,11... | collective-permute-start | bytes 294920 | tf_op jit(solution)/shard_map/ppermute | solution.py:249
  18.0 4.0 %collective-permute-start.1 = (bf16[96,256]{1,0:T(8,128)(2,1)}, bf16[96,256]{1,0:T(8,128)(2,1)S(1)}, u32[]{:S(2)}, u32[]{:S(2)}) collective-permute-start(bf16[96,256]{1,0:T(8,128)(2,1)} %param.9), channel_id=1, source_target_pairs={{0,256},{128,384},{256,0},{384,128},{1,257},{129,385},{257,1},{385... | collective-permute-start | bytes 147464 | tf_op jit(solution)/shard_map/ppermute | solution.py:231
  22.0 3.1 %collective-permute-start = (bf16[96,256]{1,0:T(8,128)(2,1)}, bf16[96,256]{1,0:T(8,128)(2,1)S(1)}, u32[]{:S(2)}, u32[]{:S(2)}) collective-permute-start(bf16[96,256]{1,0:T(8,128)(2,1)} %param.9), channel_id=1, source_target_pairs={{0,128},{128,0},{256,384},{384,256},{1,129},{129,1},{257,385},{385... | collective-permute-start | bytes 147464 | tf_op jit(solution)/shard_map/ppermute | solution.py:231
  25.1 2.2 %collective-permute-start.2 = (bf16[96,256]{1,0:T(8,128)(2,1)}, bf16[96,256]{1,0:T(8,128)(2,1)S(1)}, u32[]{:S(2)}, u32[]{:S(2)}) collective-permute-start(bf16[96,256]{1,0:T(8,128)(2,1)} %param.9), channel_id=1, source_target_pairs={{0,384},{128,256},{256,128},{384,0},{1,385},{129,257},{257,129},{3... | collective-permute-start | bytes 147464 | tf_op jit(solution)/shard_map/ppermute | solution.py:231
  27.3 0.9 pad_maximum_fusion.1.refs_0_
  28.2 3.8 %collective-permute-done.2 = bf16[96,256]{1,0:T(8,128)(2,1)S(1)} collective-permute-done((bf16[96,256]{1,0:T(8,128)(2,1)}, bf16[96,256]{1,0:T(8,128)(2,1)S(1)}, u32[]{:S(2)}, u32[]{:S(2)}) %collective-permute-start.2) | collective-permute-done | bytes 49184 | tf_op jit(solution)/shard_map/ppermute | solution.py:231
  32.0 1.5 pad_maximum_fusion.2
  33.6 5.9 %collective-permute-start.7 = (bf16[384,256]{1,0:T(8,128)(2,1)S(1)}, bf16[384,256]{1,0:T(8,128)(2,1)S(1)}, u32[]{:S(2)}, u32[]{:S(2)}) collective-permute-start(bf16[384,256]{1,0:T(8,128)(2,1)S(1)} %pad_maximum_fusion.1.refs_0_), channel_id=1, source_target_pairs={{0,12},{2,14},{4,0},{6,2},{8,4},{10,6},{12,8},{14,10},{1,13},{3,15... | collective-permute-start | bytes 589832 | tf_op jit(solution)/shard_map/ppermute | solution.py:203
  39.5 1.9 %collective-permute-start.6 = (bf16[384,256]{1,0:T(8,128)(2,1)S(1)}, bf16[384,256]{1,0:T(8,128)(2,1)S(1)}, u32[]{:S(2)}, u32[]{:S(2)}) collective-permute-start(bf16[384,256]{1,0:T(8,128)(2,1)S(1)} %pad_maximum_fusion.1.refs_0_), channel_id=1, source_target_pairs={{0,4},{2,6},{4,8},{6,10},{8,12},{10,14},{12,0},{14,2},{1,5},{3,7},... | collective-permute-start | bytes 589832 | tf_op jit(solution)/shard_map/ppermute | solution.py:203
  41.4 4.7 %collective-permute-start.5 = (bf16[384,256]{1,0:T(8,128)(2,1)S(1)}, bf16[384,256]{1,0:T(8,128)(2,1)S(1)}, u32[]{:S(2)}, u32[]{:S(2)}) collective-permute-start(bf16[384,256]{1,0:T(8,128)(2,1)S(1)} %pad_maximum_fusion.1.refs_0_), channel_id=1, source_target_pairs={{0,14},{2,0},{4,2},{6,4},{8,6},{10,8},{12,10},{14,12},{1,15},{3,1}... | collective-permute-start | bytes 589832 | tf_op jit(solution)/shard_map/ppermute | solution.py:203
  46.1 1.9 %collective-permute-start.4 = (bf16[384,256]{1,0:T(8,128)(2,1)S(1)}, bf16[384,256]{1,0:T(8,128)(2,1)S(1)}, u32[]{:S(2)}, u32[]{:S(2)}) collective-permute-start(bf16[384,256]{1,0:T(8,128)(2,1)S(1)} %pad_maximum_fusion.1.refs_0_), channel_id=1, source_target_pairs={{0,2},{2,4},{4,6},{6,8},{8,10},{10,12},{12,14},{14,0},{1,3},{3,5},... | collective-permute-start | bytes 589832 | tf_op jit(solution)/shard_map/ppermute | solution.py:203
  48.0 4.7 %collective-permute-start.10 = (bf16[384,256]{1,0:T(8,128)(2,1)S(1)}, bf16[384,256]{1,0:T(8,128)(2,1)S(1)}, u32[]{:S(2)}, u32[]{:S(2)}) collective-permute-start(bf16[384,256]{1,0:T(8,128)(2,1)S(1)} %collective-permute-done.7.refs_4_), channel_id=1, source_target_pairs={{0,12},{2,14},{4,0},{6,2},{8,4},{10,6},{12,8},{14,10},{1,13},{3,15... | collective-permute-start | bytes 589832 | tf_op jit(solution)/shard_map/ppermute | solution.py:203
  52.7 1.9 %collective-permute-start.9 = (bf16[384,256]{1,0:T(8,128)(2,1)S(1)}, bf16[384,256]{1,0:T(8,128)(2,1)S(1)}, u32[]{:S(2)}, u32[]{:S(2)}) collective-permute-start(bf16[384,256]{1,0:T(8,128)(2,1)S(1)} %collective-permute-done.7.refs_4_), channel_id=1, source_target_pairs={{0,14},{2,0},{4,2},{6,4},{8,6},{10,8},{12,10},{14,12},{1,15},{3,1}... | collective-permute-start | bytes 589832 | tf_op jit(solution)/shard_map/ppermute | solution.py:203
  54.7 3.4 %collective-permute-start.8 = (bf16[384,256]{1,0:T(8,128)(2,1)S(1)}, bf16[384,256]{1,0:T(8,128)(2,1)S(1)}, u32[]{:S(2)}, u32[]{:S(2)}) collective-permute-start(bf16[384,256]{1,0:T(8,128)(2,1)S(1)} %collective-permute-done.6.refs_3_), channel_id=1, source_target_pairs={{0,2},{2,4},{4,6},{6,8},{8,10},{10,12},{12,14},{14,0},{1,3},{3,5},... | collective-permute-start | bytes 589832 | tf_op jit(solution)/shard_map/ppermute | solution.py:203
  58.0 1.1 pad_maximum_fusion.refs_9_.refs_5_
  59.1 5.8 %collective-permute-done.9.refs_6_ = bf16[384,256]{1,0:T(8,128)(2,1)S(1)} collective-permute-done((bf16[384,256]{1,0:T(8,128)(2,1)S(1)}, bf16[384,256]{1,0:T(8,128)(2,1)S(1)}, u32[]{:S(2)}, u32[]{:S(2)}) %collective-permute-start.9) | collective-permute-done | bytes 196640 | tf_op jit(solution)/shard_map/ppermute | solution.py:203
  64.9 4.9 %shard_map.55 = (bf16[2,4,2,2,96,256]{5,4,3,2,1,0:T(8,128)(2,1)S(1)}, bf16[256,3072]{1,0:T(8,128)(2,1)}, f32[256,256]{1,0:T(8,128)S(1)}, bf16[16,96,256]{2,1,0:T(8,128)(2,1)S(1)}, bf16[16,96,256]{2,1,0:T(8,128)(2,1)S(1)}) custom-call(bf16[384,256]{1,0:T(8,128)(2,1)S(1)} %pad_maximum_fusion.1.refs_0_, bf16[384,256]{1,0:T(8,128)(2,1)S(1)} %collective-permute-done.4.refs_1_, ...), custom_call_target="tpu_custom_call" | custom-call | tf_op jit(solution)/shard_map/pallas_call | solution.py:186
  69.9 4.5 %collective-permute-start.11 = (bf16[16,96,256]{2,1,0:T(8,128)(2,1)S(1)}, bf16[16,96,256]{2,1,0:T(8,128)(2,1)S(1)}, u32[]{:S(2)}, u32[]{:S(2)}) collective-permute-start(bf16[16,96,256]{2,1,0:T(8,128)(2,1)S(1)} %get-tuple-element.27), channel_id=1, source_target_pairs={{0,16},{16,0},{1,17},{17,1},{2,18},{18,2},{3,19},{19,3},{4,20},{20... | collective-permute-start | bytes 2359304 | tf_op jit(solution)/shard_map/ppermute | solution.py:221
  74.4 1.9 %collective-permute-done.11 = bf16[16,96,256]{2,1,0:T(8,128)(2,1)S(1)} collective-permute-done((bf16[16,96,256]{2,1,0:T(8,128)(2,1)S(1)}, bf16[16,96,256]{2,1,0:T(8,128)(2,1)S(1)}, u32[]{:S(2)}, u32[]{:S(2)}) %collective-permute-start.11) | collective-permute-done | bytes 786464 | tf_op jit(solution)/shard_map/ppermute | solution.py:221
  76.5 15.8 %all_to_all.20.parts_ref = bf16[8,192,256]{2,1,0:T(8,128)(2,1)S(1)} all-to-all(bf16[8,192,256]{2,1,0:T(8,128)(2,1)S(1)} %bitcast.14), channel_id=1, replica_groups=mesh['z2'=2,'z1'=2,'x'=4,'core'=2,'y'=8,'zh'=2] {'x','z1'}, dimensions={0} | all-to-all | bytes 1572864 | tf_op jit(solution)/shard_map/all_to_all | solution.py:223
  92.5 2.7 %collective-permute-start.14 = (bf16[192,256]{1,0:T(8,128)(2,1)S(1)}, bf16[192,256]{1,0:T(8,128)(2,1)S(1)}, u32[]{:S(2)}, u32[]{:S(2)}) collective-permute-start(bf16[192,256]{1,0:T(8,128)(2,1)S(1)} %shard_map.56.mine_ref), channel_id=1, source_target_pairs={{0,384},{128,256},{256,128},{384,0},{1,385},{129,257},{257,129},{3... | collective-permute-start | bytes 294920 | tf_op jit(solution)/shard_map/ppermute | solution.py:231
  95.2 3.1 %collective-permute-start.13 = (bf16[192,256]{1,0:T(8,128)(2,1)S(1)}, bf16[192,256]{1,0:T(8,128)(2,1)S(1)}, u32[]{:S(2)}, u32[]{:S(2)}) collective-permute-start(bf16[192,256]{1,0:T(8,128)(2,1)S(1)} %shard_map.56.mine_ref), channel_id=1, source_target_pairs={{0,256},{128,384},{256,0},{384,128},{1,257},{129,385},{257,1},{385... | collective-permute-start | bytes 294920 | tf_op jit(solution)/shard_map/ppermute | solution.py:231
  98.3 3.4 %collective-permute-start.12 = (bf16[192,256]{1,0:T(8,128)(2,1)S(1)}, bf16[192,256]{1,0:T(8,128)(2,1)S(1)}, u32[]{:S(2)}, u32[]{:S(2)}) collective-permute-start(bf16[192,256]{1,0:T(8,128)(2,1)S(1)} %shard_map.56.mine_ref), channel_id=1, source_target_pairs={{0,128},{128,0},{256,384},{384,256},{1,129},{129,1},{257,385},{385... | collective-permute-start | bytes 294920 | tf_op jit(solution)/shard_map/ppermute | solution.py:231
  101.8 4.2 %collective-permute-done.13.mine_far_ref = bf16[192,256]{1,0:T(8,128)(2,1)S(1)} collective-permute-done((bf16[192,256]{1,0:T(8,128)(2,1)S(1)}, bf16[192,256]{1,0:T(8,128)(2,1)S(1)}, u32[]{:S(2)}, u32[]{:S(2)}) %collective-permute-start.13) | collective-permute-done | bytes 98336 | tf_op jit(solution)/shard_map/ppermute | solution.py:231
  106.8 17.6 %all_to_all.21 = f32[16,8,128]{2,1,0:T(8,128)S(1)} all-to-all(f32[16,8,128]{2,1,0:T(8,128)S(1)} %broadcast_in_dim.6), channel_id=1, replica_groups=mesh['z2'=2,'z1'=2,'x'=4,'core'=2,'y'=8,'zh'=2] {'zh','y'}, dimensions={0} | all-to-all | bytes 131072 | tf_op jit(solution)/shard_map/all_to_all | solution.py:227
  124.4 10.0 %all_to_all.22.refs_0_ = f32[8,8,128]{2,1,0:T(8,128)S(1)} all-to-all(f32[8,8,128]{2,1,0:T(8,128)S(1)} %broadcast_in_dim.7), channel_id=1, replica_groups=mesh['z2'=2,'z1'=2,'x'=4,'core'=2,'y'=8,'zh'=2] {'x','core'}, dimensions={0} | all-to-all | bytes 65536 | tf_op jit(solution)/shard_map/all_to_all | solution.py:227
  134.4 4.6 %shard_map.58 = (bf16[16,96,256]{2,1,0:T(8,128)(2,1)S(1)}, bf16[16,96,256]{2,1,0:T(8,128)(2,1)S(1)}) custom-call(f32[8,8,128]{2,1,0:T(8,128)S(1)} %all_to_all.22.refs_0_, f32[256,256]{1,0:T(8,128)S(1)} %get-tuple-element.29.refs_1_, bf16[8,2,192,256]{3,2,1,0:T(8,128)(2,1)} %bitcast.17, bf16[256,3072]{1,0:T(8,128)(2,1)} %get-tuple-element.31.refs_3_, ...), custom_call_target="tpu_custom_call" | custom-call | tf_op jit(solution)/shard_map/pallas_call | solution.py:186
  138.9 2.6 %collective-permute-start.15 = (bf16[16,96,256]{2,1,0:T(8,128)(2,1)S(1)}, bf16[16,96,256]{2,1,0:T(8,128)(2,1)S(1)}, u32[]{:S(2)}, u32[]{:S(2)}) collective-permute-start(bf16[16,96,256]{2,1,0:T(8,128)(2,1)S(1)} %get-tuple-element.34), channel_id=1, source_target_pairs={{0,16},{16,0},{1,17},{17,1},{2,18},{18,2},{3,19},{19,3},{4,20},{20... | collective-permute-start | bytes 2359304 | tf_op jit(solution)/shard_map/ppermute | solution.py:221
  141.6 1.9 %collective-permute-done.15 = bf16[16,96,256]{2,1,0:T(8,128)(2,1)S(1)} collective-permute-done((bf16[16,96,256]{2,1,0:T(8,128)(2,1)S(1)}, bf16[16,96,256]{2,1,0:T(8,128)(2,1)S(1)}, u32[]{:S(2)}, u32[]{:S(2)}) %collective-permute-start.15) | collective-permute-done | bytes 786464 | tf_op jit(solution)/shard_map/ppermute | solution.py:221
  143.7 14.6 %all_to_all.23 = bf16[8,192,256]{2,1,0:T(8,128)(2,1)S(1)} all-to-all(bf16[8,192,256]{2,1,0:T(8,128)(2,1)S(1)} %bitcast.15), channel_id=1, replica_groups=mesh['z2'=2,'z1'=2,'x'=4,'core'=2,'y'=8,'zh'=2] {'x','z1'}, dimensions={0} | all-to-all | bytes 1572864 | tf_op jit(solution)/shard_map/all_to_all | solution.py:223
  158.4 2.7 %collective-permute-start.16 = (bf16[96,256]{1,0:T(8,128)(2,1)S(1)}, bf16[96,256]{1,0:T(8,128)(2,1)S(1)}, u32[]{:S(2)}, u32[]{:S(2)}) collective-permute-start(bf16[96,256]{1,0:T(8,128)(2,1)S(1)} %get-tuple-element.36), channel_id=1, source_target_pairs={{0,256},{256,0},{1,257},{257,1},{2,258},{258,2},{3,259},{259,3},{4... | collective-permute-start | bytes 147464 | tf_op jit(solution)/shard_map/ppermute | solution.py:280
  161.1 3.0 %collective-permute-done.16 = bf16[96,256]{1,0:T(8,128)(2,1)S(1)} collective-permute-done((bf16[96,256]{1,0:T(8,128)(2,1)S(1)}, bf16[96,256]{1,0:T(8,128)(2,1)S(1)}, u32[]{:S(2)}, u32[]{:S(2)}) %collective-permute-start.16) | collective-permute-done | bytes 49184 | tf_op jit(solution)/shard_map/ppermute | solution.py:280
  (28 shorter events, 2.2 us)
Async XLA Ops:
  6.5 58.4 %all-gather.5.cloned.1.call-start = ((), (), s32[]{:S(2)}) async-start(), calls=%async_computation.4 | async-start | bytes 1769472 | tf_op jit(solution)/shard_map/all_gather | solution.py:235
  6.5 20.8 %collective-permute-start.3 = (bf16[192,256]{1,0:T(8,128)(2,1)}, bf16[192,256]{1,0:T(8,128)(2,1)S(1)}, u32[]{:S(2)}, u32[]{:S(2)}) collective-permute-start(bf16[192,256]{1,0:T(8,128)(2,1)} %bitcast.21), channel_id=1, source_target_pairs={{0,1},{1,0},{2,3},{3,2},{4,5},{5,4},{6,7},{7,6},{8,9},{9,8},{10,11... | collective-permute-start | bytes 294920 | tf_op jit(solution)/shard_map/ppermute | solution.py:249
  18.0 10.2 %collective-permute-start.1 = (bf16[96,256]{1,0:T(8,128)(2,1)}, bf16[96,256]{1,0:T(8,128)(2,1)S(1)}, u32[]{:S(2)}, u32[]{:S(2)}) collective-permute-start(bf16[96,256]{1,0:T(8,128)(2,1)} %param.9), channel_id=1, source_target_pairs={{0,256},{128,384},{256,0},{384,128},{1,257},{129,385},{257,1},{385... | collective-permute-start | bytes 147464 | tf_op jit(solution)/shard_map/ppermute | solution.py:231
  22.0 6.2 %collective-permute-start = (bf16[96,256]{1,0:T(8,128)(2,1)}, bf16[96,256]{1,0:T(8,128)(2,1)S(1)}, u32[]{:S(2)}, u32[]{:S(2)}) collective-permute-start(bf16[96,256]{1,0:T(8,128)(2,1)} %param.9), channel_id=1, source_target_pairs={{0,128},{128,0},{256,384},{384,256},{1,129},{129,1},{257,385},{385... | collective-permute-start | bytes 147464 | tf_op jit(solution)/shard_map/ppermute | solution.py:231
  25.1 6.9 %collective-permute-start.2 = (bf16[96,256]{1,0:T(8,128)(2,1)}, bf16[96,256]{1,0:T(8,128)(2,1)S(1)}, u32[]{:S(2)}, u32[]{:S(2)}) collective-permute-start(bf16[96,256]{1,0:T(8,128)(2,1)} %param.9), channel_id=1, source_target_pairs={{0,384},{128,256},{256,128},{384,0},{1,385},{129,257},{257,129},{3... | collective-permute-start | bytes 147464 | tf_op jit(solution)/shard_map/ppermute | solution.py:231
  33.5 100.8 %all-gather.7.cloned.1.call-start = ((), (), s32[]{:S(2)}) async-start(), calls=%async_computation.5 | async-start | bytes 1769472 | tf_op jit(solution)/shard_map/all_gather | solution.py:235
  33.6 14.4 %collective-permute-start.7 = (bf16[384,256]{1,0:T(8,128)(2,1)S(1)}, bf16[384,256]{1,0:T(8,128)(2,1)S(1)}, u32[]{:S(2)}, u32[]{:S(2)}) collective-permute-start(bf16[384,256]{1,0:T(8,128)(2,1)S(1)} %pad_maximum_fusion.1.refs_0_), channel_id=1, source_target_pairs={{0,12},{2,14},{4,0},{6,2},{8,4},{10,6},{12,8},{14,10},{1,13},{3,15... | collective-permute-start | bytes 589832 | tf_op jit(solution)/shard_map/ppermute | solution.py:203
  39.5 15.2 %collective-permute-start.6 = (bf16[384,256]{1,0:T(8,128)(2,1)S(1)}, bf16[384,256]{1,0:T(8,128)(2,1)S(1)}, u32[]{:S(2)}, u32[]{:S(2)}) collective-permute-start(bf16[384,256]{1,0:T(8,128)(2,1)S(1)} %pad_maximum_fusion.1.refs_0_), channel_id=1, source_target_pairs={{0,4},{2,6},{4,8},{6,10},{8,12},{10,14},{12,0},{14,2},{1,5},{3,7},... | collective-permute-start | bytes 589832 | tf_op jit(solution)/shard_map/ppermute | solution.py:203
  41.4 17.7 %collective-permute-start.5 = (bf16[384,256]{1,0:T(8,128)(2,1)S(1)}, bf16[384,256]{1,0:T(8,128)(2,1)S(1)}, u32[]{:S(2)}, u32[]{:S(2)}) collective-permute-start(bf16[384,256]{1,0:T(8,128)(2,1)S(1)} %pad_maximum_fusion.1.refs_0_), channel_id=1, source_target_pairs={{0,14},{2,0},{4,2},{6,4},{8,6},{10,8},{12,10},{14,12},{1,15},{3,1}... | collective-permute-start | bytes 589832 | tf_op jit(solution)/shard_map/ppermute | solution.py:203
  46.1 13.0 %collective-permute-start.4 = (bf16[384,256]{1,0:T(8,128)(2,1)S(1)}, bf16[384,256]{1,0:T(8,128)(2,1)S(1)}, u32[]{:S(2)}, u32[]{:S(2)}) collective-permute-start(bf16[384,256]{1,0:T(8,128)(2,1)S(1)} %pad_maximum_fusion.1.refs_0_), channel_id=1, source_target_pairs={{0,2},{2,4},{4,6},{6,8},{8,10},{10,12},{12,14},{14,0},{1,3},{3,5},... | collective-permute-start | bytes 589832 | tf_op jit(solution)/shard_map/ppermute | solution.py:203
  48.0 11.1 %collective-permute-start.10 = (bf16[384,256]{1,0:T(8,128)(2,1)S(1)}, bf16[384,256]{1,0:T(8,128)(2,1)S(1)}, u32[]{:S(2)}, u32[]{:S(2)}) collective-permute-start(bf16[384,256]{1,0:T(8,128)(2,1)S(1)} %collective-permute-done.7.refs_4_), channel_id=1, source_target_pairs={{0,12},{2,14},{4,0},{6,2},{8,4},{10,6},{12,8},{14,10},{1,13},{3,15... | collective-permute-start | bytes 589832 | tf_op jit(solution)/shard_map/ppermute | solution.py:203
  52.7 12.2 %collective-permute-start.9 = (bf16[384,256]{1,0:T(8,128)(2,1)S(1)}, bf16[384,256]{1,0:T(8,128)(2,1)S(1)}, u32[]{:S(2)}, u32[]{:S(2)}) collective-permute-start(bf16[384,256]{1,0:T(8,128)(2,1)S(1)} %collective-permute-done.7.refs_4_), channel_id=1, source_target_pairs={{0,14},{2,0},{4,2},{6,4},{8,6},{10,8},{12,10},{14,12},{1,15},{3,1}... | collective-permute-start | bytes 589832 | tf_op jit(solution)/shard_map/ppermute | solution.py:203
  54.7 10.3 %collective-permute-start.8 = (bf16[384,256]{1,0:T(8,128)(2,1)S(1)}, bf16[384,256]{1,0:T(8,128)(2,1)S(1)}, u32[]{:S(2)}, u32[]{:S(2)}) collective-permute-start(bf16[384,256]{1,0:T(8,128)(2,1)S(1)} %collective-permute-done.6.refs_3_), channel_id=1, source_target_pairs={{0,2},{2,4},{4,6},{6,8},{8,10},{10,12},{12,14},{14,0},{1,3},{3,5},... | collective-permute-start | bytes 589832 | tf_op jit(solution)/shard_map/ppermute | solution.py:203
  69.9 22.5 %copy-start = (bf16[2,4,2,2,96,256]{5,4,3,2,1,0:T(8,128)(2,1)}, bf16[2,4,2,2,96,256]{5,4,3,2,1,0:T(8,128)(2,1)S(1)}, u32[]{:S(2)}) copy-start(bf16[2,4,2,2,96,256]{5,4,3,2,1,0:T(8,128)(2,1)S(1)} %get-tuple-element.32.refs_4_) | copy-start | bytes 4718596
  69.9 6.4 %collective-permute-start.11 = (bf16[16,96,256]{2,1,0:T(8,128)(2,1)S(1)}, bf16[16,96,256]{2,1,0:T(8,128)(2,1)S(1)}, u32[]{:S(2)}, u32[]{:S(2)}) collective-permute-start(bf16[16,96,256]{2,1,0:T(8,128)(2,1)S(1)} %get-tuple-element.27), channel_id=1, source_target_pairs={{0,16},{16,0},{1,17},{17,1},{2,18},{18,2},{3,19},{19,3},{4,20},{20... | collective-permute-start | bytes 2359304 | tf_op jit(solution)/shard_map/ppermute | solution.py:221
  92.5 9.3 %collective-permute-start.14 = (bf16[192,256]{1,0:T(8,128)(2,1)S(1)}, bf16[192,256]{1,0:T(8,128)(2,1)S(1)}, u32[]{:S(2)}, u32[]{:S(2)}) collective-permute-start(bf16[192,256]{1,0:T(8,128)(2,1)S(1)} %shard_map.56.mine_ref), channel_id=1, source_target_pairs={{0,384},{128,256},{256,128},{384,0},{1,385},{129,257},{257,129},{3... | collective-permute-start | bytes 294920 | tf_op jit(solution)/shard_map/ppermute | solution.py:231
  95.2 10.8 %collective-permute-start.13 = (bf16[192,256]{1,0:T(8,128)(2,1)S(1)}, bf16[192,256]{1,0:T(8,128)(2,1)S(1)}, u32[]{:S(2)}, u32[]{:S(2)}) collective-permute-start(bf16[192,256]{1,0:T(8,128)(2,1)S(1)} %shard_map.56.mine_ref), channel_id=1, source_target_pairs={{0,256},{128,384},{256,0},{384,128},{1,257},{129,385},{257,1},{385... | collective-permute-start | bytes 294920 | tf_op jit(solution)/shard_map/ppermute | solution.py:231
  98.3 7.7 %collective-permute-start.12 = (bf16[192,256]{1,0:T(8,128)(2,1)S(1)}, bf16[192,256]{1,0:T(8,128)(2,1)S(1)}, u32[]{:S(2)}, u32[]{:S(2)}) collective-permute-start(bf16[192,256]{1,0:T(8,128)(2,1)S(1)} %shard_map.56.mine_ref), channel_id=1, source_target_pairs={{0,128},{128,0},{256,384},{384,256},{1,129},{129,1},{257,385},{385... | collective-permute-start | bytes 294920 | tf_op jit(solution)/shard_map/ppermute | solution.py:231
  138.9 4.5 %collective-permute-start.15 = (bf16[16,96,256]{2,1,0:T(8,128)(2,1)S(1)}, bf16[16,96,256]{2,1,0:T(8,128)(2,1)S(1)}, u32[]{:S(2)}, u32[]{:S(2)}) collective-permute-start(bf16[16,96,256]{2,1,0:T(8,128)(2,1)S(1)} %get-tuple-element.34), channel_id=1, source_target_pairs={{0,16},{16,0},{1,17},{17,1},{2,18},{18,2},{3,19},{19,3},{4,20},{20... | collective-permute-start | bytes 2359304 | tf_op jit(solution)/shard_map/ppermute | solution.py:221
  158.4 5.7 %collective-permute-start.16 = (bf16[96,256]{1,0:T(8,128)(2,1)S(1)}, bf16[96,256]{1,0:T(8,128)(2,1)S(1)}, u32[]{:S(2)}, u32[]{:S(2)}) collective-permute-start(bf16[96,256]{1,0:T(8,128)(2,1)S(1)} %get-tuple-element.36), channel_id=1, source_target_pairs={{0,256},{256,0},{1,257},{257,1},{2,258},{258,2},{3,259},{259,3},{4... | collective-permute-start | bytes 147464 | tf_op jit(solution)/shard_map/ppermute | solution.py:280
Sparse Core Ops, SparseCore 0:
  33.7 28.1 all-gather.4
  106.9 25.0 all-gather.6
